TPU v7x, 128 devices: a whole 4x4x4 slice. The times are simulated.
128 devices in a mesh: row: 8 (over y, z_lo), col: 16 (over z_hi, x, core).
Axes of the slice: x: 4, y: 4, z: 4 (z_hi: 2, z_lo: 2; z = z_hi * 2 + z_lo), core: 2. Of those that a mesh axis runs over, the one named last changes fastest.
Arguments:
- data: bfloat16 [8, 16, 32, 1024, 128], P('row', 'col'), may hold values from -6 to 6
- real_index: int32 [8, 16, 2, 2], P('row', 'col'), may hold values from 0 to 31
- latent_seed: int32 [8, 16, 2, 2], P('row', 'col'), may hold values from 0 to 255
- latent_bank: float32 [256, 128], replicated, may hold values from -6 to 6
- g_in: float32 [8, 16, 128, 128], P('row', 'col'), may hold values from -0.5 to 0.5
- g_base: float32 [8, 16, 1024, 128], P('row', 'col'), may hold values from -6 to 6
- g_one: float32 [8, 16, 128, 128], P('row', 'col'), may hold values from -0.5 to 0.5
- g_two: float32 [8, 16, 128, 128], P('row', 'col'), may hold values from -0.5 to 0.5
- d_one: float32 [8, 16, 128, 128], P('row', 'col'), may hold values from -0.5 to 0.5
- d_two: float32 [8, 16, 128, 128], P('row', 'col'), may hold values from -0.5 to 0.5
- d_out: float32 [8, 16, 128], P('row', 'col'), may hold values from -0.5 to 0.5
Outputs:
- new_g_in: float32 [8, 16, 128, 128], P('row', 'col')
- new_g_base: float32 [8, 16, 1024, 128], P('row', 'col')
- new_g_one: float32 [8, 16, 128, 128], P('row', 'col')
- new_g_two: float32 [8, 16, 128, 128], P('row', 'col')
- new_d_one: float32 [8, 16, 128, 128], P('row', 'col')
- new_d_two: float32 [8, 16, 128, 128], P('row', 'col')
- new_d_out: float32 [8, 16, 128], P('row', 'col')
- verdicts: float32 [8, 16, 2, 12], P('row', 'col')
All inputs are finite; a program needn't handle non-finite values.
Results may differ from a plain program's by a relative error of at most 0.0028.
Values may be sent and summed in bfloat16 or wider, within the bound.
No kernel may reach another device: no remote copies, remote signals or barrier semaphores. Data moves between devices by JAX's collectives and lax.ppermute only.
A program may use at most 128 MiB of HBM per device.

v0:
```python
import functools

import jax
import jax.numpy as jnp
from jax import lax
from jax.experimental import pallas as pl
from jax.experimental.pallas import tpu as pltpu
from jax.sharding import PartitionSpec as P

STEPS = 2
LEARN_RATE = 0.05
BASE_RATE = 0.1
PACKET = 272
HEAD = 256
VMEM_LIMIT = 24 * 1024 * 1024
F32 = jnp.float32
BF16 = jnp.bfloat16


def dot(left, right):
    return jnp.dot(left, right, preferred_element_type=F32)


def dot_rows(left, right):
    return lax.dot_general(left, right, (((0,), (0,)), ((), ())), preferred_element_type=F32)


def silu_parts(half):
    tanh_part = jnp.tanh(half)
    above = 1.0 + tanh_part
    value = half * above
    slope_twice = above + value * (1.0 - tanh_part)
    return value, slope_twice


def sigmoid(value):
    return 0.5 * (1.0 + jnp.tanh(0.5 * value))


def col_sums(tile):
    rows, channels = tile.shape
    return jnp.sum(tile.reshape(rows // 8, 8, channels), axis=0)


def split_two(value):
    high = value.astype(BF16)
    low = (value - high.astype(F32)).astype(BF16)
    return high, low


def call(body, out_shape, scratch=(), n_inputs=0, smem=(), **kwargs):
    in_specs = [
        pl.BlockSpec(memory_space=pltpu.SMEM if i in smem else pltpu.VMEM) for i in range(n_inputs)
    ]
    out_specs = [pl.BlockSpec(memory_space=pltpu.VMEM) for _ in out_shape]
    return pl.pallas_call(
        body,
        out_shape=tuple(out_shape),
        in_specs=in_specs,
        out_specs=tuple(out_specs),
        scratch_shapes=list(scratch),
        compiler_params=pltpu.CompilerParams(vmem_limit_bytes=VMEM_LIMIT),
        **kwargs,
    )


def shape(dims, dtype):
    return jax.ShapeDtypeStruct(dims, dtype)


def write_packet(packet_ref, one, two, out_row):
    channels = one.shape[0]
    packet_ref[0:channels, :] = one.astype(BF16)
    packet_ref[channels : 2 * channels, :] = two.astype(BF16)
    high, low = split_two(out_row)
    rest = PACKET - 2 * channels
    spot = lax.broadcasted_iota(jnp.int32, (rest, channels), 0)
    tail = jnp.where(spot == 0, high.astype(F32), jnp.where(spot == 1, low.astype(F32), 0.0))
    packet_ref[2 * channels : PACKET, :] = tail.astype(BF16)


def pack_body(one_ref, two_ref, out_ref, packet_ref):
    write_packet(packet_ref, one_ref[...], two_ref[...], out_ref[...])


def pack(d_one, d_two, d_out):
    return call(pack_body, [shape((PACKET, 128), BF16)], n_inputs=3)(d_one, d_two, d_out)[0]


def judge_tile(image, halves, weights):
    one_half, two_half, one_turned, two_half_turned, out_half = weights
    first, slope_first = silu_parts(dot(image, one_half))
    first_half = first.astype(BF16)
    feature, slope_out = silu_parts(halves + dot(first_half, two_half))
    outer = out_half * slope_out
    outer_half = outer.astype(BF16)
    inner_half = (dot(outer_half, two_half_turned) * slope_first).astype(BF16)
    unit = outer + dot(inner_half, one_turned)
    return first_half, feature, outer_half, inner_half, unit


def judge_body(fakes, reals, tile, *refs):
    refs = list(refs)
    index_ref = refs.pop(0) if reals else None
    packet_ref = refs.pop(0)
    fakes_ref = refs.pop(0)
    data_ref = refs.pop(0) if reals else None
    grads_ref, unit_ref, slope_ref = refs[:3]
    one_half, two_half, one_turned, two_turned, sum_one, sum_two, sum_out = refs[3:10]
    if reals:
        real_buf, real_sem = refs[10:12]
        copies = [
            pltpu.make_async_copy(data_ref.at[index_ref[i]], real_buf.at[i], real_sem.at[i])
            for i in range(reals)
        ]
        for copy in copies:
            copy.start()
    images = fakes + reals
    places = unit_ref.shape[1]
    channels = unit_ref.shape[2]

    one = packet_ref[0:channels, :].astype(F32)
    two = packet_ref[channels : 2 * channels, :].astype(F32)
    tail = packet_ref[2 * channels : PACKET, :].astype(F32)
    out_row = tail[0:1, :] + tail[1:2, :]
    one_half[...] = (0.5 * one).astype(BF16)
    two_half[...] = (0.5 * two).astype(BF16)
    one_turned[...] = one.T.astype(BF16)
    two_turned[...] = (0.5 * two).T.astype(BF16)
    sum_one[...] = jnp.zeros_like(sum_one)
    sum_two[...] = jnp.zeros_like(sum_two)
    sum_out[...] = jnp.zeros_like(sum_out)
    out_half = 0.5 * out_row

    def run(members, source, with_unit):
        def step(number, carry):
            rows = pl.ds(pl.multiple_of(number * tile, tile), tile)
            weights = (one_half[...], two_half[...], one_turned[...], two_turned[...], out_half)
            for member in members:
                image = source(member, rows)
                halves = 0.5 * image.astype(F32)
                first_half, feature, outer_half, inner_half, unit = judge_tile(image, halves, weights)
                if with_unit:
                    unit_ref[member, rows, :] = unit.astype(BF16)
                sum_out[member] += col_sums(feature)
                sum_two[member] += dot_rows(first_half, outer_half)
                sum_one[member] += dot_rows(image, inner_half)
            return carry

        lax.fori_loop(0, places // tile, step, 0)

    run(list(range(fakes)), lambda member, rows: fakes_ref[member, rows, :], True)
    if reals:
        for copy in copies:
            copy.wait()
        run(list(range(fakes, images)), lambda member, rows: real_buf[member - fakes, rows, :], False)

    total_one = jnp.zeros((channels, channels), F32)
    total_two = jnp.zeros((channels, channels), F32)
    total_out = jnp.zeros((1, channels), F32)
    scale = 1.0 / places
    verdict_rows = []
    for member in range(images):
        feature_sum = jnp.sum(sum_out[member], axis=0, keepdims=True)
        verdict = jnp.sum(feature_sum * out_row, axis=1, keepdims=True) * scale
        verdict = jnp.broadcast_to(verdict, (1, channels))
        verdict_rows.append(verdict)
        minus = -sigmoid(-verdict)
        slope = sigmoid(verdict) if member < fakes else minus
        slope = slope * scale
        if member < fakes:
            slope_ref[member : member + 1, :] = minus * scale
        total_one = total_one + slope * sum_one[member]
        total_two = total_two + slope * sum_two[member]
        total_out = total_out + slope * feature_sum
    if reals:
        grads_ref[0:channels, :] = total_one
        grads_ref[channels : 2 * channels, :] = total_two
        grads_ref[HEAD : HEAD + 1, :] = total_out
        for member in range(images):
            grads_ref[HEAD + 1 + member : HEAD + 2 + member, :] = verdict_rows[member]
    else:
        write_packet(grads_ref, total_one, total_two, total_out)
        rows = []
        for member in range(images):
            rows.extend(split_two(verdict_rows[member]))
        high, low = split_two(total_out)
        rows = [high, low] + rows
        spot = lax.broadcasted_iota(jnp.int32, (PACKET - HEAD, channels), 0)
        tail_rows = jnp.zeros((PACKET - HEAD, channels), F32)
        for place, row in enumerate(rows):
            tail_rows = jnp.where(spot == place, row.astype(F32), tail_rows)
        grads_ref[HEAD:PACKET, :] = tail_rows.astype(BF16)


def judge(packet, fakes, data=None, index=None, tile=256):
    fake_count, places, channels = fakes.shape
    reals = 0 if index is None else index.shape[0]
    square = (channels, channels)
    images = fake_count + reals
    scratch = [pltpu.VMEM(square, BF16)] * 4 + [
        pltpu.VMEM((images,) + square, F32),
        pltpu.VMEM((images,) + square, F32),
        pltpu.VMEM((images, 8, channels), F32),
    ]
    outs = [
        shape((PACKET, channels), F32 if reals else BF16),
        shape((fake_count, places, channels), BF16),
        shape((8, channels), F32),
    ]
    body = functools.partial(judge_body, fake_count, reals, tile)
    vmem = pl.BlockSpec(memory_space=pltpu.VMEM)
    if reals:
        scratch = scratch + [
            pltpu.VMEM((reals, places, channels), BF16),
            pltpu.SemaphoreType.DMA((reals,)),
        ]
        in_specs = [pl.BlockSpec(memory_space=pltpu.SMEM), vmem, vmem, pl.BlockSpec(memory_space=pl.ANY)]
        operands = (index, packet, fakes, data)
    else:
        in_specs = [vmem, vmem]
        operands = (packet, fakes)
    flops = images * places * channels * channels * 12
    return pl.pallas_call(
        body,
        out_shape=tuple(outs),
        in_specs=in_specs,
        out_specs=(vmem,) * 3,
        scratch_shapes=scratch,
        compiler_params=pltpu.CompilerParams(vmem_limit_bytes=VMEM_LIMIT),
        cost_estimate=pl.CostEstimate(flops=flops, bytes_accessed=2 * 1024 * 1024, transcendentals=0),
    )(*operands)


def gen_forward(seeds, bank_ref, w_in, base_ref, w_one, w_two, outs, tile):
    fakes_ref, hidden_ref, middle_ref, gen_slope_ref, mid_slope_ref, latent_ref = outs
    places, channels = base_ref.shape
    batch = len(seeds)
    latent_ref[...] = jnp.zeros_like(latent_ref)
    for member, seed in enumerate(seeds):
        latent_ref[member : member + 1, :] = (
            bank_ref[pl.ds(seed, 1), :].astype(BF16).astype(F32)
        )
    shifted = dot(latent_ref[...].astype(BF16), w_in.astype(BF16)) * 0.5
    one_half = (0.5 * w_one).astype(BF16)
    two = w_two.astype(BF16)

    def step(number, carry):
        rows = pl.ds(pl.multiple_of(number * tile, tile), tile)
        base = 0.5 * base_ref[rows, :].astype(BF16).astype(F32)
        for member in range(batch):
            hidden, slope_gen = silu_parts(base + shifted[member : member + 1, :])
            hidden_half = hidden.astype(BF16)
            middle, slope_mid = silu_parts(dot(hidden_half, one_half))
            middle_half = middle.astype(BF16)
            fake = hidden_half.astype(F32) + dot(middle_half, two)
            fakes_ref[member, rows, :] = fake.astype(BF16)
            hidden_ref[member, rows, :] = hidden_half
            middle_ref[member, rows, :] = middle_half
            gen_slope_ref[member, rows, :] = slope_gen
            mid_slope_ref[member, rows, :] = slope_mid
        return carry

    lax.fori_loop(0, places // tile, step, 0)


def gen_body(which, tile, seed_ref, bank_ref, in_ref, base_ref, one_ref, two_ref, *outs):
    seeds = [seed_ref[which, member] for member in range(seed_ref.shape[1])]
    gen_forward(seeds, bank_ref, in_ref[...], base_ref, one_ref[...], two_ref[...], outs, tile)


def stored_shapes(batch, places, channels):
    whole = (batch, places, channels)
    return [
        shape(whole, BF16),
        shape(whole, BF16),
        shape(whole, BF16),
        shape(whole, F32),
        shape(whole, F32),
        shape((8, channels), F32),
    ]


def generate(seed, which, bank, weights, tile=256):
    places, channels = weights[1].shape
    outs = stored_shapes(seed.shape[1], places, channels)
    return call(functools.partial(gen_body, which, tile), outs, n_inputs=6, smem=(0,))(
        seed, bank, *weights
    )


def gen_back_body(which, tile, judges, batch, *refs):
    refs = list(refs)
    units = [refs.pop(0) for _ in range(judges)]
    slopes = [refs.pop(0) for _ in range(judges)]
    hidden_ref, middle_ref, gen_slope_ref, mid_slope_ref, latent_ref = [refs.pop(0) for _ in range(5)]
    in_ref, base_ref, one_ref, two_ref = [refs.pop(0) for _ in range(4)]
    if which is not None:
        seed_ref, bank_ref = [refs.pop(0) for _ in range(2)]
    new_in, new_base, new_one, new_two = [refs.pop(0) for _ in range(4)]
    nexts = [refs.pop(0) for _ in range(6)] if which is not None else None
    one_turned, two_turned, sum_one, sum_two, sum_rows = refs
    places, channels = base_ref.shape
    base_step = BASE_RATE * places * 0.5

    one_turned[...] = one_ref[...].T.astype(BF16)
    two_turned[...] = (0.5 * two_ref[...]).T.astype(BF16)
    sum_one[...] = jnp.zeros_like(sum_one)
    sum_two[...] = jnp.zeros_like(sum_two)
    sum_rows[...] = jnp.zeros_like(sum_rows)

    def step(number, carry):
        rows = pl.ds(pl.multiple_of(number * tile, tile), tile)
        total = None
        for member in range(batch):
            cotangent = None
            for unit_ref, slope_ref in zip(units, slopes):
                part = slope_ref[member : member + 1, :] * unit_ref[member, rows, :].astype(F32)
                cotangent = part if cotangent is None else cotangent + part
            cotangent_half = cotangent.astype(BF16)
            inner = dot(cotangent_half, two_turned[...]) * mid_slope_ref[member, rows, :]
            inner_half = inner.astype(BF16)
            outer = (cotangent + dot(inner_half, one_turned[...])) * gen_slope_ref[member, rows, :]
            sum_two[...] += dot_rows(middle_ref[member, rows, :], cotangent_half)
            sum_one[...] += dot_rows(hidden_ref[member, rows, :], inner_half)
            sum_rows[member] += col_sums(outer)
            total = outer if total is None else total + outer
        new_base[rows, :] = base_ref[rows, :] - base_step * total
        return carry

    lax.fori_loop(0, places // tile, step, 0)
    new_one[...] = one_ref[...] - LEARN_RATE * sum_one[...]
    new_two[...] = two_ref[...] - LEARN_RATE * sum_two[...]
    latent_turned = latent_ref[...].T
    grad_in = jnp.zeros((channels, channels), F32)
    for member in range(batch):
        row = 0.5 * jnp.sum(sum_rows[member], axis=0, keepdims=True)
        grad_in = grad_in + latent_turned[:, member : member + 1] * row
    new_in[...] = in_ref[...] - LEARN_RATE * grad_in
    if which is not None:
        seeds = [seed_ref[which, member] for member in range(batch)]
        gen_forward(seeds, bank_ref, new_in[...], new_base, new_one[...], new_two[...], nexts, tile)


def gen_back(units, slopes, stored, weights, which, seed, bank, tile=256):
    batch, places, channels = units[0].shape
    square = (channels, channels)
    operands = list(units) + list(slopes) + list(stored[1:]) + list(weights)
    outs = [shape(member.shape, F32) for member in weights]
    smem = ()
    if which is not None:
        smem = (len(operands),)
        operands = operands + [seed, bank]
        outs = outs + stored_shapes(batch, places, channels)
    scratch = [
        pltpu.VMEM(square, BF16),
        pltpu.VMEM(square, BF16),
        pltpu.VMEM(square, F32),
        pltpu.VMEM(square, F32),
        pltpu.VMEM((batch, 8, channels), F32),
    ]
    body = functools.partial(gen_back_body, which, tile, len(units), batch)
    results = call(body, outs, scratch, n_inputs=len(operands), smem=smem)(*operands)
    return results[:4], results[4:]


def disc_update_body(batch, reals, is_last, grads_ref, *refs):
    refs = list(refs)
    returns = [refs.pop(0) for _ in range(4)]
    params = [refs.pop(0) for _ in range(3)]
    before = refs.pop(0) if is_last else None
    news = [refs.pop(0) for _ in range(3)]
    last_ref = refs.pop(0)
    channels = params[0].shape[0]
    one = grads_ref[0:channels, :]
    two = grads_ref[channels : 2 * channels, :]
    out = grads_ref[HEAD : HEAD + 1, :]
    verdicts = [grads_ref[HEAD + 1 + i : HEAD + 2 + i, :] for i in range(batch + reals)]
    fakes = verdicts[:batch]
    for back in returns:
        one = one + back[0:channels, :].astype(F32)
        two = two + back[channels : 2 * channels, :].astype(F32)
        tail = back[HEAD:PACKET, :].astype(F32)
        out = out + (tail[0:1, :] + tail[1:2, :])
        for i in range(batch):
            fakes.append(tail[2 + 2 * i : 3 + 2 * i, :] + tail[3 + 2 * i : 4 + 2 * i, :])
    verdicts = fakes + verdicts[batch:]
    updated = [
        member[...] - LEARN_RATE * grad for member, grad in zip(params, (one, two, out))
    ]
    for new, value in zip(news, updated):
        new[...] = value
    lanes = lax.broadcasted_iota(jnp.int32, (1, channels), 1)
    line = jnp.zeros((1, channels), F32)
    for place, value in enumerate(verdicts):
        line = jnp.where(lanes == place, value, line)
    count = len(verdicts)
    if is_last:
        last_ref[0:1, :] = before[0:1, 0:count]
        last_ref[1:2, :] = line[:, 0:count]
    else:
        last_ref[...] = line
        write_packet(refs[0], *updated)


def disc_update(grads, returns, params, before, batch, reals):
    is_last = before is not None
    operands = [grads] + list(returns) + list(params) + ([before] if is_last else [])
    outs = [shape(member.shape, F32) for member in params]
    if is_last:
        outs = outs + [shape((STEPS, 5 * batch + reals), F32)]
    else:
        outs = outs + [shape((1, 128), F32), shape((PACKET, 128), BF16)]
    body = functools.partial(disc_update_body, batch, reals, is_last)
    return call(body, outs, n_inputs=len(operands))(*operands)


def shifted(block, axis, distance):
    count = lax.axis_size(axis)
    return lax.ppermute(block, axis, [(i, (i + distance) % count) for i in range(count)])


SLOTS = (("row", 1), ("row", -1), ("col", 1), ("col", -1))


def on_device(
    data, real_index, latent_seed, latent_bank, g_in, g_base, g_one, g_two, d_one, d_two, d_out
):
    batch = latent_seed.shape[3]
    reals = real_index.shape[3]
    gens = [member[0, 0] for member in (g_in, g_base, g_one, g_two)]
    discs = [d_one[0, 0], d_two[0, 0], d_out[0]]
    seed = latent_seed[0, 0]
    index = real_index[0, 0]
    samples = data[0, 0]
    packet = pack(*discs)
    stored = None
    verdict = None
    for step in range(STEPS):
        is_last = step == STEPS - 1
        arrived = [shifted(packet, axis, -distance) for axis, distance in SLOTS]
        if stored is None:
            stored = generate(seed, step, latent_bank, gens)
        fakes = stored[0]
        own_grads, own_unit, own_slope = judge(packet, fakes, samples, index[step])
        units = [own_unit]
        slopes = [own_slope]
        returns = []
        for (axis, distance), theirs in zip(SLOTS, arrived):
            grads, unit, slope = judge(theirs, fakes)
            returns.append(shifted(grads, axis, distance))
            units.append(unit)
            slopes.append(slope)
        gens, stored = gen_back(
            units, slopes, stored, gens, None if is_last else step + 1, seed, latent_bank
        )
        results = disc_update(
            own_grads, returns, discs, verdict if is_last else None, batch, reals
        )
        discs = results[:3]
        verdict = results[3]
        packet = None if is_last else results[4]
    finals = [member[None, None] for member in gens] + [
        discs[0][None, None],
        discs[1][None, None],
        discs[2][None],
        verdict[None, None],
    ]
    return tuple(finals)


def solution(mesh):
    matrix = P("row", "col", None, None)
    return jax.shard_map(
        on_device,
        mesh=mesh,
        in_specs=(
            P("row", "col", None, None, None),
            matrix,
            matrix,
            P(),
            matrix,
            matrix,
            matrix,
            matrix,
            matrix,
            matrix,
            P("row", "col", None),
        ),
        out_specs=(
            matrix,
            matrix,
            matrix,
            matrix,
            matrix,
            matrix,
            P("row", "col", None),
            matrix,
        ),
        check_vma=False,
    )
```

profile of v0, /device:TPU:0, one launch (start us, length us, event | category | flops | bytes accessed | tf_op | source)
XLA Modules:
  0.0 100.9 jit_solution(3244842656505389918)
XLA Ops:
  3.1 4.5 %collective-permute-start = (bf16[272,128]{1,0:T(8,128)(2,1)S(1)}, bf16[272,128]{1,0:T(8,128)(2,1)S(1)}, u32[]{:S(2)}, u32[]{:S(2)}) collective-permute-start(bf16[272,128]{1,0:T(8,128)(2,1)S(1)} %shard_map.170.refs_1_), channel_id=1, source_target_pairs={{0,112},{16,0},{32,16},{48,32},{64,48},{80,64},{96,80},{112,96},{1... | collective-permute-start | bytes 208904 | tf_op jit(solution)/shard_map/ppermute | solution.py:420
  7.6 4.9 %collective-permute-start.4 = (bf16[272,128]{1,0:T(8,128)(2,1)S(1)}, bf16[272,128]{1,0:T(8,128)(2,1)S(1)}, u32[]{:S(2)}, u32[]{:S(2)}) collective-permute-start(bf16[272,128]{1,0:T(8,128)(2,1)S(1)} %shard_map.170.refs_1_), channel_id=1, source_target_pairs={{0,15},{1,0},{2,1},{3,2},{4,3},{5,4},{6,5},{7,6},{8,7},{9,8},{10,9... | collective-permute-start | bytes 208904 | tf_op jit(solution)/shard_map/ppermute | solution.py:420
  13.3 1.0 %copy-done.1 = f32[1,1,1024,128]{3,2,1,0:T(8,128)S(1)} copy-done((f32[1,1,1024,128]{3,2,1,0:T(8,128)S(1)}, f32[1,1,1024,128]{3,2,1,0:T(8,128)}, u32[]{:S(2)}) %copy-start.1) | copy-done | bytes 524312
  14.3 0.9 copy-done.3
  18.4 2.0 %shard_map.171 = (bf16[2,1024,128]{2,1,0:T(8,128)(2,1)S(1)}, bf16[2,1024,128]{2,1,0:T(8,128)(2,1)S(1)}, bf16[2,1024,128]{2,1,0:T(8,128)(2,1)S(1)}, f32[2,1024,12...) custom-call(s32[2,2]{1,0:T(2,128)S(1)} %bitcast.37, f32[256,128]{1,0:T(8,128)S(1)} %copy-done.3, ...), custom_call_target="tpu_custom_call" | custom-call | tf_op jit(solution)/shard_map/pallas_call | solution.py:287
  20.5 3.8 %shard_map.173 = (bf16[272,128]{1,0:T(8,128)(2,1)S(1)}, bf16[2,1024,128]{2,1,0:T(8,128)(2,1)S(1)}, f32[8,128]{1,0:T(8,128)S(1)}) custom-call(bf16[272,128]{1,0:T(8,128)(2,1)S(1)} %collective-permute-done.refs_0_, bf16[2,1024,128]{2,1,0:T(8,128)(2,1)S(1)} %get-tuple-element.67.refs_2_.refs_1_), custom_call_target="tpu_custom_call" | custom-call | flops 402653184 | bytes 2097152 | tf_op jit(solution)/shard_map/pallas_call | solution.py:224
  24.4 3.8 %shard_map.174 = (bf16[272,128]{1,0:T(8,128)(2,1)S(1)}, bf16[2,1024,128]{2,1,0:T(8,128)(2,1)S(1)}, f32[8,128]{1,0:T(8,128)S(1)}) custom-call(bf16[272,128]{1,0:T(8,128)(2,1)S(1)} %collective-permute-done.2.refs_0_, bf16[2,1024,128]{2,1,0:T(8,128)(2,1)S(1)} %get-tuple-element.67.refs_2_.refs_1_), custom_call_target="tpu_custom_call" | custom-call | flops 402653184 | bytes 2097152 | tf_op jit(solution)/shard_map/pallas_call | solution.py:224
  28.3 4.2 %collective-permute-start.3 = (bf16[272,128]{1,0:T(8,128)(2,1)S(1)}, bf16[272,128]{1,0:T(8,128)(2,1)S(1)}, u32[]{:S(2)}, u32[]{:S(2)}) collective-permute-start(bf16[272,128]{1,0:T(8,128)(2,1)S(1)} %get-tuple-element.70), channel_id=1, source_target_pairs={{0,112},{16,0},{32,16},{48,32},{64,48},{80,64},{96,80},{112,96},{1... | collective-permute-start | bytes 208904 | tf_op jit(solution)/shard_map/ppermute | solution.py:420
  32.4 3.8 %shard_map.175 = (bf16[272,128]{1,0:T(8,128)(2,1)S(1)}, bf16[2,1024,128]{2,1,0:T(8,128)(2,1)S(1)}, f32[8,128]{1,0:T(8,128)S(1)}) custom-call(bf16[272,128]{1,0:T(8,128)(2,1)S(1)} %collective-permute-done.4.refs_0_, bf16[2,1024,128]{2,1,0:T(8,128)(2,1)S(1)} %get-tuple-element.67.refs_2_.refs_1_), custom_call_target="tpu_custom_call" | custom-call | flops 402653184 | bytes 2097152 | tf_op jit(solution)/shard_map/pallas_call | solution.py:224
  36.4 3.8 %shard_map.176 = (bf16[272,128]{1,0:T(8,128)(2,1)S(1)}, bf16[2,1024,128]{2,1,0:T(8,128)(2,1)S(1)}, f32[8,128]{1,0:T(8,128)S(1)}) custom-call(bf16[272,128]{1,0:T(8,128)(2,1)S(1)} %collective-permute-done.6.refs_0_, bf16[2,1024,128]{2,1,0:T(8,128)(2,1)S(1)} %get-tuple-element.67.refs_2_.refs_1_), custom_call_target="tpu_custom_call" | custom-call | flops 402653184 | bytes 2097152 | tf_op jit(solution)/shard_map/pallas_call | solution.py:224
  40.2 5.4 %collective-permute-start.7 = (bf16[272,128]{1,0:T(8,128)(2,1)S(1)}, bf16[272,128]{1,0:T(8,128)(2,1)S(1)}, u32[]{:S(2)}, u32[]{:S(2)}) collective-permute-start(bf16[272,128]{1,0:T(8,128)(2,1)S(1)} %get-tuple-element.72), channel_id=1, source_target_pairs={{0,15},{1,0},{2,1},{3,2},{4,3},{5,4},{6,5},{7,6},{8,7},{9,8},{10,9... | collective-permute-start | bytes 208904 | tf_op jit(solution)/shard_map/ppermute | solution.py:420
  45.6 3.4 %copy-done = bf16[1,1,32,1024,128]{4,3,2,1,0:T(8,128)(2,1)S(1)} copy-done((bf16[1,1,32,1024,128]{4,3,2,1,0:T(8,128)(2,1)S(1)}, bf16[1,1,32,1024,128]{4,3,2,1,0:T(8,128)(2,1)}, u32[]{:S(2)}) %copy-start) | copy-done | bytes 8388632
  49.0 8.1 %shard_map.172 = (f32[272,128]{1,0:T(8,128)S(1)}, bf16[2,1024,128]{2,1,0:T(8,128)(2,1)S(1)}, f32[8,128]{1,0:T(8,128)S(1)}) custom-call(s32[2]{0:T(128)S(1)} %get-tuple-element.126.refs_0_, bf16[272,128]{1,0:T(8,128)(2,1)S(1)} %shard_map.170.refs_1_, bf16[2,1024,128]{2,1,0:T(8,128)(2,1)S(1)} %get-tuple-element.67.refs_2_.refs_1_, ...), custom_call_target="tpu_custom_call" | custom-call | flops 805306368 | bytes 2097152 | tf_op jit(solution)/shard_map/pallas_call | solution.py:224
  57.3 1.2 %collective-permute-start.8 = (bf16[272,128]{1,0:T(8,128)(2,1)S(1)}, bf16[272,128]{1,0:T(8,128)(2,1)S(1)}, u32[]{:S(2)}, u32[]{:S(2)}) collective-permute-start(bf16[272,128]{1,0:T(8,128)(2,1)S(1)} %get-tuple-element.73.refs_1_), channel_id=1, source_target_pairs={{0,112},{16,0},{32,16},{48,32},{64,48},{80,64},{96,80},{112,96},{1... | collective-permute-start | bytes 208904 | tf_op jit(solution)/shard_map/ppermute | solution.py:420
  58.5 0.9 collective-permute-start.9
  59.5 4.0 %shard_map.178 = (f32[128,128]{1,0:T(8,128)S(1)}, f32[1024,128]{1,0:T(8,128)S(1)}, f32[128,128]{1,0:T(8,128)S(1)}, f32[128,128]{1,0:T(8,128)S(1)}, bf16[2,1024,1...) custom-call(bf16[2,1024,128]{2,1,0:T(8,128)(2,1)S(1)} %get-tuple-ele, ...), custom_call_target="tpu_custom_call" | custom-call | tf_op jit(solution)/shard_map/pallas_call | solution.py:363
  64.0 3.8 %shard_map.180 = (bf16[272,128]{1,0:T(8,128)(2,1)S(1)}, bf16[2,1024,128]{2,1,0:T(8,128)(2,1)S(1)}, f32[8,128]{1,0:T(8,128)S(1)}) custom-call(bf16[272,128]{1,0:T(8,128)(2,1)S(1)} %collective-permute-done.8.refs_0_, bf16[2,1024,128]{2,1,0:T(8,128)(2,1)S(1)} %get-tuple-element.89.refs_2_.refs_1_), custom_call_target="tpu_custom_call" | custom-call | flops 402653184 | bytes 2097152 | tf_op jit(solution)/shard_map/pallas_call | solution.py:224
  68.0 3.8 %shard_map.181 = (bf16[272,128]{1,0:T(8,128)(2,1)S(1)}, bf16[2,1024,128]{2,1,0:T(8,128)(2,1)S(1)}, f32[8,128]{1,0:T(8,128)S(1)}) custom-call(bf16[272,128]{1,0:T(8,128)(2,1)S(1)} %collective-permute-done.9.refs_0_, bf16[2,1024,128]{2,1,0:T(8,128)(2,1)S(1)} %get-tuple-element.89.refs_2_.refs_1_), custom_call_target="tpu_custom_call" | custom-call | flops 402653184 | bytes 2097152 | tf_op jit(solution)/shard_map/pallas_call | solution.py:224
  71.8 4.4 %collective-permute-start.13 = (bf16[272,128]{1,0:T(8,128)(2,1)S(1)}, bf16[272,128]{1,0:T(8,128)(2,1)S(1)}, u32[]{:S(2)}, u32[]{:S(2)}) collective-permute-start(bf16[272,128]{1,0:T(8,128)(2,1)S(1)} %get-tuple-element.115), channel_id=1, source_target_pairs={{0,112},{16,0},{32,16},{48,32},{64,48},{80,64},{96,80},{112,96},{1... | collective-permute-start | bytes 208904 | tf_op jit(solution)/shard_map/ppermute | solution.py:420
  76.2 3.8 %shard_map.182 = (bf16[272,128]{1,0:T(8,128)(2,1)S(1)}, bf16[2,1024,128]{2,1,0:T(8,128)(2,1)S(1)}, f32[8,128]{1,0:T(8,128)S(1)}) custom-call(bf16[272,128]{1,0:T(8,128)(2,1)S(1)} %collective-permute-done.10.refs_0_, bf16[2,1024,128]{2,1,0:T(8,128)(2,1)S(1)} %get-tuple-element.89.refs_2_.refs_1_), custom_call_target="tpu_custom_call" | custom-call | flops 402653184 | bytes 2097152 | tf_op jit(solution)/shard_map/pallas_call | solution.py:224
  80.1 3.8 %shard_map.183 = (bf16[272,128]{1,0:T(8,128)(2,1)S(1)}, bf16[2,1024,128]{2,1,0:T(8,128)(2,1)S(1)}, f32[8,128]{1,0:T(8,128)S(1)}) custom-call(bf16[272,128]{1,0:T(8,128)(2,1)S(1)} %collective-permute-done.11.refs_0_, bf16[2,1024,128]{2,1,0:T(8,128)(2,1)S(1)} %get-tuple-element.89.refs_2_.refs_1_), custom_call_target="tpu_custom_call" | custom-call | flops 402653184 | bytes 2097152 | tf_op jit(solution)/shard_map/pallas_call | solution.py:224
  84.0 5.4 %collective-permute-start.15 = (bf16[272,128]{1,0:T(8,128)(2,1)S(1)}, bf16[272,128]{1,0:T(8,128)(2,1)S(1)}, u32[]{:S(2)}, u32[]{:S(2)}) collective-permute-start(bf16[272,128]{1,0:T(8,128)(2,1)S(1)} %get-tuple-element.117), channel_id=1, source_target_pairs={{0,15},{1,0},{2,1},{3,2},{4,3},{5,4},{6,5},{7,6},{8,7},{9,8},{10,9... | collective-permute-start | bytes 208904 | tf_op jit(solution)/shard_map/ppermute | solution.py:420
  89.4 8.2 %shard_map.179 = (f32[272,128]{1,0:T(8,128)S(1)}, bf16[2,1024,128]{2,1,0:T(8,128)(2,1)S(1)}, f32[8,128]{1,0:T(8,128)S(1)}) custom-call(s32[2]{0:T(128)S(1)} %get-tuple-element.127.refs_0_, bf16[272,128]{1,0:T(8,128)(2,1)S(1)} %get-tuple-element.73.refs_1_, bf16[2,1024,128]{2,1,0:T(8,128)(2,1)S(1)} %get-tuple-element.89.refs_2_.refs_1_, ...), custom_call_target="tpu_custom_call" | custom-call | flops 805306368 | bytes 2097152 | tf_op jit(solution)/shard_map/pallas_call | solution.py:224
  97.5 2.6 %shard_map.184 = (f32[128,128]{1,0:T(8,128)}, f32[1024,128]{1,0:T(8,128)}, f32[128,128]{1,0:T(8,128)}, f32[128,128]{1,0:T(8,128)}) custom-call(bf16[2,1024,128]{2,1,0:T(8,128)(2,1)S(1)} %get-tuple-element.90.refs_0_, bf16[2,1024,128]{2,1,0:T(8,128)(2,1)S(1)} %get-tuple-element.91.refs_1_, bf16[2,1024,128]{2,1,0:T(8,128)(2,1)S(1)} %get-tuple-element.92.refs_2_, ...), custom_call_target="tpu_custom_call" | custom-call | tf_op jit(solution)/shard_map/pallas_call | solution.py:363
  (68 shorter events, 8.1 us)
Async XLA Ops:
  0.6 58.8 %copy-start.4 = (f32[256,128]{1,0:T(8,128)S(1)}, f32[256,128]{1,0:T(8,128)}, u32[]{:S(2)}) copy-start(f32[256,128]{1,0:T(8,128)} %refs_20_.1) | copy-start | bytes 393220
  0.6 58.8 %copy-start.6 = (f32[1,1,128,128]{3,2,1,0:T(8,128)S(1)}, f32[1,1,128,128]{3,2,1,0:T(8,128)}, u32[]{:S(2)}) copy-start(f32[1,1,128,128]{3,2,1,0:T(8,128)} %param.15) | copy-start | bytes 196612
  3.0 54.2 %copy-start.18 = (f32[1,1,128]{2,1,0:T(1,128)S(1)}, f32[1,1,128]{2,1,0:T(1,128)}, u32[]{:S(2)}) copy-start(f32[1,1,128]{2,1,0:T(1,128)} %param.21) | copy-start | bytes 1540
  3.0 56.4 %copy-start.16 = (s32[1,1,2,2]{3,2,1,0:T(2,128)S(1)}, s32[1,1,2,2]{3,2,1,0:T(2,128)}, u32[]{:S(2)}) copy-start(s32[1,1,2,2]{3,2,1,0:T(2,128)} %param.13) | copy-start | bytes 52
  3.1 17.4 %collective-permute-start = (bf16[272,128]{1,0:T(8,128)(2,1)S(1)}, bf16[272,128]{1,0:T(8,128)(2,1)S(1)}, u32[]{:S(2)}, u32[]{:S(2)}) collective-permute-start(bf16[272,128]{1,0:T(8,128)(2,1)S(1)} %shard_map.170.refs_1_), channel_id=1, source_target_pairs={{0,112},{16,0},{32,16},{48,32},{64,48},{80,64},{96,80},{112,96},{1... | collective-permute-start | bytes 208904 | tf_op jit(solution)/shard_map/ppermute | solution.py:420
  7.6 16.8 %collective-permute-start.2 = (bf16[272,128]{1,0:T(8,128)(2,1)S(1)}, bf16[272,128]{1,0:T(8,128)(2,1)S(1)}, u32[]{:S(2)}, u32[]{:S(2)}) collective-permute-start(bf16[272,128]{1,0:T(8,128)(2,1)S(1)} %shard_map.170.refs_1_), channel_id=1, source_target_pairs={{0,16},{16,32},{32,48},{48,64},{64,80},{80,96},{96,112},{112,0},{1... | collective-permute-start | bytes 208904 | tf_op jit(solution)/shard_map/ppermute | solution.py:420
  7.6 24.9 %collective-permute-start.4 = (bf16[272,128]{1,0:T(8,128)(2,1)S(1)}, bf16[272,128]{1,0:T(8,128)(2,1)S(1)}, u32[]{:S(2)}, u32[]{:S(2)}) collective-permute-start(bf16[272,128]{1,0:T(8,128)(2,1)S(1)} %shard_map.170.refs_1_), channel_id=1, source_target_pairs={{0,15},{1,0},{2,1},{3,2},{4,3},{5,4},{6,5},{7,6},{8,7},{9,8},{10,9... | collective-permute-start | bytes 208904 | tf_op jit(solution)/shard_map/ppermute | solution.py:420
  12.5 23.9 %collective-permute-start.6 = (bf16[272,128]{1,0:T(8,128)(2,1)S(1)}, bf16[272,128]{1,0:T(8,128)(2,1)S(1)}, u32[]{:S(2)}, u32[]{:S(2)}) collective-permute-start(bf16[272,128]{1,0:T(8,128)(2,1)S(1)} %shard_map.170.refs_1_), channel_id=1, source_target_pairs={{0,1},{1,2},{2,3},{3,4},{4,5},{5,6},{6,7},{7,8},{8,9},{9,10},{10,1... | collective-permute-start | bytes 208904 | tf_op jit(solution)/shard_map/ppermute | solution.py:420
  18.4 41.0 %copy-start.2 = (f32[1,1,1024,128]{3,2,1,0:T(8,128)S(1)}, f32[1,1,1024,128]{3,2,1,0:T(8,128)}, u32[]{:S(2)}) copy-start(f32[1,1,1024,128]{3,2,1,0:T(8,128)} %param.16) | copy-start | bytes 1572868
  18.4 41.0 %copy-start.8 = (f32[1,1,128,128]{3,2,1,0:T(8,128)S(1)}, f32[1,1,128,128]{3,2,1,0:T(8,128)}, u32[]{:S(2)}) copy-start(f32[1,1,128,128]{3,2,1,0:T(8,128)} %param.17) | copy-start | bytes 196612
  18.4 41.0 %copy-start.10 = (f32[1,1,128,128]{3,2,1,0:T(8,128)S(1)}, f32[1,1,128,128]{3,2,1,0:T(8,128)}, u32[]{:S(2)}) copy-start(f32[1,1,128,128]{3,2,1,0:T(8,128)} %param.18) | copy-start | bytes 196612
  24.3 32.8 %collective-permute-start.1 = (bf16[272,128]{1,0:T(8,128)(2,1)S(1)}, bf16[272,128]{1,0:T(8,128)(2,1)S(1)}, u32[]{:S(2)}, u32[]{:S(2)}) collective-permute-start(bf16[272,128]{1,0:T(8,128)(2,1)S(1)} %get-tuple-element.69), channel_id=1, source_target_pairs={{0,16},{16,32},{32,48},{48,64},{64,80},{80,96},{96,112},{112,0},{1... | collective-permute-start | bytes 208904 | tf_op jit(solution)/shard_map/ppermute | solution.py:420
  28.3 28.9 %collective-permute-start.3 = (bf16[272,128]{1,0:T(8,128)(2,1)S(1)}, bf16[272,128]{1,0:T(8,128)(2,1)S(1)}, u32[]{:S(2)}, u32[]{:S(2)}) collective-permute-start(bf16[272,128]{1,0:T(8,128)(2,1)S(1)} %get-tuple-element.70), channel_id=1, source_target_pairs={{0,112},{16,0},{32,16},{48,32},{64,48},{80,64},{96,80},{112,96},{1... | collective-permute-start | bytes 208904 | tf_op jit(solution)/shard_map/ppermute | solution.py:420
  36.3 20.9 %collective-permute-start.5 = (bf16[272,128]{1,0:T(8,128)(2,1)S(1)}, bf16[272,128]{1,0:T(8,128)(2,1)S(1)}, u32[]{:S(2)}, u32[]{:S(2)}) collective-permute-start(bf16[272,128]{1,0:T(8,128)(2,1)S(1)} %get-tuple-element.71), channel_id=1, source_target_pairs={{0,1},{1,2},{2,3},{3,4},{4,5},{5,6},{6,7},{7,8},{8,9},{9,10},{10,1... | collective-permute-start | bytes 208904 | tf_op jit(solution)/shard_map/ppermute | solution.py:420
  40.2 17.0 %collective-permute-start.7 = (bf16[272,128]{1,0:T(8,128)(2,1)S(1)}, bf16[272,128]{1,0:T(8,128)(2,1)S(1)}, u32[]{:S(2)}, u32[]{:S(2)}) collective-permute-start(bf16[272,128]{1,0:T(8,128)(2,1)S(1)} %get-tuple-element.72), channel_id=1, source_target_pairs={{0,15},{1,0},{2,1},{3,2},{4,3},{5,4},{6,5},{7,6},{8,7},{9,8},{10,9... | collective-permute-start | bytes 208904 | tf_op jit(solution)/shard_map/ppermute | solution.py:420
  49.0 40.4 %slice-start = ((s8[8388608]{0:T(1024)(128)(4,1)}), s8[4194304]{0:T(1024)(128)(4,1)S(1)}, s32[]{:S(2)}) async-start(s8[8388608]{0:T(1024)(128)(4,1)} %bitcast.22), calls=%async_computation | async-start | bytes 8388608
  57.3 6.7 %collective-permute-start.8 = (bf16[272,128]{1,0:T(8,128)(2,1)S(1)}, bf16[272,128]{1,0:T(8,128)(2,1)S(1)}, u32[]{:S(2)}, u32[]{:S(2)}) collective-permute-start(bf16[272,128]{1,0:T(8,128)(2,1)S(1)} %get-tuple-element.73.refs_1_), channel_id=1, source_target_pairs={{0,112},{16,0},{32,16},{48,32},{64,48},{80,64},{96,80},{112,96},{1... | collective-permute-start | bytes 208904 | tf_op jit(solution)/shard_map/ppermute | solution.py:420
  58.5 9.4 %collective-permute-start.9 = (bf16[272,128]{1,0:T(8,128)(2,1)S(1)}, bf16[272,128]{1,0:T(8,128)(2,1)S(1)}, u32[]{:S(2)}, u32[]{:S(2)}) collective-permute-start(bf16[272,128]{1,0:T(8,128)(2,1)S(1)} %get-tuple-element.73.refs_1_), channel_id=1, source_target_pairs={{0,16},{16,32},{32,48},{48,64},{64,80},{80,96},{96,112},{112,0},{1... | collective-permute-start | bytes 208904 | tf_op jit(solution)/shard_map/ppermute | solution.py:420
  63.4 12.7 %collective-permute-start.10 = (bf16[272,128]{1,0:T(8,128)(2,1)S(1)}, bf16[272,128]{1,0:T(8,128)(2,1)S(1)}, u32[]{:S(2)}, u32[]{:S(2)}) collective-permute-start(bf16[272,128]{1,0:T(8,128)(2,1)S(1)} %get-tuple-element.73.refs_1_), channel_id=1, source_target_pairs={{0,15},{1,0},{2,1},{3,2},{4,3},{5,4},{6,5},{7,6},{8,7},{9,8},{10,9... | collective-permute-start | bytes 208904 | tf_op jit(solution)/shard_map/ppermute | solution.py:420
  63.5 16.6 %collective-permute-start.11 = (bf16[272,128]{1,0:T(8,128)(2,1)S(1)}, bf16[272,128]{1,0:T(8,128)(2,1)S(1)}, u32[]{:S(2)}, u32[]{:S(2)}) collective-permute-start(bf16[272,128]{1,0:T(8,128)(2,1)S(1)} %get-tuple-element.73.refs_1_), channel_id=1, source_target_pairs={{0,1},{1,2},{2,3},{3,4},{4,5},{5,6},{6,7},{7,8},{8,9},{9,10},{10,1... | collective-permute-start | bytes 208904 | tf_op jit(solution)/shard_map/ppermute | solution.py:420
  67.9 32.3 %collective-permute-start.12 = (bf16[272,128]{1,0:T(8,128)(2,1)S(1)}, bf16[272,128]{1,0:T(8,128)(2,1)S(1)}, u32[]{:S(2)}, u32[]{:S(2)}) collective-permute-start(bf16[272,128]{1,0:T(8,128)(2,1)S(1)} %get-tuple-element.114), channel_id=1, source_target_pairs={{0,16},{16,32},{32,48},{48,64},{64,80},{80,96},{96,112},{112,0},{1... | collective-permute-start | bytes 208904 | tf_op jit(solution)/shard_map/ppermute | solution.py:420
  71.8 28.4 %collective-permute-start.13 = (bf16[272,128]{1,0:T(8,128)(2,1)S(1)}, bf16[272,128]{1,0:T(8,128)(2,1)S(1)}, u32[]{:S(2)}, u32[]{:S(2)}) collective-permute-start(bf16[272,128]{1,0:T(8,128)(2,1)S(1)} %get-tuple-element.115), channel_id=1, source_target_pairs={{0,112},{16,0},{32,16},{48,32},{64,48},{80,64},{96,80},{112,96},{1... | collective-permute-start | bytes 208904 | tf_op jit(solution)/shard_map/ppermute | solution.py:420
  80.0 20.2 %collective-permute-start.14 = (bf16[272,128]{1,0:T(8,128)(2,1)S(1)}, bf16[272,128]{1,0:T(8,128)(2,1)S(1)}, u32[]{:S(2)}, u32[]{:S(2)}) collective-permute-start(bf16[272,128]{1,0:T(8,128)(2,1)S(1)} %get-tuple-element.116), channel_id=1, source_target_pairs={{0,1},{1,2},{2,3},{3,4},{4,5},{5,6},{6,7},{7,8},{8,9},{9,10},{10,1... | collective-permute-start | bytes 208904 | tf_op jit(solution)/shard_map/ppermute | solution.py:420
  84.0 16.2 %collective-permute-start.15 = (bf16[272,128]{1,0:T(8,128)(2,1)S(1)}, bf16[272,128]{1,0:T(8,128)(2,1)S(1)}, u32[]{:S(2)}, u32[]{:S(2)}) collective-permute-start(bf16[272,128]{1,0:T(8,128)(2,1)S(1)} %get-tuple-element.117), channel_id=1, source_target_pairs={{0,15},{1,0},{2,1},{3,2},{4,3},{5,4},{6,5},{7,6},{8,7},{9,8},{10,9... | collective-permute-start | bytes 208904 | tf_op jit(solution)/shard_map/ppermute | solution.py:420
  (13 other events, 118.4 us)
where the time goes:
time: 101 us
  Pallas kernels  56.4 us (56%)
  starting transfers between devices  31.8 us (31%)
  local copies, waits for them, and re-layouts  11.7 us (12%)
    pallas_call x10, Pallas kernels, judge(): pl.pallas_call(body, out_shape=tuple(outs), in_specs=in_specs, out_specs=...  47 us
    ppermute x16, starting transfers between devices, shifted(): lax.ppermute(block, axis, [(i, (i + distance) % count) for i in range(cou...  31.8 us
    unnamed x42, local copies, waits for them, and re-layouts  10.9 us
    pallas_call x2, Pallas kernels, gen_back(): call(body, outs, scratch, n_inputs=len(operands), smem=smem)(*operands)  6.6 us
  transfers between devices with their start and end apart: 16, of which 0 were waited for; matrix products, arithmetic and copies ran while one was open for 1% of the time, Pallas kernels for 55%

commit v1 on v0

v1 whole, which is shorter than its diff:
```python
import functools

import jax
import jax.numpy as jnp
from jax import lax
from jax.experimental import pallas as pl
from jax.experimental.pallas import tpu as pltpu
from jax.sharding import PartitionSpec as P

STEPS = 2
LEARN_RATE = 0.05
BASE_RATE = 0.1
PACKET = 272
HEAD = 256
VMEM_LIMIT = 24 * 1024 * 1024
F32 = jnp.float32
BF16 = jnp.bfloat16


def dot(left, right):
    return jnp.dot(left, right, preferred_element_type=F32)


def dot_rows(left, right):
    return lax.dot_general(left, right, (((0,), (0,)), ((), ())), preferred_element_type=F32)


def silu_parts(half):
    tanh_part = jnp.tanh(half)
    above = 1.0 + tanh_part
    value = half * above
    slope_twice = above + value * (1.0 - tanh_part)
    return value, slope_twice


def sigmoid(value):
    return 0.5 * (1.0 + jnp.tanh(0.5 * value))


def col_sums(tile):
    rows, channels = tile.shape
    return jnp.sum(tile.reshape(rows // 8, 8, channels), axis=0)


def split_two(value):
    high = value.astype(BF16)
    low = (value - high.astype(F32)).astype(BF16)
    return high, low


def shape(dims, dtype):
    return jax.ShapeDtypeStruct(dims, dtype)


def call(body, operands, out_shape, scratch=(), smem=(), hbm=(), flops=0):
    spaces = [pltpu.VMEM] * len(operands)
    for i in range(len(operands)):
        spaces[i] = pltpu.SMEM if i in smem else pltpu.HBM if i in hbm else pltpu.VMEM
    operands = [
        pltpu.with_memory_space_constraint(member, pltpu.HBM) if i in hbm else member
        for i, member in enumerate(operands)
    ]
    return pl.pallas_call(
        body,
        out_shape=tuple(out_shape),
        in_specs=[pl.BlockSpec(memory_space=space) for space in spaces],
        out_specs=tuple(pl.BlockSpec(memory_space=pltpu.VMEM) for _ in out_shape),
        scratch_shapes=list(scratch),
        compiler_params=pltpu.CompilerParams(vmem_limit_bytes=VMEM_LIMIT),
        cost_estimate=pl.CostEstimate(flops=flops, bytes_accessed=flops // 1000, transcendentals=0),
    )(*operands)


def start_all(pairs, semaphores):
    copies = [
        pltpu.make_async_copy(source, target, semaphores.at[i])
        for i, (source, target) in enumerate(pairs)
    ]
    for copy in copies:
        copy.start()
    return copies


def write_packet(packet_ref, one, two, rows):
    channels = one.shape[1]
    packet_ref[0:channels, :] = one.astype(BF16)
    packet_ref[channels:HEAD, :] = two.astype(BF16)
    spot = lax.broadcasted_iota(jnp.int32, (PACKET - HEAD, channels), 0)
    tail = jnp.zeros((PACKET - HEAD, channels), F32)
    for place, row in enumerate(rows):
        high, low = split_two(row)
        tail = jnp.where(spot == 2 * place, high.astype(F32), tail)
        tail = jnp.where(spot == 2 * place + 1, low.astype(F32), tail)
    packet_ref[HEAD:PACKET, :] = tail.astype(BF16)


def packet_row(tail, place):
    return tail[2 * place : 2 * place + 1, :] + tail[2 * place + 1 : 2 * place + 2, :]


def pack_body(one_hbm, two_hbm, out_hbm, packet_ref, one_ref, two_ref, out_ref, semaphores):
    pairs = [(one_hbm, one_ref), (two_hbm, two_ref), (out_hbm, out_ref)]
    for copy in start_all(pairs, semaphores):
        copy.wait()
    write_packet(packet_ref, one_ref[...], two_ref[...], [out_ref[...]])


def pack(params):
    outs = [shape((PACKET, params[0].shape[1]), BF16)] + [shape(m.shape, F32) for m in params]
    results = call(pack_body, params, outs, [pltpu.SemaphoreType.DMA((3,))], hbm=(0, 1, 2))
    return results[0], results[1:]


def dot_turned(left, right):
    return lax.dot_general(left, right, (((1,), (1,)), ((), ())), preferred_element_type=F32)


def unpack(packet_ref):
    channels = packet_ref.shape[1]
    tail = packet_ref[HEAD:PACKET, :].astype(F32)
    return packet_ref[0:channels, :], packet_ref[channels:HEAD, :], tail[0:1, :] + tail[1:2, :]


def both(left, right):
    blank = jnp.zeros_like(left)
    return jnp.concatenate(
        [jnp.concatenate([left, blank], axis=1), jnp.concatenate([blank, right], axis=1)], axis=0
    )


def judge_pair(images, one, two, out_row, shared):
    channels = images.shape[1] if shared else images.shape[1] // 2
    half = BF16(0.5)
    left = slice(0, channels)
    right = slice(channels, 2 * channels)
    one_both = both(*one)
    one_first = jnp.concatenate(one, axis=1) if shared else one_both
    first, slope_first = silu_parts(dot(images, one_first * half))
    first_half = first.astype(BF16)
    two_half = both(*two) * half
    image_half = 0.5 * images.astype(F32)
    if shared:
        image_half = jnp.concatenate([image_half, image_half], axis=1)
    feature, slope_out = silu_parts(image_half + dot(first_half, two_half))
    outer = (0.5 * out_row) * slope_out
    outer_half = outer.astype(BF16)
    inner_half = (dot_turned(outer_half, two_half) * slope_first).astype(BF16)
    unit = outer + dot_turned(inner_half, one_both)
    if shared:
        wide = dot_rows(images, inner_half)
        ones = [wide[:, left], wide[:, right]]
    else:
        ones = [dot_rows(images[:, part], inner_half[:, part]) for part in (left, right)]
    sums = jnp.sum(feature.reshape(-1, 8, 2 * channels), axis=0)
    sums = jnp.sum(sums, axis=0, keepdims=True)
    triples = [
        (ones[i], dot_rows(first_half[:, part], outer_half[:, part]), sums[:, part])
        for i, part in enumerate((left, right))
    ]
    return unit.astype(BF16), triples


def finish(sums, out_row, signs, places, lines_ref):
    count = len(sums)
    channels = out_row.shape[1]
    lines_ref[...] = jnp.zeros_like(lines_ref)
    for member in range(count):
        lines_ref[member : member + 1, :] = sums[member][2]
    features = lines_ref[...]
    scale = 1.0 / places
    verdicts = jnp.sum(features * out_row, axis=1, keepdims=True) * scale
    verdicts = jnp.broadcast_to(verdicts, features.shape)
    spot = lax.broadcasted_iota(jnp.int32, features.shape, 0)
    plus = sigmoid(verdicts) * scale
    minus = -sigmoid(-verdicts) * scale
    slopes = jnp.where(spot < signs, plus, minus)
    total_out = jnp.sum(features * slopes, axis=0, keepdims=True)
    total_one = None
    total_two = None
    for member in range(count):
        slope = slopes[member : member + 1, :]
        part_one = slope * sums[member][0]
        part_two = slope * sums[member][1]
        total_one = part_one if total_one is None else total_one + part_one
        total_two = part_two if total_two is None else total_two + part_two
    return verdicts, minus, total_one, total_two, total_out


def judge_own_body(step, batch, reals, packet_ref, fakes_ref, reals_ref, grads_ref, unit_ref, slope_ref, lines_ref):
    rows, channels = fakes_ref.shape
    places = rows // batch
    one, two, out_row = unpack(packet_ref)
    out_pair = jnp.concatenate([out_row, out_row], axis=1)
    kept = [None] * (batch + reals)
    for member in range(batch):
        span = slice(member * places, (member + 1) * places)
        images = jnp.concatenate([fakes_ref[span, :], reals_ref[step * reals + member]], axis=1)
        unit, triples = judge_pair(images, (one, one), (two, two), out_pair, False)
        unit_ref[span, :] = unit[:, 0:channels]
        kept[member], kept[batch + member] = triples
    verdicts, minus, total_one, total_two, total_out = finish(kept, out_row, batch, places, lines_ref)
    slope_ref[...] = minus
    grads_ref[0:channels, :] = total_one
    grads_ref[channels:HEAD, :] = total_two
    grads_ref[HEAD : HEAD + 8, :] = verdicts
    grads_ref[HEAD + 8 : PACKET, :] = jnp.broadcast_to(total_out, (8, channels))


def judge_own(packet, fakes, reals_rows, step, batch, reals):
    rows, channels = fakes.shape
    outs = [
        shape((PACKET, channels), F32),
        shape((rows, channels), BF16),
        shape((8, channels), F32),
    ]
    body = functools.partial(judge_own_body, step, batch, reals)
    flops = 4 * 6 * 2 * 1024 * 128 * 128
    return call(body, [packet, fakes, reals_rows], outs, [pltpu.VMEM((8, channels), F32)], flops=flops)


def judge_others_body(judges, batch, *refs):
    refs = list(refs)
    packets = [refs.pop(0) for _ in range(judges)]
    fakes_ref = refs.pop(0)
    refs.pop(0)
    grads = [refs.pop(0) for _ in range(judges)]
    units = [refs.pop(0) for _ in range(judges)]
    slope_ref = refs.pop(0)
    lines_ref = refs.pop(0)
    rows, channels = fakes_ref.shape
    places = rows // batch
    kept = [[None] * batch for _ in range(judges)]
    parts = [unpack(packet) for packet in packets]
    for pair in range(0, judges, 2):
        ones, twos, outs = zip(*parts[pair : pair + 2])
        out_pair = jnp.concatenate(outs, axis=1)
        for member in range(batch):
            span = slice(member * places, (member + 1) * places)
            unit, triples = judge_pair(fakes_ref[span, :], ones, twos, out_pair, True)
            for side in range(2):
                units[pair + side][span, :] = unit[:, side * channels : (side + 1) * channels]
                kept[pair + side][member] = triples[side]
    for which in range(judges):
        verdicts, minus, total_one, total_two, total_out = finish(
            kept[which], parts[which][2], batch, places, lines_ref.at[which]
        )
        slope_ref[which * batch : (which + 1) * batch, :] = minus[0:batch, :]
        tail = [total_out] + [verdicts[member : member + 1, :] for member in range(batch)]
        write_packet(grads[which], total_one, total_two, tail)


def judge_others(packets, fakes, batch, after):
    rows, channels = fakes.shape
    judges = len(packets)
    outs = [shape((PACKET, channels), BF16)] * judges
    outs = outs + [shape((rows, channels), BF16)] * judges
    outs = outs + [shape((judges * batch, channels), F32)]
    body = functools.partial(judge_others_body, judges, batch)
    scratch = [pltpu.VMEM((judges, 8, channels), F32)]
    flops = 8 * 6 * 2 * 1024 * 128 * 128
    results = call(body, list(packets) + [fakes, after], outs, scratch, flops=flops)
    return results[:judges], results[judges : 2 * judges], results[2 * judges]


def twice(tile):
    return jnp.concatenate([tile, tile], axis=1)


def gen_forward(latent, w_in, base, w_one, w_two, outs):
    fakes_ref, hidden_ref, middle_ref, gen_slope_ref, mid_slope_ref = outs
    places, channels = base.shape
    shifted = 0.5 * dot(latent.astype(BF16), w_in.astype(BF16))
    shift_row = jnp.concatenate([shifted[0:1, :], shifted[1:2, :]], axis=1)
    one = w_one.astype(BF16) * BF16(0.5)
    two = w_two.astype(BF16)
    hidden, slope_gen = silu_parts(twice(0.5 * base.astype(BF16).astype(F32)) + shift_row)
    hidden_half = hidden.astype(BF16)
    middle, slope_mid = silu_parts(dot(hidden_half, both(one, one)))
    middle_half = middle.astype(BF16)
    fakes = (hidden_half.astype(F32) + dot(middle_half, both(two, two))).astype(BF16)
    fakes_ref[0:places, :] = fakes[:, 0:channels]
    fakes_ref[places : 2 * places, :] = fakes[:, channels : 2 * channels]
    hidden_ref[...] = hidden_half
    middle_ref[...] = middle_half
    gen_slope_ref[...] = slope_gen
    mid_slope_ref[...] = slope_mid


def stored_shapes(places, channels):
    wide = (places, 2 * channels)
    return [
        shape((2 * places, channels), BF16),
        shape(wide, BF16),
        shape(wide, BF16),
        shape(wide, F32),
        shape(wide, F32),
    ]


def begin_body(batch, reals, seed_hbm, index_hbm, *refs):
    bank, data, *weights = refs[:6]
    weight_refs = refs[6:10]
    latent_ref, reals_ref = refs[10:12]
    outs = refs[12:17]
    raw_ref, seed_ref, index_ref, semaphores = refs[17:]
    count = len(weights)
    copies = start_all(list(zip(weights, weight_refs)), semaphores)
    chosen = start_all(
        [(seed_hbm, seed_ref), (index_hbm, index_ref)], semaphores.at[pl.ds(count, 2)]
    )
    raw_ref[...] = jnp.zeros_like(raw_ref)
    for copy in chosen:
        copy.wait()
    early = []
    late = []
    for step in range(STEPS):
        for member in range(batch):
            early.append(
                (bank.at[pl.ds(seed_ref[step, member], 1)], raw_ref.at[step, pl.ds(member, 1)])
            )
        for member in range(reals):
            late.append((data.at[index_ref[step, member]], reals_ref.at[step * reals + member]))
    rest = len(early + late)
    others = start_all(early + late, semaphores.at[pl.ds(count + 2, rest)])
    copies = copies + others
    for copy in copies[: count + len(early)]:
        copy.wait()
    latent_ref[...] = raw_ref[...].astype(BF16).astype(F32)
    w_in, base, w_one, w_two = [ref[...] for ref in weight_refs]
    gen_forward(latent_ref[0], w_in, base, w_one, w_two, outs)
    for copy in copies[count + len(early) :]:
        copy.wait()


def begin(seed, index, bank, data, weights):
    batch = seed.shape[1]
    reals = index.shape[1]
    places, channels = weights[1].shape
    outs = [shape(member.shape, F32) for member in weights]
    outs = outs + [shape((STEPS, 8, channels), F32), shape((STEPS * reals, places, channels), BF16)]
    outs = outs + stored_shapes(places, channels)
    scratch = [
        pltpu.VMEM((STEPS, 8, channels), F32),
        pltpu.SMEM(seed.shape, jnp.int32),
        pltpu.SMEM(index.shape, jnp.int32),
        pltpu.SemaphoreType.DMA((len(weights) + 2 + STEPS * (batch + reals),)),
    ]
    operands = [seed, index, bank, data] + list(weights)
    body = functools.partial(begin_body, batch, reals)
    flops = 4 * 2 * 1024 * 128 * 128
    results = call(body, operands, outs, scratch, hbm=range(8), flops=flops)
    return results[:4], results[4], results[5], results[6:]


def gen_back_body(step, judges, *refs):
    is_last = step == STEPS - 1
    refs = list(refs)
    units = [refs.pop(0) for _ in range(judges)]
    own_slope, other_slopes = [refs.pop(0) for _ in range(2)]
    hidden_ref, middle_ref, gen_slope_ref, mid_slope_ref, latent_ref = [refs.pop(0) for _ in range(5)]
    in_ref, base_ref, one_ref, two_ref = [refs.pop(0) for _ in range(4)]
    new_in, new_base, new_one, new_two = [refs.pop(0) for _ in range(4)]
    places, channels = base_ref.shape
    sides = (slice(0, channels), slice(channels, 2 * channels))
    spans = (slice(0, places), slice(places, 2 * places))

    halves = []
    for member, span in enumerate(spans):
        total = own_slope[member : member + 1, :] * units[0][span, :].astype(F32)
        for which in range(1, judges):
            place = 2 * (which - 1) + member
            total = total + other_slopes[place : place + 1, :] * units[which][span, :].astype(F32)
        halves.append(total)
    cotangent = jnp.concatenate(halves, axis=1)
    cotangent_half = cotangent.astype(BF16)
    one = one_ref[...].astype(BF16)
    two = two_ref[...].astype(BF16) * BF16(0.5)
    inner_half = (dot_turned(cotangent_half, both(two, two)) * mid_slope_ref[...]).astype(BF16)
    outer = (cotangent + dot_turned(inner_half, both(one, one))) * gen_slope_ref[...]
    grad_two = [dot_rows(middle_ref[:, side], cotangent_half[:, side]) for side in sides]
    grad_one = [dot_rows(hidden_ref[:, side], inner_half[:, side]) for side in sides]
    sums = jnp.sum(jnp.sum(outer.reshape(-1, 8, 2 * channels), axis=0), axis=0, keepdims=True)
    latent_turned = latent_ref[step].T
    grad_in = [
        latent_turned[:, member : member + 1] * (0.5 * sums[:, side])
        for member, side in enumerate(sides)
    ]
    base = base_ref[...] - (0.5 * BASE_RATE * places) * (outer[:, sides[0]] + outer[:, sides[1]])
    w_one = one_ref[...] - LEARN_RATE * (grad_one[0] + grad_one[1])
    w_two = two_ref[...] - LEARN_RATE * (grad_two[0] + grad_two[1])
    w_in = in_ref[...] - LEARN_RATE * (grad_in[0] + grad_in[1])
    new_in[...] = w_in
    new_base[...] = base
    new_one[...] = w_one
    new_two[...] = w_two
    if not is_last:
        gen_forward(latent_ref[step + 1], w_in, base, w_one, w_two, refs)


def gen_back(step, units, own_slope, other_slopes, stored, latents, weights):
    places, channels = weights[1].shape
    operands = list(units) + [own_slope, other_slopes] + list(stored[1:]) + [latents] + list(weights)
    outs = [shape(member.shape, F32) for member in weights]
    if step < STEPS - 1:
        outs = outs + stored_shapes(places, channels)
    body = functools.partial(gen_back_body, step, len(units))
    flops = 12 * 2 * 1024 * 128 * 128
    results = call(body, operands, outs, flops=flops)
    return results[:4], results[4:]


def disc_update_body(batch, reals, is_last, grads_ref, *refs):
    refs = list(refs)
    returns = [refs.pop(0) for _ in range(4)]
    refs.pop(0)
    params = [refs.pop(0) for _ in range(3)]
    before = refs.pop(0) if is_last else None
    news = [refs.pop(0) for _ in range(3)]
    last_ref = refs.pop(0)
    channels = params[0].shape[0]
    one = grads_ref[0:channels, :]
    two = grads_ref[channels:HEAD, :]
    out = grads_ref[HEAD + 8 : HEAD + 9, :]
    verdicts = [grads_ref[HEAD + i : HEAD + 1 + i, :] for i in range(batch + reals)]
    tails = []
    for back in returns:
        one = one + back[0:channels, :].astype(F32)
        two = two + back[channels:HEAD, :].astype(F32)
        tail = back[HEAD:PACKET, :].astype(F32)
        out = out + packet_row(tail, 0)
        tails.append([packet_row(tail, 1 + i) for i in range(batch)])
    ordered = verdicts[:batch]
    for axis, (inner, outer) in (("row", tails[0:2]), ("col", tails[2:4])):
        is_odd = lax.rem(lax.axis_index(axis), 2) == 1
        ordered = ordered + [jnp.where(is_odd, a, b) for a, b in zip(inner, outer)]
        ordered = ordered + [jnp.where(is_odd, b, a) for a, b in zip(inner, outer)]
    ordered = ordered + verdicts[batch:]
    updated = [member[...] - LEARN_RATE * grad for member, grad in zip(params, (one, two, out))]
    for new, value in zip(news, updated):
        new[...] = value
    lanes = lax.broadcasted_iota(jnp.int32, (1, channels), 1)
    line = jnp.zeros((1, channels), F32)
    for place, value in enumerate(ordered):
        line = jnp.where(lanes == place, value, line)
    count = len(ordered)
    if is_last:
        last_ref[0:1, :] = before[0:1, 0:count]
        last_ref[1:2, :] = line[:, 0:count]
    else:
        last_ref[...] = line
        write_packet(refs[0], updated[0], updated[1], [updated[2]])


def disc_update(grads, returns, after, params, before, batch, reals):
    is_last = before is not None
    operands = [grads] + list(returns) + [after] + list(params) + ([before] if is_last else [])
    outs = [shape(member.shape, F32) for member in params]
    if is_last:
        outs = outs + [shape((STEPS, 5 * batch + reals), F32)]
    else:
        outs = outs + [shape((1, 128), F32), shape((PACKET, 128), BF16)]
    body = functools.partial(disc_update_body, batch, reals, is_last)
    return call(body, operands, outs, hbm=(5,) if is_last else ())


def paired(block, axis, offset):
    count = lax.axis_size(axis)
    route = []
    for i in range(0, count, 2):
        first, second = (i + offset) % count, (i + offset + 1) % count
        route += [(first, second), (second, first)]
    return lax.ppermute(block, axis, route)


EDGES = (("row", 0), ("row", 1), ("col", 0), ("col", 1))


def on_device(
    data, real_index, latent_seed, latent_bank, g_in, g_base, g_one, g_two, d_one, d_two, d_out
):
    batch = latent_seed.shape[3]
    reals = real_index.shape[3]
    packet, discs = pack([d_one[0, 0], d_two[0, 0], d_out[0]])
    verdict = None
    for step in range(STEPS):
        is_last = step == STEPS - 1
        arrived = [paired(packet, axis, offset) for axis, offset in EDGES]
        if step == 0:
            gens, latents, reals_rows, stored = begin(
                latent_seed[0, 0],
                real_index[0, 0],
                latent_bank,
                data[0, 0],
                [member[0, 0] for member in (g_in, g_base, g_one, g_two)],
            )
        fakes = stored[0]
        own_grads, own_unit, own_slope = judge_own(packet, fakes, reals_rows, step, batch, reals)
        grads, units, other_slopes = judge_others(arrived, fakes, batch, own_slope)
        returns = [paired(member, axis, offset) for member, (axis, offset) in zip(grads, EDGES)]
        gens, stored = gen_back(
            step, [own_unit] + list(units), own_slope, other_slopes, stored, latents, gens
        )
        results = disc_update(
            own_grads, returns, gens[0], discs, verdict if is_last else None, batch, reals
        )
        discs = results[:3]
        verdict = results[3]
        packet = None if is_last else results[4]
    finals = [member[None, None] for member in gens] + [
        discs[0][None, None],
        discs[1][None, None],
        discs[2][None],
        verdict[None, None],
    ]
    return tuple(finals)


def solution(mesh):
    matrix = P("row", "col", None, None)
    return jax.shard_map(
        on_device,
        mesh=mesh,
        in_specs=(
            P("row", "col", None, None, None),
            matrix,
            matrix,
            P(),
            matrix,
            matrix,
            matrix,
            matrix,
            matrix,
            matrix,
            P("row", "col", None),
        ),
        out_specs=(
            matrix,
            matrix,
            matrix,
            matrix,
            matrix,
            matrix,
            P("row", "col", None),
            matrix,
        ),
        check_vma=False,
    )
```

time: 101 us -> 56.7 us (0.56)
  Pallas kernels: 56.4 us -> 22 us
  local copies, waits for them, and re-layouts: 11.7 us -> 0 us
  waiting for transfers between devices: 0.04 us -> 11.3 us
  starting transfers between devices: 31.8 us -> 22.5 us
    pallas_call x16 -> x10, Pallas kernels: 56.4 us -> 22 us  [call(): pl.pallas_call(body, out_shape=tuple(out_shape), in_specs=[pl.BlockSpec(m...]
    ppermute x16, waiting for transfers between devices: 0.04 us -> 11.3 us  [paired(): return lax.ppermute(block, axis, route)]
    unnamed x42 -> x0, local copies, waits for them, and re-layouts: 10.9 us -> none
    ppermute x16, starting transfers between devices: 31.8 us -> 22.5 us  [paired(): return lax.ppermute(block, axis, route)]
  transfers between devices with their start and end apart: 16 -> 16, of which waited for: 0 -> 6; matrix products, arithmetic and copies ran while one was open for 1% -> 0% of each run, Pallas kernels for 55% -> 20%
where the time goes in v1:
time: 56.7 us; the launch traced here: 56.5 us
  starting transfers between devices  22.5 us (40%)
  Pallas kernels  22 us (39%)
  waiting for transfers between devices  11.3 us (20%)
  between operations  0.75 us (1%)
    ppermute x16, starting transfers between devices, paired(): return lax.ppermute(block, axis, route)  22.5 us
    pallas_call x10, Pallas kernels, call(): pl.pallas_call(body, out_shape=tuple(out_shape), in_specs=[pl.BlockSpec(m...  22 us
    ppermute x16, waiting for transfers between devices, paired(): return lax.ppermute(block, axis, route)  11.3 us
  transfers between devices with their start and end apart: 16, of which 6 were waited for; matrix products, arithmetic and copies ran while one was open for 0% of the time, Pallas kernels for 20%

profile of v1, /device:TPU:0, one launch (start us, length us, event | category | flops | bytes accessed | tf_op | source)
XLA Modules:
  0.0 56.5 jit_solution(14224915272237402117)
XLA Ops:
  0.6 0.9 %shard_map.170 = (bf16[272,128]{1,0:T(8,128)(2,1)S(1)}, f32[128,128]{1,0:T(8,128)S(1)}, f32[128,128]{1,0:T(8,128)S(1)}, f32[1,128]{1,0:T(1,128)S(1)}) custom-call(f32[128,128]{1,0:T(8,128)} %bitcast.24, f32[128,128]{1,0:T(8,128)} %bitcast.25, f32[1,128]{1,0:T(1,128)} %bitcast.28), custom_call_target="tpu_custom_call" | custom-call | tf_op jit(solution)/shard_map/pallas_call | solution.py:63
  1.6 2.1 %collective-permute-start = (bf16[272,128]{1,0:T(8,128)(2,1)S(1)}, bf16[272,128]{1,0:T(8,128)(2,1)S(1)}, u32[]{:S(2)}, u32[]{:S(2)}) collective-permute-start(bf16[272,128]{1,0:T(8,128)(2,1)S(1)} %get-tuple-element.69.packet_ref), channel_id=1, source_target_pairs={{0,16},{16,0},{32,48},{48,32},{64,80},{80,64},{96,112},{112,96},{1... | collective-permute-start | bytes 208904 | tf_op jit(solution)/shard_map/ppermute | solution.py:472
  3.6 2.6 %collective-permute-start.1 = (bf16[272,128]{1,0:T(8,128)(2,1)S(1)}, bf16[272,128]{1,0:T(8,128)(2,1)S(1)}, u32[]{:S(2)}, u32[]{:S(2)}) collective-permute-start(bf16[272,128]{1,0:T(8,128)(2,1)S(1)} %get-tuple-element.69.packet_ref), channel_id=1, source_target_pairs={{16,32},{32,16},{48,64},{64,48},{80,96},{96,80},{112,0},{0,112},{1... | collective-permute-start | bytes 208904 | tf_op jit(solution)/shard_map/ppermute | solution.py:472
  6.2 6.2 %collective-permute-start.3 = (bf16[272,128]{1,0:T(8,128)(2,1)S(1)}, bf16[272,128]{1,0:T(8,128)(2,1)S(1)}, u32[]{:S(2)}, u32[]{:S(2)}) collective-permute-start(bf16[272,128]{1,0:T(8,128)(2,1)S(1)} %get-tuple-element.69.packet_ref), channel_id=1, source_target_pairs={{1,2},{2,1},{3,4},{4,3},{5,6},{6,5},{7,8},{8,7},{9,10},{10,9},{11,... | collective-permute-start | bytes 208904 | tf_op jit(solution)/shard_map/ppermute | solution.py:472
  12.4 2.6 %shard_map.171 = (f32[128,128]{1,0:T(8,128)S(1)}, f32[1024,128]{1,0:T(8,128)S(1)}, f32[128,128]{1,0:T(8,128)S(1)}, f32[128,128]{1,0:T(8,128)S(1)}, f32[2,8,128]{...) custom-call(s32[2,2]{1,0:T(2,128)} %bitcast.26, ...), custom_call_target="tpu_custom_call" | custom-call | flops 134217728 | bytes 134217 | tf_op jit(solution)/shard_map/pallas_call | solution.py:63
  15.0 2.5 %shard_map.172 = (f32[272,128]{1,0:T(8,128)S(1)}, bf16[2048,128]{1,0:T(8,128)(2,1)S(1)}, f32[8,128]{1,0:T(8,128)S(1)}) custom-call(bf16[272,128]{1,0:T(8,128)(2,1)S(1)} %get-tuple-element.69.packet_ref, bf16[2048,128]{1,0:T(8,128)(2,1)S(1)} %get-tuple-element.70.fakes_ref.refs_4_, bf16[4,1024,128]{2,1,0:T(8,128)(2,1)S(1)} %get-tuple-element.71.reals_ref), custom_call_target="tpu_custom_call" | custom-call | flops 805306368 | bytes 805306 | tf_op jit(solution)/shard_map/pallas_call | solution.py:63
  17.6 4.5 %shard_map.173 = (bf16[272,128]{1,0:T(8,128)(2,1)S(1)}, bf16[272,128]{1,0:T(8,128)(2,1)S(1)}, bf16[272,128]{1,0:T(8,128)(2,1)S(1)}, bf16[272,128]{1,0:T(8,128)(2...) custom-call(bf16[272,128]{1,0:T(8,128)(2,1)S(1)} %collective-permute, ...), custom_call_target="tpu_custom_call" | custom-call | flops 1610612736 | bytes 1610612 | tf_op jit(solution)/shard_map/pallas_call | solution.py:63
  22.1 2.2 %collective-permute-start.5 = (bf16[272,128]{1,0:T(8,128)(2,1)S(1)}, bf16[272,128]{1,0:T(8,128)(2,1)S(1)}, u32[]{:S(2)}, u32[]{:S(2)}) collective-permute-start(bf16[272,128]{1,0:T(8,128)(2,1)S(1)} %get-tuple-element.75), channel_id=1, source_target_pairs={{16,32},{32,16},{48,64},{64,48},{80,96},{96,80},{112,0},{0,112},{1... | collective-permute-start | bytes 208904 | tf_op jit(solution)/shard_map/ppermute | solution.py:472
  24.3 1.6 %collective-permute-start.7 = (bf16[272,128]{1,0:T(8,128)(2,1)S(1)}, bf16[272,128]{1,0:T(8,128)(2,1)S(1)}, u32[]{:S(2)}, u32[]{:S(2)}) collective-permute-start(bf16[272,128]{1,0:T(8,128)(2,1)S(1)} %get-tuple-element.77), channel_id=1, source_target_pairs={{1,2},{2,1},{3,4},{4,3},{5,6},{6,5},{7,8},{8,7},{9,10},{10,9},{11,... | collective-permute-start | bytes 208904 | tf_op jit(solution)/shard_map/ppermute | solution.py:472
  25.9 1.8 %shard_map.174 = (f32[128,128]{1,0:T(8,128)S(1)}, f32[1024,128]{1,0:T(8,128)S(1)}, f32[128,128]{1,0:T(8,128)S(1)}, f32[128,128]{1,0:T(8,128)S(1)}, bf16[2048,128...) custom-call(bf16[2048,128]{1,0:T(8,128)(2,1)S(1)} %get-tuple-element, ...), custom_call_target="tpu_custom_call" | custom-call | flops 402653184 | bytes 402653 | tf_op jit(solution)/shard_map/pallas_call | solution.py:63
  27.7 1.1 %collective-permute-done.5.refs_1_ = bf16[272,128]{1,0:T(8,128)(2,1)S(1)} collective-permute-done((bf16[272,128]{1,0:T(8,128)(2,1)S(1)}, bf16[272,128]{1,0:T(8,128)(2,1)S(1)}, u32[]{:S(2)}, u32[]{:S(2)}) %collective-permute-start.5) | collective-permute-done | bytes 69664 | tf_op jit(solution)/shard_map/ppermute | solution.py:472
  28.9 2.9 %collective-permute-done.7.refs_3_ = bf16[272,128]{1,0:T(8,128)(2,1)S(1)} collective-permute-done((bf16[272,128]{1,0:T(8,128)(2,1)S(1)}, bf16[272,128]{1,0:T(8,128)(2,1)S(1)}, u32[]{:S(2)}, u32[]{:S(2)}) %collective-permute-start.7) | collective-permute-done | bytes 69664 | tf_op jit(solution)/shard_map/ppermute | solution.py:472
  32.3 1.6 %collective-permute-start.9 = (bf16[272,128]{1,0:T(8,128)(2,1)S(1)}, bf16[272,128]{1,0:T(8,128)(2,1)S(1)}, u32[]{:S(2)}, u32[]{:S(2)}) collective-permute-start(bf16[272,128]{1,0:T(8,128)(2,1)S(1)} %get-tuple-element.97.packet_ref), channel_id=1, source_target_pairs={{16,32},{32,16},{48,64},{64,48},{80,96},{96,80},{112,0},{0,112},{1... | collective-permute-start | bytes 208904 | tf_op jit(solution)/shard_map/ppermute | solution.py:472
  33.9 1.7 %collective-permute-start.11 = (bf16[272,128]{1,0:T(8,128)(2,1)S(1)}, bf16[272,128]{1,0:T(8,128)(2,1)S(1)}, u32[]{:S(2)}, u32[]{:S(2)}) collective-permute-start(bf16[272,128]{1,0:T(8,128)(2,1)S(1)} %get-tuple-element.97.packet_ref), channel_id=1, source_target_pairs={{1,2},{2,1},{3,4},{4,3},{5,6},{6,5},{7,8},{8,7},{9,10},{10,9},{11,... | collective-permute-start | bytes 208904 | tf_op jit(solution)/shard_map/ppermute | solution.py:472
  35.6 2.5 %shard_map.176 = (f32[272,128]{1,0:T(8,128)S(1)}, bf16[2048,128]{1,0:T(8,128)(2,1)S(1)}, f32[8,128]{1,0:T(8,128)S(1)}) custom-call(bf16[272,128]{1,0:T(8,128)(2,1)S(1)} %get-tuple-element.97.packet_ref, bf16[2048,128]{1,0:T(8,128)(2,1)S(1)} %get-tuple-element.98.fakes_ref.refs_4_, bf16[4,1024,128]{2,1,0:T(8,128)(2,1)S(1)} %get-tuple-element.71.reals_ref), custom_call_target="tpu_custom_call" | custom-call | flops 805306368 | bytes 805306 | tf_op jit(solution)/shard_map/pallas_call | solution.py:63
  38.2 0.8 %collective-permute-done.9.refs_1_ = bf16[272,128]{1,0:T(8,128)(2,1)S(1)} collective-permute-done((bf16[272,128]{1,0:T(8,128)(2,1)S(1)}, bf16[272,128]{1,0:T(8,128)(2,1)S(1)}, u32[]{:S(2)}, u32[]{:S(2)}) %collective-permute-start.9) | collective-permute-done | bytes 69664 | tf_op jit(solution)/shard_map/ppermute | solution.py:472
  38.9 2.4 %collective-permute-done.11.refs_3_ = bf16[272,128]{1,0:T(8,128)(2,1)S(1)} collective-permute-done((bf16[272,128]{1,0:T(8,128)(2,1)S(1)}, bf16[272,128]{1,0:T(8,128)(2,1)S(1)}, u32[]{:S(2)}, u32[]{:S(2)}) %collective-permute-start.11) | collective-permute-done | bytes 69664 | tf_op jit(solution)/shard_map/ppermute | solution.py:472
  41.3 4.5 %shard_map.177 = (bf16[272,128]{1,0:T(8,128)(2,1)S(1)}, bf16[272,128]{1,0:T(8,128)(2,1)S(1)}, bf16[272,128]{1,0:T(8,128)(2,1)S(1)}, bf16[272,128]{1,0:T(8,128)(2...) custom-call(bf16[272,128]{1,0:T(8,128)(2,1)S(1)} %collective-permute, ...), custom_call_target="tpu_custom_call" | custom-call | flops 1610612736 | bytes 1610612 | tf_op jit(solution)/shard_map/pallas_call | solution.py:63
  45.8 1.1 %collective-permute-start.12 = (bf16[272,128]{1,0:T(8,128)(2,1)S(1)}, bf16[272,128]{1,0:T(8,128)(2,1)S(1)}, u32[]{:S(2)}, u32[]{:S(2)}) collective-permute-start(bf16[272,128]{1,0:T(8,128)(2,1)S(1)} %get-tuple-element.118), channel_id=1, source_target_pairs={{0,16},{16,0},{32,48},{48,32},{64,80},{80,64},{96,112},{112,96},{1... | collective-permute-start | bytes 208904 | tf_op jit(solution)/shard_map/ppermute | solution.py:472
  46.9 1.6 %collective-permute-start.13 = (bf16[272,128]{1,0:T(8,128)(2,1)S(1)}, bf16[272,128]{1,0:T(8,128)(2,1)S(1)}, u32[]{:S(2)}, u32[]{:S(2)}) collective-permute-start(bf16[272,128]{1,0:T(8,128)(2,1)S(1)} %get-tuple-element.119), channel_id=1, source_target_pairs={{16,32},{32,16},{48,64},{64,48},{80,96},{96,80},{112,0},{0,112},{1... | collective-permute-start | bytes 208904 | tf_op jit(solution)/shard_map/ppermute | solution.py:472
  48.5 1.3 %collective-permute-start.15 = (bf16[272,128]{1,0:T(8,128)(2,1)S(1)}, bf16[272,128]{1,0:T(8,128)(2,1)S(1)}, u32[]{:S(2)}, u32[]{:S(2)}) collective-permute-start(bf16[272,128]{1,0:T(8,128)(2,1)S(1)} %get-tuple-element.121), channel_id=1, source_target_pairs={{1,2},{2,1},{3,4},{4,3},{5,6},{6,5},{7,8},{8,7},{9,10},{10,9},{11,... | collective-permute-start | bytes 208904 | tf_op jit(solution)/shard_map/ppermute | solution.py:472
  49.8 1.9 %shard_map.178 = (f32[128,128]{1,0:T(8,128)}, f32[1024,128]{1,0:T(8,128)}, f32[128,128]{1,0:T(8,128)}, f32[128,128]{1,0:T(8,128)}) custom-call(bf16[2048,128]{1,0:T(8,128)(2,1)S(1)} %get-tuple-element.99.refs_0_, bf16[2048,128]{1,0:T(8,128)(2,1)S(1)} %get-tuple-element.101.refs_1_, bf16[2048,128]{1,0:T(8,128)(2,1)S(1)} %get-tuple-element.102.refs_2_, ...), custom_call_target="tpu_custom_call" | custom-call | flops 402653184 | bytes 402653 | tf_op jit(solution)/shard_map/pallas_call | solution.py:63
  51.7 2.0 %collective-permute-done.13.refs_1_ = bf16[272,128]{1,0:T(8,128)(2,1)S(1)} collective-permute-done((bf16[272,128]{1,0:T(8,128)(2,1)S(1)}, bf16[272,128]{1,0:T(8,128)(2,1)S(1)}, u32[]{:S(2)}, u32[]{:S(2)}) %collective-permute-start.13) | collective-permute-done | bytes 69664 | tf_op jit(solution)/shard_map/ppermute | solution.py:472
  53.7 2.1 %collective-permute-done.15.refs_3_ = bf16[272,128]{1,0:T(8,128)(2,1)S(1)} collective-permute-done((bf16[272,128]{1,0:T(8,128)(2,1)S(1)}, bf16[272,128]{1,0:T(8,128)(2,1)S(1)}, u32[]{:S(2)}, u32[]{:S(2)}) %collective-permute-start.15) | collective-permute-done | bytes 69664 | tf_op jit(solution)/shard_map/ppermute | solution.py:472
  (18 shorter events, 1.4 us)
Async XLA Ops:
  1.6 16.0 %collective-permute-start = (bf16[272,128]{1,0:T(8,128)(2,1)S(1)}, bf16[272,128]{1,0:T(8,128)(2,1)S(1)}, u32[]{:S(2)}, u32[]{:S(2)}) collective-permute-start(bf16[272,128]{1,0:T(8,128)(2,1)S(1)} %get-tuple-element.69.packet_ref), channel_id=1, source_target_pairs={{0,16},{16,0},{32,48},{48,32},{64,80},{80,64},{96,112},{112,96},{1... | collective-permute-start | bytes 208904 | tf_op jit(solution)/shard_map/ppermute | solution.py:472
  3.6 13.9 %collective-permute-start.1 = (bf16[272,128]{1,0:T(8,128)(2,1)S(1)}, bf16[272,128]{1,0:T(8,128)(2,1)S(1)}, u32[]{:S(2)}, u32[]{:S(2)}) collective-permute-start(bf16[272,128]{1,0:T(8,128)(2,1)S(1)} %get-tuple-element.69.packet_ref), channel_id=1, source_target_pairs={{16,32},{32,16},{48,64},{64,48},{80,96},{96,80},{112,0},{0,112},{1... | collective-permute-start | bytes 208904 | tf_op jit(solution)/shard_map/ppermute | solution.py:472
  6.2 11.3 %collective-permute-start.2 = (bf16[272,128]{1,0:T(8,128)(2,1)S(1)}, bf16[272,128]{1,0:T(8,128)(2,1)S(1)}, u32[]{:S(2)}, u32[]{:S(2)}) collective-permute-start(bf16[272,128]{1,0:T(8,128)(2,1)S(1)} %get-tuple-element.69.packet_ref), channel_id=1, source_target_pairs={{0,1},{1,0},{2,3},{3,2},{4,5},{5,4},{6,7},{7,6},{8,9},{9,8},{10,11... | collective-permute-start | bytes 208904 | tf_op jit(solution)/shard_map/ppermute | solution.py:472
  6.2 11.4 %collective-permute-start.3 = (bf16[272,128]{1,0:T(8,128)(2,1)S(1)}, bf16[272,128]{1,0:T(8,128)(2,1)S(1)}, u32[]{:S(2)}, u32[]{:S(2)}) collective-permute-start(bf16[272,128]{1,0:T(8,128)(2,1)S(1)} %get-tuple-element.69.packet_ref), channel_id=1, source_target_pairs={{1,2},{2,1},{3,4},{4,3},{5,6},{6,5},{7,8},{8,7},{9,10},{10,9},{11,... | collective-permute-start | bytes 208904 | tf_op jit(solution)/shard_map/ppermute | solution.py:472
  22.0 5.7 %collective-permute-start.4 = (bf16[272,128]{1,0:T(8,128)(2,1)S(1)}, bf16[272,128]{1,0:T(8,128)(2,1)S(1)}, u32[]{:S(2)}, u32[]{:S(2)}) collective-permute-start(bf16[272,128]{1,0:T(8,128)(2,1)S(1)} %get-tuple-element.74), channel_id=1, source_target_pairs={{0,16},{16,0},{32,48},{48,32},{64,80},{80,64},{96,112},{112,96},{1... | collective-permute-start | bytes 208904 | tf_op jit(solution)/shard_map/ppermute | solution.py:472
  22.1 6.8 %collective-permute-start.5 = (bf16[272,128]{1,0:T(8,128)(2,1)S(1)}, bf16[272,128]{1,0:T(8,128)(2,1)S(1)}, u32[]{:S(2)}, u32[]{:S(2)}) collective-permute-start(bf16[272,128]{1,0:T(8,128)(2,1)S(1)} %get-tuple-element.75), channel_id=1, source_target_pairs={{16,32},{32,16},{48,64},{64,48},{80,96},{96,80},{112,0},{0,112},{1... | collective-permute-start | bytes 208904 | tf_op jit(solution)/shard_map/ppermute | solution.py:472
  24.3 4.6 %collective-permute-start.6 = (bf16[272,128]{1,0:T(8,128)(2,1)S(1)}, bf16[272,128]{1,0:T(8,128)(2,1)S(1)}, u32[]{:S(2)}, u32[]{:S(2)}) collective-permute-start(bf16[272,128]{1,0:T(8,128)(2,1)S(1)} %get-tuple-element.76), channel_id=1, source_target_pairs={{0,1},{1,0},{2,3},{3,2},{4,5},{5,4},{6,7},{7,6},{8,9},{9,8},{10,11... | collective-permute-start | bytes 208904 | tf_op jit(solution)/shard_map/ppermute | solution.py:472
  24.3 7.5 %collective-permute-start.7 = (bf16[272,128]{1,0:T(8,128)(2,1)S(1)}, bf16[272,128]{1,0:T(8,128)(2,1)S(1)}, u32[]{:S(2)}, u32[]{:S(2)}) collective-permute-start(bf16[272,128]{1,0:T(8,128)(2,1)S(1)} %get-tuple-element.77), channel_id=1, source_target_pairs={{1,2},{2,1},{3,4},{4,3},{5,6},{6,5},{7,8},{8,7},{9,10},{10,9},{11,... | collective-permute-start | bytes 208904 | tf_op jit(solution)/shard_map/ppermute | solution.py:472
  31.9 6.3 %collective-permute-start.8 = (bf16[272,128]{1,0:T(8,128)(2,1)S(1)}, bf16[272,128]{1,0:T(8,128)(2,1)S(1)}, u32[]{:S(2)}, u32[]{:S(2)}) collective-permute-start(bf16[272,128]{1,0:T(8,128)(2,1)S(1)} %get-tuple-element.97.packet_ref), channel_id=1, source_target_pairs={{0,16},{16,0},{32,48},{48,32},{64,80},{80,64},{96,112},{112,96},{1... | collective-permute-start | bytes 208904 | tf_op jit(solution)/shard_map/ppermute | solution.py:472
  32.3 6.6 %collective-permute-start.9 = (bf16[272,128]{1,0:T(8,128)(2,1)S(1)}, bf16[272,128]{1,0:T(8,128)(2,1)S(1)}, u32[]{:S(2)}, u32[]{:S(2)}) collective-permute-start(bf16[272,128]{1,0:T(8,128)(2,1)S(1)} %get-tuple-element.97.packet_ref), channel_id=1, source_target_pairs={{16,32},{32,16},{48,64},{64,48},{80,96},{96,80},{112,0},{0,112},{1... | collective-permute-start | bytes 208904 | tf_op jit(solution)/shard_map/ppermute | solution.py:472
  33.9 5.0 %collective-permute-start.10 = (bf16[272,128]{1,0:T(8,128)(2,1)S(1)}, bf16[272,128]{1,0:T(8,128)(2,1)S(1)}, u32[]{:S(2)}, u32[]{:S(2)}) collective-permute-start(bf16[272,128]{1,0:T(8,128)(2,1)S(1)} %get-tuple-element.97.packet_ref), channel_id=1, source_target_pairs={{0,1},{1,0},{2,3},{3,2},{4,5},{5,4},{6,7},{7,6},{8,9},{9,8},{10,11... | collective-permute-start | bytes 208904 | tf_op jit(solution)/shard_map/ppermute | solution.py:472
  33.9 7.3 %collective-permute-start.11 = (bf16[272,128]{1,0:T(8,128)(2,1)S(1)}, bf16[272,128]{1,0:T(8,128)(2,1)S(1)}, u32[]{:S(2)}, u32[]{:S(2)}) collective-permute-start(bf16[272,128]{1,0:T(8,128)(2,1)S(1)} %get-tuple-element.97.packet_ref), channel_id=1, source_target_pairs={{1,2},{2,1},{3,4},{4,3},{5,6},{6,5},{7,8},{8,7},{9,10},{10,9},{11,... | collective-permute-start | bytes 208904 | tf_op jit(solution)/shard_map/ppermute | solution.py:472
  45.8 5.9 %collective-permute-start.12 = (bf16[272,128]{1,0:T(8,128)(2,1)S(1)}, bf16[272,128]{1,0:T(8,128)(2,1)S(1)}, u32[]{:S(2)}, u32[]{:S(2)}) collective-permute-start(bf16[272,128]{1,0:T(8,128)(2,1)S(1)} %get-tuple-element.118), channel_id=1, source_target_pairs={{0,16},{16,0},{32,48},{48,32},{64,80},{80,64},{96,112},{112,96},{1... | collective-permute-start | bytes 208904 | tf_op jit(solution)/shard_map/ppermute | solution.py:472
  46.9 6.8 %collective-permute-start.13 = (bf16[272,128]{1,0:T(8,128)(2,1)S(1)}, bf16[272,128]{1,0:T(8,128)(2,1)S(1)}, u32[]{:S(2)}, u32[]{:S(2)}) collective-permute-start(bf16[272,128]{1,0:T(8,128)(2,1)S(1)} %get-tuple-element.119), channel_id=1, source_target_pairs={{16,32},{32,16},{48,64},{64,48},{80,96},{96,80},{112,0},{0,112},{1... | collective-permute-start | bytes 208904 | tf_op jit(solution)/shard_map/ppermute | solution.py:472
  48.5 5.2 %collective-permute-start.14 = (bf16[272,128]{1,0:T(8,128)(2,1)S(1)}, bf16[272,128]{1,0:T(8,128)(2,1)S(1)}, u32[]{:S(2)}, u32[]{:S(2)}) collective-permute-start(bf16[272,128]{1,0:T(8,128)(2,1)S(1)} %get-tuple-element.120), channel_id=1, source_target_pairs={{0,1},{1,0},{2,3},{3,2},{4,5},{5,4},{6,7},{7,6},{8,9},{9,8},{10,11... | collective-permute-start | bytes 208904 | tf_op jit(solution)/shard_map/ppermute | solution.py:472
  48.5 7.3 %collective-permute-start.15 = (bf16[272,128]{1,0:T(8,128)(2,1)S(1)}, bf16[272,128]{1,0:T(8,128)(2,1)S(1)}, u32[]{:S(2)}, u32[]{:S(2)}) collective-permute-start(bf16[272,128]{1,0:T(8,128)(2,1)S(1)} %get-tuple-element.121), channel_id=1, source_target_pairs={{1,2},{2,1},{3,4},{4,3},{5,6},{6,5},{7,8},{8,7},{9,10},{10,9},{11,... | collective-permute-start | bytes 208904 | tf_op jit(solution)/shard_map/ppermute | solution.py:472

commit v2 on v1

--- a/solution.py
+++ b/solution.py
@@ -26,20 +26,21 @@
 
 
 def silu_parts(half):
-    tanh_part = jnp.tanh(half)
-    above = 1.0 + tanh_part
+    above = 1.0 + jnp.tanh(half)
     value = half * above
-    slope_twice = above + value * (1.0 - tanh_part)
-    return value, slope_twice
+    value_half = value.astype(BF16)
+    above_half = above.astype(BF16)
+    return value, value_half, above_half + value_half * (BF16(2.0) - above_half)
+
+
+def silu_exact(half):
+    above = 1.0 + jnp.tanh(half)
+    value = half * above
+    return value, above + value * (2.0 - above)
 
 
 def sigmoid(value):
     return 0.5 * (1.0 + jnp.tanh(0.5 * value))
-
-
-def col_sums(tile):
-    rows, channels = tile.shape
-    return jnp.sum(tile.reshape(rows // 8, 8, channels), axis=0)
 
 
 def split_two(value):
@@ -128,77 +129,101 @@
     )
 
 
-def judge_pair(images, one, two, out_row, shared):
-    channels = images.shape[1] if shared else images.shape[1] // 2
+OFFSET = 2
+
+
+def judge_steps(pair, result):
+    images, one, two, out_row, shared = pair
     half = BF16(0.5)
-    left = slice(0, channels)
-    right = slice(channels, 2 * channels)
-    one_both = both(*one)
-    one_first = jnp.concatenate(one, axis=1) if shared else one_both
-    first, slope_first = silu_parts(dot(images, one_first * half))
-    first_half = first.astype(BF16)
-    two_half = both(*two) * half
+    one_first = jnp.concatenate(one, axis=1) if shared else both(*one)
+    halves = dot(images, one_first * half)
+    yield
+    _, first_half, slope_first = silu_parts(halves)
     image_half = 0.5 * images.astype(F32)
     if shared:
-        image_half = jnp.concatenate([image_half, image_half], axis=1)
-    feature, slope_out = silu_parts(image_half + dot(first_half, two_half))
+        image_half = twice(image_half)
+    product = dot(first_half, both(*two) * half)
+    yield
+    feature, slope_out = silu_exact(image_half + product)
+    sums = jnp.sum(feature.reshape(-1, 8, feature.shape[1]), axis=0)
+    sums = jnp.sum(sums, axis=0, keepdims=True)
     outer = (0.5 * out_row) * slope_out
     outer_half = outer.astype(BF16)
-    inner_half = (dot_turned(outer_half, two_half) * slope_first).astype(BF16)
-    unit = outer + dot_turned(inner_half, one_both)
+    product = dot_turned(outer_half, both(*two) * half)
+    yield
+    inner_half = product.astype(BF16) * slope_first
+    product = dot_turned(inner_half, both(*one))
+    channels = inner_half.shape[1] // 2
+    sides = [slice(0, channels), slice(channels, 2 * channels)]
+    grad_two = [dot_rows(first_half[:, s], outer_half[:, s]) for s in sides]
+    yield
+    result.append((outer + product).astype(BF16))
     if shared:
         wide = dot_rows(images, inner_half)
-        ones = [wide[:, left], wide[:, right]]
+        grad_one = [wide[:, s] for s in sides]
     else:
-        ones = [dot_rows(images[:, part], inner_half[:, part]) for part in (left, right)]
-    sums = jnp.sum(feature.reshape(-1, 8, 2 * channels), axis=0)
-    sums = jnp.sum(sums, axis=0, keepdims=True)
-    triples = [
-        (ones[i], dot_rows(first_half[:, part], outer_half[:, part]), sums[:, part])
-        for i, part in enumerate((left, right))
-    ]
-    return unit.astype(BF16), triples
-
-
-def finish(sums, out_row, signs, places, lines_ref):
-    count = len(sums)
-    channels = out_row.shape[1]
+        grad_one = [dot_rows(images[:, s], inner_half[:, s]) for s in sides]
+    for i, s in enumerate(sides):
+        result.append((grad_one[i], grad_two[i], sums[:, s]))
+
+
+def judge_pairs(pairs):
+    results = [[] for _ in pairs]
+    works = [judge_steps(pair, result) for pair, result in zip(pairs, results)]
+    beat = 0
+    left = set(range(len(works)))
+    while left:
+        for place in sorted(left):
+            if beat >= place * OFFSET and next(works[place], True):
+                left.discard(place)
+        beat += 1
+    return results
+
+
+def verdict_lines(triples, out_rows, signs, places, lines_ref):
     lines_ref[...] = jnp.zeros_like(lines_ref)
-    for member in range(count):
-        lines_ref[member : member + 1, :] = sums[member][2]
+    spot = lax.broadcasted_iota(jnp.int32, lines_ref.shape, 0)
+    outs = jnp.zeros(lines_ref.shape, F32)
+    is_fake = jnp.zeros(lines_ref.shape, jnp.bool_)
+    for member, (triple, out_row) in enumerate(zip(triples, out_rows)):
+        lines_ref[member : member + 1, :] = triple[2]
+        outs = jnp.where(spot == member, out_row, outs)
+        if signs[member]:
+            is_fake = is_fake | (spot == member)
     features = lines_ref[...]
     scale = 1.0 / places
-    verdicts = jnp.sum(features * out_row, axis=1, keepdims=True) * scale
+    verdicts = jnp.sum(features * outs, axis=1, keepdims=True) * scale
     verdicts = jnp.broadcast_to(verdicts, features.shape)
-    spot = lax.broadcasted_iota(jnp.int32, features.shape, 0)
     plus = sigmoid(verdicts) * scale
     minus = -sigmoid(-verdicts) * scale
-    slopes = jnp.where(spot < signs, plus, minus)
-    total_out = jnp.sum(features * slopes, axis=0, keepdims=True)
-    total_one = None
-    total_two = None
-    for member in range(count):
-        slope = slopes[member : member + 1, :]
-        part_one = slope * sums[member][0]
-        part_two = slope * sums[member][1]
-        total_one = part_one if total_one is None else total_one + part_one
-        total_two = part_two if total_two is None else total_two + part_two
-    return verdicts, minus, total_one, total_two, total_out
-
-
-def judge_own_body(step, batch, reals, packet_ref, fakes_ref, reals_ref, grads_ref, unit_ref, slope_ref, lines_ref):
+    return verdicts, minus, jnp.where(is_fake, plus, minus)
+
+
+def weigh(triples, slopes):
+    totals = None
+    for triple, slope in zip(triples, slopes):
+        parts = [slope * member for member in triple]
+        totals = parts if totals is None else [x + y for x, y in zip(totals, parts)]
+    return totals
+
+
+def judge_own_body(step, batch, reals, packet_ref, fakes_ref, reals_ref, _, grads_ref, unit_ref, slope_ref, lines_ref):
     rows, channels = fakes_ref.shape
     places = rows // batch
     one, two, out_row = unpack(packet_ref)
-    out_pair = jnp.concatenate([out_row, out_row], axis=1)
-    kept = [None] * (batch + reals)
+    out_pair = twice(out_row)
+    pairs = []
     for member in range(batch):
         span = slice(member * places, (member + 1) * places)
         images = jnp.concatenate([fakes_ref[span, :], reals_ref[step * reals + member]], axis=1)
-        unit, triples = judge_pair(images, (one, one), (two, two), out_pair, False)
-        unit_ref[span, :] = unit[:, 0:channels]
-        kept[member], kept[batch + member] = triples
-    verdicts, minus, total_one, total_two, total_out = finish(kept, out_row, batch, places, lines_ref)
+        pairs.append((images, (one, one), (two, two), out_pair, False))
+    results = judge_pairs(pairs)
+    for member, result in enumerate(results):
+        unit_ref[member * places : (member + 1) * places, :] = result[0][:, 0:channels]
+    triples = [result[1] for result in results] + [result[2] for result in results]
+    signs = [1] * batch + [0] * reals
+    verdicts, minus, slopes = verdict_lines(triples, [out_row] * len(signs), signs, places, lines_ref)
+    total_one, total_two, total_out = weigh(triples, [slopes[i : i + 1, :] for i in range(len(signs))])
     slope_ref[...] = minus
     grads_ref[0:channels, :] = total_one
     grads_ref[channels:HEAD, :] = total_two
@@ -206,7 +231,7 @@
     grads_ref[HEAD + 8 : PACKET, :] = jnp.broadcast_to(total_out, (8, channels))
 
 
-def judge_own(packet, fakes, reals_rows, step, batch, reals):
+def judge_own(packet, fakes, reals_rows, after, step, batch, reals):
     rows, channels = fakes.shape
     outs = [
         shape((PACKET, channels), F32),
@@ -215,7 +240,7 @@
     ]
     body = functools.partial(judge_own_body, step, batch, reals)
     flops = 4 * 6 * 2 * 1024 * 128 * 128
-    return call(body, [packet, fakes, reals_rows], outs, [pltpu.VMEM((8, channels), F32)], flops=flops)
+    return call(body, [packet, fakes, reals_rows, after], outs, [pltpu.VMEM((8, channels), F32)], flops=flops)
 
 
 def judge_others_body(judges, batch, *refs):
@@ -229,24 +254,35 @@
     lines_ref = refs.pop(0)
     rows, channels = fakes_ref.shape
     places = rows // batch
-    kept = [[None] * batch for _ in range(judges)]
     parts = [unpack(packet) for packet in packets]
-    for pair in range(0, judges, 2):
-        ones, twos, outs = zip(*parts[pair : pair + 2])
-        out_pair = jnp.concatenate(outs, axis=1)
-        for member in range(batch):
-            span = slice(member * places, (member + 1) * places)
-            unit, triples = judge_pair(fakes_ref[span, :], ones, twos, out_pair, True)
-            for side in range(2):
-                units[pair + side][span, :] = unit[:, side * channels : (side + 1) * channels]
-                kept[pair + side][member] = triples[side]
+    spans = [slice(member * places, (member + 1) * places) for member in range(batch)]
+    pairs = []
+    homes = []
+    for which in range(0, judges - 1, 2):
+        ones, twos, outs = zip(*parts[which : which + 2])
+        for member, span in enumerate(spans):
+            pairs.append((fakes_ref[span, :], ones, twos, jnp.concatenate(outs, axis=1), True))
+            homes.append(((which, member), (which + 1, member)))
+    if judges % 2:
+        one, two, out_row = parts[-1]
+        images = jnp.concatenate([fakes_ref[span, :] for span in spans], axis=1)
+        pairs.append((images, (one, one), (two, two), twice(out_row), False))
+        homes.append(tuple((judges - 1, member) for member in range(batch)))
+    found = {}
+    for result, home in zip(judge_pairs(pairs), homes):
+        for side, (which, member) in enumerate(home):
+            units[which][spans[member], :] = result[0][:, side * channels : (side + 1) * channels]
+            found[which, member] = result[1 + side]
+    keys = sorted(found)
+    triples = [found[key] for key in keys]
+    out_rows = [parts[which][2] for which, _ in keys]
+    verdicts, minus, slopes = verdict_lines(triples, out_rows, [1] * len(triples), places, lines_ref)
+    slope_ref[...] = minus
     for which in range(judges):
-        verdicts, minus, total_one, total_two, total_out = finish(
-            kept[which], parts[which][2], batch, places, lines_ref.at[which]
-        )
-        slope_ref[which * batch : (which + 1) * batch, :] = minus[0:batch, :]
-        tail = [total_out] + [verdicts[member : member + 1, :] for member in range(batch)]
-        write_packet(grads[which], total_one, total_two, tail)
+        mine = range(which * batch, (which + 1) * batch)
+        totals = weigh([triples[i] for i in mine], [slopes[i : i + 1, :] for i in mine])
+        tail = [totals[2]] + [verdicts[i : i + 1, :] for i in mine]
+        write_packet(grads[which], totals[0], totals[1], tail)
 
 
 def judge_others(packets, fakes, batch, after):
@@ -254,9 +290,9 @@
     judges = len(packets)
     outs = [shape((PACKET, channels), BF16)] * judges
     outs = outs + [shape((rows, channels), BF16)] * judges
-    outs = outs + [shape((judges * batch, channels), F32)]
+    outs = outs + [shape((8, channels), F32)]
     body = functools.partial(judge_others_body, judges, batch)
-    scratch = [pltpu.VMEM((judges, 8, channels), F32)]
+    scratch = [pltpu.VMEM((8, channels), F32)]
     flops = 8 * 6 * 2 * 1024 * 128 * 128
     results = call(body, list(packets) + [fakes, after], outs, scratch, flops=flops)
     return results[:judges], results[judges : 2 * judges], results[2 * judges]
@@ -273,10 +309,8 @@
     shift_row = jnp.concatenate([shifted[0:1, :], shifted[1:2, :]], axis=1)
     one = w_one.astype(BF16) * BF16(0.5)
     two = w_two.astype(BF16)
-    hidden, slope_gen = silu_parts(twice(0.5 * base.astype(BF16).astype(F32)) + shift_row)
-    hidden_half = hidden.astype(BF16)
-    middle, slope_mid = silu_parts(dot(hidden_half, both(one, one)))
-    middle_half = middle.astype(BF16)
+    _, hidden_half, slope_gen = silu_parts(twice(0.5 * base.astype(BF16).astype(F32)) + shift_row)
+    _, middle_half, slope_mid = silu_parts(dot(hidden_half, both(one, one)))
     fakes = (hidden_half.astype(F32) + dot(middle_half, both(two, two))).astype(BF16)
     fakes_ref[0:places, :] = fakes[:, 0:channels]
     fakes_ref[places : 2 * places, :] = fakes[:, channels : 2 * channels]
@@ -292,8 +326,8 @@
         shape((2 * places, channels), BF16),
         shape(wide, BF16),
         shape(wide, BF16),
-        shape(wide, F32),
-        shape(wide, F32),
+        shape(wide, BF16),
+        shape(wide, BF16),
     ]
 
 
@@ -352,11 +386,11 @@
     return results[:4], results[4], results[5], results[6:]
 
 
-def gen_back_body(step, judges, *refs):
+def gen_back_body(step, judges, groups, *refs):
     is_last = step == STEPS - 1
     refs = list(refs)
     units = [refs.pop(0) for _ in range(judges)]
-    own_slope, other_slopes = [refs.pop(0) for _ in range(2)]
+    slopes = [refs.pop(0) for _ in range(1 + len(groups))]
     hidden_ref, middle_ref, gen_slope_ref, mid_slope_ref, latent_ref = [refs.pop(0) for _ in range(5)]
     in_ref, base_ref, one_ref, two_ref = [refs.pop(0) for _ in range(4)]
     new_in, new_base, new_one, new_two = [refs.pop(0) for _ in range(4)]
@@ -366,17 +400,20 @@
 
     halves = []
     for member, span in enumerate(spans):
-        total = own_slope[member : member + 1, :] * units[0][span, :].astype(F32)
-        for which in range(1, judges):
-            place = 2 * (which - 1) + member
-            total = total + other_slopes[place : place + 1, :] * units[which][span, :].astype(F32)
+        total = slopes[0][member : member + 1, :] * units[0][span, :].astype(F32)
+        others = iter(units[1:])
+        for slope_ref, size in zip(slopes[1:], groups):
+            for which in range(size):
+                place = which * len(spans) + member
+                unit_ref = next(others)
+                total = total + slope_ref[place : place + 1, :] * unit_ref[span, :].astype(F32)
         halves.append(total)
     cotangent = jnp.concatenate(halves, axis=1)
     cotangent_half = cotangent.astype(BF16)
     one = one_ref[...].astype(BF16)
     two = two_ref[...].astype(BF16) * BF16(0.5)
-    inner_half = (dot_turned(cotangent_half, both(two, two)) * mid_slope_ref[...]).astype(BF16)
-    outer = (cotangent + dot_turned(inner_half, both(one, one))) * gen_slope_ref[...]
+    inner_half = (dot_turned(cotangent_half, both(two, two)).astype(BF16) * mid_slope_ref[...])
+    outer = (cotangent + dot_turned(inner_half, both(one, one))) * gen_slope_ref[...].astype(F32)
     grad_two = [dot_rows(middle_ref[:, side], cotangent_half[:, side]) for side in sides]
     grad_one = [dot_rows(hidden_ref[:, side], inner_half[:, side]) for side in sides]
     sums = jnp.sum(jnp.sum(outer.reshape(-1, 8, 2 * channels), axis=0), axis=0, keepdims=True)
@@ -397,13 +434,13 @@
         gen_forward(latent_ref[step + 1], w_in, base, w_one, w_two, refs)
 
 
-def gen_back(step, units, own_slope, other_slopes, stored, latents, weights):
+def gen_back(step, units, slopes, groups, stored, latents, weights):
     places, channels = weights[1].shape
-    operands = list(units) + [own_slope, other_slopes] + list(stored[1:]) + [latents] + list(weights)
+    operands = list(units) + list(slopes) + list(stored[1:]) + [latents] + list(weights)
     outs = [shape(member.shape, F32) for member in weights]
     if step < STEPS - 1:
         outs = outs + stored_shapes(places, channels)
-    body = functools.partial(gen_back_body, step, len(units))
+    body = functools.partial(gen_back_body, step, len(units), groups)
     flops = 12 * 2 * 1024 * 128 * 128
     results = call(body, operands, outs, flops=flops)
     return results[:4], results[4:]
@@ -430,7 +467,7 @@
         out = out + packet_row(tail, 0)
         tails.append([packet_row(tail, 1 + i) for i in range(batch)])
     ordered = verdicts[:batch]
-    for axis, (inner, outer) in (("row", tails[0:2]), ("col", tails[2:4])):
+    for axis, (inner, outer) in (("row", (tails[2], tails[1])), ("col", (tails[3], tails[0]))):
         is_odd = lax.rem(lax.axis_index(axis), 2) == 1
         ordered = ordered + [jnp.where(is_odd, a, b) for a, b in zip(inner, outer)]
         ordered = ordered + [jnp.where(is_odd, b, a) for a, b in zip(inner, outer)]
@@ -472,7 +509,8 @@
     return lax.ppermute(block, axis, route)
 
 
-EDGES = (("row", 0), ("row", 1), ("col", 0), ("col", 1))
+EDGES = (("col", 1), ("row", 1), ("row", 0), ("col", 0))
+GROUPS = ((0, 1, 2, 3),)
 
 
 def on_device(
@@ -494,12 +532,19 @@
                 [member[0, 0] for member in (g_in, g_base, g_one, g_two)],
             )
         fakes = stored[0]
-        own_grads, own_unit, own_slope = judge_own(packet, fakes, reals_rows, step, batch, reals)
-        grads, units, other_slopes = judge_others(arrived, fakes, batch, own_slope)
-        returns = [paired(member, axis, offset) for member, (axis, offset) in zip(grads, EDGES)]
-        gens, stored = gen_back(
-            step, [own_unit] + list(units), own_slope, other_slopes, stored, latents, gens
-        )
+        returns = [None] * len(EDGES)
+        units = [None] * len(EDGES)
+        own_grads, own_unit, after = judge_own(packet, fakes, reals_rows, stored[1], step, batch, reals)
+        slopes = [after]
+        for group in GROUPS:
+            grads, some, after = judge_others([arrived[i] for i in group], fakes, batch, after)
+            slopes.append(after)
+            for i, grad, unit in zip(group, grads, some):
+                returns[i] = paired(grad, *EDGES[i])
+                units[i] = unit
+        units = [own_unit] + [units[i] for group in GROUPS for i in group]
+        sizes = [len(group) for group in GROUPS]
+        gens, stored = gen_back(step, units, slopes, sizes, stored, latents, gens)
         results = disc_update(
             own_grads, returns, gens[0], discs, verdict if is_last else None, batch, reals
         )

time: 56.7 us -> 51.7 us (0.912)
  waiting for transfers between devices: 11.3 us -> 7.81 us
  Pallas kernels: 22 us -> 21.1 us
  starting transfers between devices: 22.5 us -> 21.9 us
    ppermute x16, waiting for transfers between devices: 11.3 us -> 7.81 us  [paired(): return lax.ppermute(block, axis, route)]
    pallas_call x10, Pallas kernels: 22 us -> 21.1 us  [call(): pl.pallas_call(body, out_shape=tuple(out_shape), in_specs=[pl.BlockSpec(m...]
    ppermute x16, starting transfers between devices: 22.5 us -> 21.9 us  [paired(): return lax.ppermute(block, axis, route)]
  transfers between devices with their start and end apart: 16 -> 16, of which waited for: 6 -> 7; matrix products, arithmetic and copies ran while one was open for 0% -> 0% of each run, Pallas kernels for 20% -> 22%
where the time goes in v2:
time: 51.7 us; the launch traced here: 51.5 us
  starting transfers between devices  21.9 us (42%)
  Pallas kernels  21.1 us (41%)
  waiting for transfers between devices  7.81 us (15%)
  between operations  0.73 us (1%)
    ppermute x16, starting transfers between devices, paired(): return lax.ppermute(block, axis, route)  21.9 us
    pallas_call x10, Pallas kernels, call(): pl.pallas_call(body, out_shape=tuple(out_shape), in_specs=[pl.BlockSpec(m...  21.1 us
    ppermute x16, waiting for transfers between devices, paired(): return lax.ppermute(block, axis, route)  7.81 us
  transfers between devices with their start and end apart: 16, of which 7 were waited for; matrix products, arithmetic and copies ran while one was open for 0% of the time, Pallas kernels for 22%

profile of v2, /device:TPU:0, one launch (start us, length us, event | category | flops | bytes accessed | tf_op | source)
XLA Modules:
  0.0 51.5 jit_solution(14177032348605835241)
XLA Ops:
  0.6 0.9 %shard_map.170 = (bf16[272,128]{1,0:T(8,128)(2,1)S(1)}, f32[128,128]{1,0:T(8,128)S(1)}, f32[128,128]{1,0:T(8,128)S(1)}, f32[1,128]{1,0:T(1,128)S(1)}) custom-call(f32[128,128]{1,0:T(8,128)} %bitcast.24, f32[128,128]{1,0:T(8,128)} %bitcast.25, f32[1,128]{1,0:T(1,128)} %bitcast.28), custom_call_target="tpu_custom_call" | custom-call | tf_op jit(solution)/shard_map/pallas_call | solution.py:64
  1.6 5.7 %collective-permute-start = (bf16[272,128]{1,0:T(8,128)(2,1)S(1)}, bf16[272,128]{1,0:T(8,128)(2,1)S(1)}, u32[]{:S(2)}, u32[]{:S(2)}) collective-permute-start(bf16[272,128]{1,0:T(8,128)(2,1)S(1)} %get-tuple-element.69.packet_ref), channel_id=1, source_target_pairs={{1,2},{2,1},{3,4},{4,3},{5,6},{6,5},{7,8},{8,7},{9,10},{10,9},{11,... | collective-permute-start | bytes 208904 | tf_op jit(solution)/shard_map/ppermute | solution.py:509
  7.2 3.5 %collective-permute-start.1 = (bf16[272,128]{1,0:T(8,128)(2,1)S(1)}, bf16[272,128]{1,0:T(8,128)(2,1)S(1)}, u32[]{:S(2)}, u32[]{:S(2)}) collective-permute-start(bf16[272,128]{1,0:T(8,128)(2,1)S(1)} %get-tuple-element.69.packet_ref), channel_id=1, source_target_pairs={{16,32},{32,16},{48,64},{64,48},{80,96},{96,80},{112,0},{0,112},{1... | collective-permute-start | bytes 208904 | tf_op jit(solution)/shard_map/ppermute | solution.py:509
  10.7 2.6 %shard_map.171 = (f32[128,128]{1,0:T(8,128)S(1)}, f32[1024,128]{1,0:T(8,128)S(1)}, f32[128,128]{1,0:T(8,128)S(1)}, f32[128,128]{1,0:T(8,128)S(1)}, f32[2,8,128]{...) custom-call(s32[2,2]{1,0:T(2,128)} %bitcast.26, ...), custom_call_target="tpu_custom_call" | custom-call | flops 134217728 | bytes 134217 | tf_op jit(solution)/shard_map/pallas_call | solution.py:64
  13.3 2.5 %shard_map.172 = (f32[272,128]{1,0:T(8,128)S(1)}, bf16[2048,128]{1,0:T(8,128)(2,1)S(1)}, f32[8,128]{1,0:T(8,128)S(1)}) custom-call(bf16[272,128]{1,0:T(8,128)(2,1)S(1)} %get-tuple-element.69.packet_ref, bf16[2048,128]{1,0:T(8,128)(2,1)S(1)} %get-tuple-element.70.fakes_ref.refs_4_, bf16[4,1024,128]{2,1,0:T(8,128)(2,1)S(1)} %get-tuple-element.71.reals_ref, ...), custom_call_target="tpu_custom_call" | custom-call | flops 805306368 | bytes 805306 | tf_op jit(solution)/shard_map/pallas_call | solution.py:64
  15.8 4.1 %shard_map.173 = (bf16[272,128]{1,0:T(8,128)(2,1)S(1)}, bf16[272,128]{1,0:T(8,128)(2,1)S(1)}, bf16[272,128]{1,0:T(8,128)(2,1)S(1)}, bf16[272,128]{1,0:T(8,128)(2...) custom-call(bf16[272,128]{1,0:T(8,128)(2,1)S(1)} %collective-permute, ...), custom_call_target="tpu_custom_call" | custom-call | flops 1610612736 | bytes 1610612 | tf_op jit(solution)/shard_map/pallas_call | solution.py:64
  19.9 1.6 %collective-permute-start.4 = (bf16[272,128]{1,0:T(8,128)(2,1)S(1)}, bf16[272,128]{1,0:T(8,128)(2,1)S(1)}, u32[]{:S(2)}, u32[]{:S(2)}) collective-permute-start(bf16[272,128]{1,0:T(8,128)(2,1)S(1)} %get-tuple-element.75), channel_id=1, source_target_pairs={{1,2},{2,1},{3,4},{4,3},{5,6},{6,5},{7,8},{8,7},{9,10},{10,9},{11,... | collective-permute-start | bytes 208904 | tf_op jit(solution)/shard_map/ppermute | solution.py:509
  21.6 1.6 %collective-permute-start.5 = (bf16[272,128]{1,0:T(8,128)(2,1)S(1)}, bf16[272,128]{1,0:T(8,128)(2,1)S(1)}, u32[]{:S(2)}, u32[]{:S(2)}) collective-permute-start(bf16[272,128]{1,0:T(8,128)(2,1)S(1)} %get-tuple-element.76), channel_id=1, source_target_pairs={{16,32},{32,16},{48,64},{64,48},{80,96},{96,80},{112,0},{0,112},{1... | collective-permute-start | bytes 208904 | tf_op jit(solution)/shard_map/ppermute | solution.py:509
  23.6 1.7 %shard_map.174 = (f32[128,128]{1,0:T(8,128)S(1)}, f32[1024,128]{1,0:T(8,128)S(1)}, f32[128,128]{1,0:T(8,128)S(1)}, f32[128,128]{1,0:T(8,128)S(1)}, bf16[2048,128...) custom-call(bf16[2048,128]{1,0:T(8,128)(2,1)S(1)} %get-tuple-element, ...), custom_call_target="tpu_custom_call" | custom-call | flops 402653184 | bytes 402653 | tf_op jit(solution)/shard_map/pallas_call | solution.py:64
  25.3 2.1 %collective-permute-done.4.refs_0_ = bf16[272,128]{1,0:T(8,128)(2,1)S(1)} collective-permute-done((bf16[272,128]{1,0:T(8,128)(2,1)S(1)}, bf16[272,128]{1,0:T(8,128)(2,1)S(1)}, u32[]{:S(2)}, u32[]{:S(2)}) %collective-permute-start.4) | collective-permute-done | bytes 69664 | tf_op jit(solution)/shard_map/ppermute | solution.py:509
  27.4 0.7 %collective-permute-done.5.refs_1_ = bf16[272,128]{1,0:T(8,128)(2,1)S(1)} collective-permute-done((bf16[272,128]{1,0:T(8,128)(2,1)S(1)}, bf16[272,128]{1,0:T(8,128)(2,1)S(1)}, u32[]{:S(2)}, u32[]{:S(2)}) %collective-permute-start.5) | collective-permute-done | bytes 69664 | tf_op jit(solution)/shard_map/ppermute | solution.py:509
  28.0 0.8 %collective-permute-done.6.refs_2_ = bf16[272,128]{1,0:T(8,128)(2,1)S(1)} collective-permute-done((bf16[272,128]{1,0:T(8,128)(2,1)S(1)}, bf16[272,128]{1,0:T(8,128)(2,1)S(1)}, u32[]{:S(2)}, u32[]{:S(2)}) %collective-permute-start.6) | collective-permute-done | bytes 69664 | tf_op jit(solution)/shard_map/ppermute | solution.py:509
  28.9 2.6 %collective-permute-start.8 = (bf16[272,128]{1,0:T(8,128)(2,1)S(1)}, bf16[272,128]{1,0:T(8,128)(2,1)S(1)}, u32[]{:S(2)}, u32[]{:S(2)}) collective-permute-start(bf16[272,128]{1,0:T(8,128)(2,1)S(1)} %get-tuple-element.97.packet_ref), channel_id=1, source_target_pairs={{1,2},{2,1},{3,4},{4,3},{5,6},{6,5},{7,8},{8,7},{9,10},{10,9},{11,... | collective-permute-start | bytes 208904 | tf_op jit(solution)/shard_map/ppermute | solution.py:509
  31.6 1.5 %collective-permute-start.9 = (bf16[272,128]{1,0:T(8,128)(2,1)S(1)}, bf16[272,128]{1,0:T(8,128)(2,1)S(1)}, u32[]{:S(2)}, u32[]{:S(2)}) collective-permute-start(bf16[272,128]{1,0:T(8,128)(2,1)S(1)} %get-tuple-element.97.packet_ref), channel_id=1, source_target_pairs={{16,32},{32,16},{48,64},{64,48},{80,96},{96,80},{112,0},{0,112},{1... | collective-permute-start | bytes 208904 | tf_op jit(solution)/shard_map/ppermute | solution.py:509
  33.0 0.9 %collective-permute-start.10 = (bf16[272,128]{1,0:T(8,128)(2,1)S(1)}, bf16[272,128]{1,0:T(8,128)(2,1)S(1)}, u32[]{:S(2)}, u32[]{:S(2)}) collective-permute-start(bf16[272,128]{1,0:T(8,128)(2,1)S(1)} %get-tuple-element.97.packet_ref), channel_id=1, source_target_pairs={{0,16},{16,0},{32,48},{48,32},{64,80},{80,64},{96,112},{112,96},{1... | collective-permute-start | bytes 208904 | tf_op jit(solution)/shard_map/ppermute | solution.py:509
  34.0 2.5 %shard_map.176 = (f32[272,128]{1,0:T(8,128)S(1)}, bf16[2048,128]{1,0:T(8,128)(2,1)S(1)}, f32[8,128]{1,0:T(8,128)S(1)}) custom-call(bf16[272,128]{1,0:T(8,128)(2,1)S(1)} %get-tuple-element.97.packet_ref, bf16[2048,128]{1,0:T(8,128)(2,1)S(1)} %get-tuple-element.98.fakes_ref.refs_4_, bf16[4,1024,128]{2,1,0:T(8,128)(2,1)S(1)} %get-tuple-element.71.reals_ref, ...), custom_call_target="tpu_custom_call" | custom-call | flops 805306368 | bytes 805306 | tf_op jit(solution)/shard_map/pallas_call | solution.py:64
  36.5 1.5 %collective-permute-done.9.refs_1_ = bf16[272,128]{1,0:T(8,128)(2,1)S(1)} collective-permute-done((bf16[272,128]{1,0:T(8,128)(2,1)S(1)}, bf16[272,128]{1,0:T(8,128)(2,1)S(1)}, u32[]{:S(2)}, u32[]{:S(2)}) %collective-permute-start.9) | collective-permute-done | bytes 69664 | tf_op jit(solution)/shard_map/ppermute | solution.py:509
  38.1 4.1 %shard_map.177 = (bf16[272,128]{1,0:T(8,128)(2,1)S(1)}, bf16[272,128]{1,0:T(8,128)(2,1)S(1)}, bf16[272,128]{1,0:T(8,128)(2,1)S(1)}, bf16[272,128]{1,0:T(8,128)(2...) custom-call(bf16[272,128]{1,0:T(8,128)(2,1)S(1)} %collective-permute, ...), custom_call_target="tpu_custom_call" | custom-call | flops 1610612736 | bytes 1610612 | tf_op jit(solution)/shard_map/pallas_call | solution.py:64
  42.2 2.1 %collective-permute-start.12 = (bf16[272,128]{1,0:T(8,128)(2,1)S(1)}, bf16[272,128]{1,0:T(8,128)(2,1)S(1)}, u32[]{:S(2)}, u32[]{:S(2)}) collective-permute-start(bf16[272,128]{1,0:T(8,128)(2,1)S(1)} %get-tuple-element.118), channel_id=1, source_target_pairs={{1,2},{2,1},{3,4},{4,3},{5,6},{6,5},{7,8},{8,7},{9,10},{10,9},{11,... | collective-permute-start | bytes 208904 | tf_op jit(solution)/shard_map/ppermute | solution.py:509
  44.3 1.5 %collective-permute-start.13 = (bf16[272,128]{1,0:T(8,128)(2,1)S(1)}, bf16[272,128]{1,0:T(8,128)(2,1)S(1)}, u32[]{:S(2)}, u32[]{:S(2)}) collective-permute-start(bf16[272,128]{1,0:T(8,128)(2,1)S(1)} %get-tuple-element.119), channel_id=1, source_target_pairs={{16,32},{32,16},{48,64},{64,48},{80,96},{96,80},{112,0},{0,112},{1... | collective-permute-start | bytes 208904 | tf_op jit(solution)/shard_map/ppermute | solution.py:509
  45.8 0.5 %collective-permute-start.14 = (bf16[272,128]{1,0:T(8,128)(2,1)S(1)}, bf16[272,128]{1,0:T(8,128)(2,1)S(1)}, u32[]{:S(2)}, u32[]{:S(2)}) collective-permute-start(bf16[272,128]{1,0:T(8,128)(2,1)S(1)} %get-tuple-element.120), channel_id=1, source_target_pairs={{0,16},{16,0},{32,48},{48,32},{64,80},{80,64},{96,112},{112,96},{1... | collective-permute-start | bytes 208904 | tf_op jit(solution)/shard_map/ppermute | solution.py:509
  46.3 1.9 %shard_map.178 = (f32[128,128]{1,0:T(8,128)}, f32[1024,128]{1,0:T(8,128)}, f32[128,128]{1,0:T(8,128)}, f32[128,128]{1,0:T(8,128)}) custom-call(bf16[2048,128]{1,0:T(8,128)(2,1)S(1)} %get-tuple-element.100.refs_0_, bf16[2048,128]{1,0:T(8,128)(2,1)S(1)} %get-tuple-element.102.refs_1_, bf16[2048,128]{1,0:T(8,128)(2,1)S(1)} %get-tuple-element.103.refs_2_, ...), custom_call_target="tpu_custom_call" | custom-call | flops 402653184 | bytes 402653 | tf_op jit(solution)/shard_map/pallas_call | solution.py:64
  48.2 2.2 %collective-permute-done.12.refs_0_ = bf16[272,128]{1,0:T(8,128)(2,1)S(1)} collective-permute-done((bf16[272,128]{1,0:T(8,128)(2,1)S(1)}, bf16[272,128]{1,0:T(8,128)(2,1)S(1)}, u32[]{:S(2)}, u32[]{:S(2)}) %collective-permute-start.12) | collective-permute-done | bytes 69664 | tf_op jit(solution)/shard_map/ppermute | solution.py:509
  50.8 0.7 %shard_map.179 = (f32[128,128]{1,0:T(8,128)}, f32[128,128]{1,0:T(8,128)}, f32[1,128]{1,0:T(1,128)}, f32[2,12]{1,0:T(2,128)}) custom-call(f32[272,128]{1,0:T(8,128)S(1)} %get-tuple-element.117.grads_ref, bf16[272,128]{1,0:T(8,128)(2,1)S(1)} %collective-permute-done.12.refs_0_, bf16[272,128]{1,0:T(8,128)(2,1)S(1)} %collective-permute-done.13.refs_1_, ...), custom_call_target="tpu_custom_call" | custom-call | tf_op jit(solution)/shard_map/pallas_call | solution.py:64
  (18 shorter events, 1.0 us)
Async XLA Ops:
  1.6 14.2 %collective-permute-start = (bf16[272,128]{1,0:T(8,128)(2,1)S(1)}, bf16[272,128]{1,0:T(8,128)(2,1)S(1)}, u32[]{:S(2)}, u32[]{:S(2)}) collective-permute-start(bf16[272,128]{1,0:T(8,128)(2,1)S(1)} %get-tuple-element.69.packet_ref), channel_id=1, source_target_pairs={{1,2},{2,1},{3,4},{4,3},{5,6},{6,5},{7,8},{8,7},{9,10},{10,9},{11,... | collective-permute-start | bytes 208904 | tf_op jit(solution)/shard_map/ppermute | solution.py:509
  7.2 8.5 %collective-permute-start.1 = (bf16[272,128]{1,0:T(8,128)(2,1)S(1)}, bf16[272,128]{1,0:T(8,128)(2,1)S(1)}, u32[]{:S(2)}, u32[]{:S(2)}) collective-permute-start(bf16[272,128]{1,0:T(8,128)(2,1)S(1)} %get-tuple-element.69.packet_ref), channel_id=1, source_target_pairs={{16,32},{32,16},{48,64},{64,48},{80,96},{96,80},{112,0},{0,112},{1... | collective-permute-start | bytes 208904 | tf_op jit(solution)/shard_map/ppermute | solution.py:509
  10.7 5.1 %collective-permute-start.2 = (bf16[272,128]{1,0:T(8,128)(2,1)S(1)}, bf16[272,128]{1,0:T(8,128)(2,1)S(1)}, u32[]{:S(2)}, u32[]{:S(2)}) collective-permute-start(bf16[272,128]{1,0:T(8,128)(2,1)S(1)} %get-tuple-element.69.packet_ref), channel_id=1, source_target_pairs={{0,16},{16,0},{32,48},{48,32},{64,80},{80,64},{96,112},{112,96},{1... | collective-permute-start | bytes 208904 | tf_op jit(solution)/shard_map/ppermute | solution.py:509
  10.7 5.1 %collective-permute-start.3 = (bf16[272,128]{1,0:T(8,128)(2,1)S(1)}, bf16[272,128]{1,0:T(8,128)(2,1)S(1)}, u32[]{:S(2)}, u32[]{:S(2)}) collective-permute-start(bf16[272,128]{1,0:T(8,128)(2,1)S(1)} %get-tuple-element.69.packet_ref), channel_id=1, source_target_pairs={{0,1},{1,0},{2,3},{3,2},{4,5},{5,4},{6,7},{7,6},{8,9},{9,8},{10,11... | collective-permute-start | bytes 208904 | tf_op jit(solution)/shard_map/ppermute | solution.py:509
  19.9 7.4 %collective-permute-start.4 = (bf16[272,128]{1,0:T(8,128)(2,1)S(1)}, bf16[272,128]{1,0:T(8,128)(2,1)S(1)}, u32[]{:S(2)}, u32[]{:S(2)}) collective-permute-start(bf16[272,128]{1,0:T(8,128)(2,1)S(1)} %get-tuple-element.75), channel_id=1, source_target_pairs={{1,2},{2,1},{3,4},{4,3},{5,6},{6,5},{7,8},{8,7},{9,10},{10,9},{11,... | collective-permute-start | bytes 208904 | tf_op jit(solution)/shard_map/ppermute | solution.py:509
  21.6 6.5 %collective-permute-start.5 = (bf16[272,128]{1,0:T(8,128)(2,1)S(1)}, bf16[272,128]{1,0:T(8,128)(2,1)S(1)}, u32[]{:S(2)}, u32[]{:S(2)}) collective-permute-start(bf16[272,128]{1,0:T(8,128)(2,1)S(1)} %get-tuple-element.76), channel_id=1, source_target_pairs={{16,32},{32,16},{48,64},{64,48},{80,96},{96,80},{112,0},{0,112},{1... | collective-permute-start | bytes 208904 | tf_op jit(solution)/shard_map/ppermute | solution.py:509
  23.2 5.7 %collective-permute-start.6 = (bf16[272,128]{1,0:T(8,128)(2,1)S(1)}, bf16[272,128]{1,0:T(8,128)(2,1)S(1)}, u32[]{:S(2)}, u32[]{:S(2)}) collective-permute-start(bf16[272,128]{1,0:T(8,128)(2,1)S(1)} %get-tuple-element.77), channel_id=1, source_target_pairs={{0,16},{16,0},{32,48},{48,32},{64,80},{80,64},{96,112},{112,96},{1... | collective-permute-start | bytes 208904 | tf_op jit(solution)/shard_map/ppermute | solution.py:509
  23.6 5.3 %collective-permute-start.7 = (bf16[272,128]{1,0:T(8,128)(2,1)S(1)}, bf16[272,128]{1,0:T(8,128)(2,1)S(1)}, u32[]{:S(2)}, u32[]{:S(2)}) collective-permute-start(bf16[272,128]{1,0:T(8,128)(2,1)S(1)} %get-tuple-element.78), channel_id=1, source_target_pairs={{0,1},{1,0},{2,3},{3,2},{4,5},{5,4},{6,7},{7,6},{8,9},{9,8},{10,11... | collective-permute-start | bytes 208904 | tf_op jit(solution)/shard_map/ppermute | solution.py:509
  28.9 7.6 %collective-permute-start.8 = (bf16[272,128]{1,0:T(8,128)(2,1)S(1)}, bf16[272,128]{1,0:T(8,128)(2,1)S(1)}, u32[]{:S(2)}, u32[]{:S(2)}) collective-permute-start(bf16[272,128]{1,0:T(8,128)(2,1)S(1)} %get-tuple-element.97.packet_ref), channel_id=1, source_target_pairs={{1,2},{2,1},{3,4},{4,3},{5,6},{6,5},{7,8},{8,7},{9,10},{10,9},{11,... | collective-permute-start | bytes 208904 | tf_op jit(solution)/shard_map/ppermute | solution.py:509
  31.6 6.5 %collective-permute-start.9 = (bf16[272,128]{1,0:T(8,128)(2,1)S(1)}, bf16[272,128]{1,0:T(8,128)(2,1)S(1)}, u32[]{:S(2)}, u32[]{:S(2)}) collective-permute-start(bf16[272,128]{1,0:T(8,128)(2,1)S(1)} %get-tuple-element.97.packet_ref), channel_id=1, source_target_pairs={{16,32},{32,16},{48,64},{64,48},{80,96},{96,80},{112,0},{0,112},{1... | collective-permute-start | bytes 208904 | tf_op jit(solution)/shard_map/ppermute | solution.py:509
  33.0 5.1 %collective-permute-start.10 = (bf16[272,128]{1,0:T(8,128)(2,1)S(1)}, bf16[272,128]{1,0:T(8,128)(2,1)S(1)}, u32[]{:S(2)}, u32[]{:S(2)}) collective-permute-start(bf16[272,128]{1,0:T(8,128)(2,1)S(1)} %get-tuple-element.97.packet_ref), channel_id=1, source_target_pairs={{0,16},{16,0},{32,48},{48,32},{64,80},{80,64},{96,112},{112,96},{1... | collective-permute-start | bytes 208904 | tf_op jit(solution)/shard_map/ppermute | solution.py:509
  34.0 4.1 %collective-permute-start.11 = (bf16[272,128]{1,0:T(8,128)(2,1)S(1)}, bf16[272,128]{1,0:T(8,128)(2,1)S(1)}, u32[]{:S(2)}, u32[]{:S(2)}) collective-permute-start(bf16[272,128]{1,0:T(8,128)(2,1)S(1)} %get-tuple-element.97.packet_ref), channel_id=1, source_target_pairs={{0,1},{1,0},{2,3},{3,2},{4,5},{5,4},{6,7},{7,6},{8,9},{9,8},{10,11... | collective-permute-start | bytes 208904 | tf_op jit(solution)/shard_map/ppermute | solution.py:509
  42.2 8.2 %collective-permute-start.12 = (bf16[272,128]{1,0:T(8,128)(2,1)S(1)}, bf16[272,128]{1,0:T(8,128)(2,1)S(1)}, u32[]{:S(2)}, u32[]{:S(2)}) collective-permute-start(bf16[272,128]{1,0:T(8,128)(2,1)S(1)} %get-tuple-element.118), channel_id=1, source_target_pairs={{1,2},{2,1},{3,4},{4,3},{5,6},{6,5},{7,8},{8,7},{9,10},{10,9},{11,... | collective-permute-start | bytes 208904 | tf_op jit(solution)/shard_map/ppermute | solution.py:509
  44.3 6.5 %collective-permute-start.13 = (bf16[272,128]{1,0:T(8,128)(2,1)S(1)}, bf16[272,128]{1,0:T(8,128)(2,1)S(1)}, u32[]{:S(2)}, u32[]{:S(2)}) collective-permute-start(bf16[272,128]{1,0:T(8,128)(2,1)S(1)} %get-tuple-element.119), channel_id=1, source_target_pairs={{16,32},{32,16},{48,64},{64,48},{80,96},{96,80},{112,0},{0,112},{1... | collective-permute-start | bytes 208904 | tf_op jit(solution)/shard_map/ppermute | solution.py:509
  45.8 5.1 %collective-permute-start.14 = (bf16[272,128]{1,0:T(8,128)(2,1)S(1)}, bf16[272,128]{1,0:T(8,128)(2,1)S(1)}, u32[]{:S(2)}, u32[]{:S(2)}) collective-permute-start(bf16[272,128]{1,0:T(8,128)(2,1)S(1)} %get-tuple-element.120), channel_id=1, source_target_pairs={{0,16},{16,0},{32,48},{48,32},{64,80},{80,64},{96,112},{112,96},{1... | collective-permute-start | bytes 208904 | tf_op jit(solution)/shard_map/ppermute | solution.py:509
  46.3 4.5 %collective-permute-start.15 = (bf16[272,128]{1,0:T(8,128)(2,1)S(1)}, bf16[272,128]{1,0:T(8,128)(2,1)S(1)}, u32[]{:S(2)}, u32[]{:S(2)}) collective-permute-start(bf16[272,128]{1,0:T(8,128)(2,1)S(1)} %get-tuple-element.121), channel_id=1, source_target_pairs={{0,1},{1,0},{2,3},{3,2},{4,5},{5,4},{6,7},{7,6},{8,9},{9,8},{10,11... | collective-permute-start | bytes 208904 | tf_op jit(solution)/shard_map/ppermute | solution.py:509

commit v3 on v2

--- a/solution.py
+++ b/solution.py
@@ -152,12 +152,11 @@
     product = dot_turned(outer_half, both(*two) * half)
     yield
     inner_half = product.astype(BF16) * slope_first
-    product = dot_turned(inner_half, both(*one))
     channels = inner_half.shape[1] // 2
     sides = [slice(0, channels), slice(channels, 2 * channels)]
     grad_two = [dot_rows(first_half[:, s], outer_half[:, s]) for s in sides]
     yield
-    result.append((outer + product).astype(BF16))
+    result.append((outer_half, inner_half))
     if shared:
         wide = dot_rows(images, inner_half)
         grad_one = [wide[:, s] for s in sides]
@@ -207,7 +206,7 @@
     return totals
 
 
-def judge_own_body(step, batch, reals, packet_ref, fakes_ref, reals_ref, _, grads_ref, unit_ref, slope_ref, lines_ref):
+def judge_own_body(step, batch, reals, packet_ref, fakes_ref, reals_ref, _, grads_ref, outer_ref, inner_ref, slope_ref, lines_ref):
     rows, channels = fakes_ref.shape
     places = rows // batch
     one, two, out_row = unpack(packet_ref)
@@ -219,7 +218,9 @@
         pairs.append((images, (one, one), (two, two), out_pair, False))
     results = judge_pairs(pairs)
     for member, result in enumerate(results):
-        unit_ref[member * places : (member + 1) * places, :] = result[0][:, 0:channels]
+        side = slice(member * channels, (member + 1) * channels)
+        outer_ref[:, side] = result[0][0][:, 0:channels]
+        inner_ref[:, side] = result[0][1][:, 0:channels]
     triples = [result[1] for result in results] + [result[2] for result in results]
     signs = [1] * batch + [0] * reals
     verdicts, minus, slopes = verdict_lines(triples, [out_row] * len(signs), signs, places, lines_ref)
@@ -233,9 +234,11 @@
 
 def judge_own(packet, fakes, reals_rows, after, step, batch, reals):
     rows, channels = fakes.shape
+    wide = (rows // batch, batch * channels)
     outs = [
         shape((PACKET, channels), F32),
-        shape((rows, channels), BF16),
+        shape(wide, BF16),
+        shape(wide, BF16),
         shape((8, channels), F32),
     ]
     body = functools.partial(judge_own_body, step, batch, reals)
@@ -249,7 +252,7 @@
     fakes_ref = refs.pop(0)
     refs.pop(0)
     grads = [refs.pop(0) for _ in range(judges)]
-    units = [refs.pop(0) for _ in range(judges)]
+    terms = [(refs.pop(0), refs.pop(0)) for _ in range(judges * batch // 2)]
     slope_ref = refs.pop(0)
     lines_ref = refs.pop(0)
     rows, channels = fakes_ref.shape
@@ -258,21 +261,16 @@
     spans = [slice(member * places, (member + 1) * places) for member in range(batch)]
     pairs = []
     homes = []
-    for which in range(0, judges - 1, 2):
+    for which in range(0, judges, 2):
         ones, twos, outs = zip(*parts[which : which + 2])
         for member, span in enumerate(spans):
             pairs.append((fakes_ref[span, :], ones, twos, jnp.concatenate(outs, axis=1), True))
             homes.append(((which, member), (which + 1, member)))
-    if judges % 2:
-        one, two, out_row = parts[-1]
-        images = jnp.concatenate([fakes_ref[span, :] for span in spans], axis=1)
-        pairs.append((images, (one, one), (two, two), twice(out_row), False))
-        homes.append(tuple((judges - 1, member) for member in range(batch)))
     found = {}
-    for result, home in zip(judge_pairs(pairs), homes):
-        for side, (which, member) in enumerate(home):
-            units[which][spans[member], :] = result[0][:, side * channels : (side + 1) * channels]
-            found[which, member] = result[1 + side]
+    for result, home, (outer_ref, inner_ref) in zip(judge_pairs(pairs), homes, terms):
+        outer_ref[...], inner_ref[...] = result[0]
+        for side, key in enumerate(home):
+            found[key] = result[1 + side]
     keys = sorted(found)
     triples = [found[key] for key in keys]
     out_rows = [parts[which][2] for which, _ in keys]
@@ -289,13 +287,13 @@
     rows, channels = fakes.shape
     judges = len(packets)
     outs = [shape((PACKET, channels), BF16)] * judges
-    outs = outs + [shape((rows, channels), BF16)] * judges
+    outs = outs + [shape((rows // batch, 2 * channels), BF16)] * (judges * batch)
     outs = outs + [shape((8, channels), F32)]
     body = functools.partial(judge_others_body, judges, batch)
     scratch = [pltpu.VMEM((8, channels), F32)]
-    flops = 8 * 6 * 2 * 1024 * 128 * 128
+    flops = 2 * judges * 6 * 2 * 1024 * 128 * 128
     results = call(body, list(packets) + [fakes, after], outs, scratch, flops=flops)
-    return results[:judges], results[judges : 2 * judges], results[2 * judges]
+    return results[:judges], results[judges:-1], results[-1]
 
 
 def twice(tile):
@@ -336,33 +334,27 @@
     weight_refs = refs[6:10]
     latent_ref, reals_ref = refs[10:12]
     outs = refs[12:17]
-    raw_ref, seed_ref, index_ref, semaphores = refs[17:]
-    count = len(weights)
-    copies = start_all(list(zip(weights, weight_refs)), semaphores)
-    chosen = start_all(
-        [(seed_hbm, seed_ref), (index_hbm, index_ref)], semaphores.at[pl.ds(count, 2)]
-    )
-    raw_ref[...] = jnp.zeros_like(raw_ref)
-    for copy in chosen:
+    bank_ref, seed_ref, index_ref, semaphores = refs[17:]
+    count = len(weights) + 3
+    pairs = [(seed_hbm, seed_ref), (index_hbm, index_ref), (bank, bank_ref)]
+    copies = start_all(pairs + list(zip(weights, weight_refs)), semaphores)
+    latent_ref[...] = jnp.zeros_like(latent_ref)
+    for copy in copies[:2]:
         copy.wait()
-    early = []
     late = []
     for step in range(STEPS):
-        for member in range(batch):
-            early.append(
-                (bank.at[pl.ds(seed_ref[step, member], 1)], raw_ref.at[step, pl.ds(member, 1)])
-            )
         for member in range(reals):
             late.append((data.at[index_ref[step, member]], reals_ref.at[step * reals + member]))
-    rest = len(early + late)
-    others = start_all(early + late, semaphores.at[pl.ds(count + 2, rest)])
-    copies = copies + others
-    for copy in copies[: count + len(early)]:
+    late = start_all(late, semaphores.at[pl.ds(count, len(late))])
+    for copy in copies[2:]:
         copy.wait()
-    latent_ref[...] = raw_ref[...].astype(BF16).astype(F32)
+    for step in range(STEPS):
+        for member in range(batch):
+            row = bank_ref[pl.ds(seed_ref[step, member], 1), :]
+            latent_ref[step, member : member + 1, :] = row.astype(BF16).astype(F32)
     w_in, base, w_one, w_two = [ref[...] for ref in weight_refs]
     gen_forward(latent_ref[0], w_in, base, w_one, w_two, outs)
-    for copy in copies[count + len(early) :]:
+    for copy in late:
         copy.wait()
 
 
@@ -374,10 +366,10 @@
     outs = outs + [shape((STEPS, 8, channels), F32), shape((STEPS * reals, places, channels), BF16)]
     outs = outs + stored_shapes(places, channels)
     scratch = [
-        pltpu.VMEM((STEPS, 8, channels), F32),
+        pltpu.VMEM(bank.shape, F32),
         pltpu.SMEM(seed.shape, jnp.int32),
         pltpu.SMEM(index.shape, jnp.int32),
-        pltpu.SemaphoreType.DMA((len(weights) + 2 + STEPS * (batch + reals),)),
+        pltpu.SemaphoreType.DMA((len(weights) + 3 + STEPS * reals,)),
     ]
     operands = [seed, index, bank, data] + list(weights)
     body = functools.partial(begin_body, batch, reals)
@@ -386,29 +378,39 @@
     return results[:4], results[4], results[5], results[6:]
 
 
-def gen_back_body(step, judges, groups, *refs):
+def gen_back_body(step, judges, batch, *refs):
     is_last = step == STEPS - 1
     refs = list(refs)
-    units = [refs.pop(0) for _ in range(judges)]
-    slopes = [refs.pop(0) for _ in range(1 + len(groups))]
+    packets = [refs.pop(0) for _ in range(1 + judges)]
+    own_terms = [refs.pop(0) for _ in range(2)]
+    terms = [(refs.pop(0), refs.pop(0)) for _ in range(judges * batch // 2)]
+    own_slope, slope_ref = [refs.pop(0) for _ in range(2)]
     hidden_ref, middle_ref, gen_slope_ref, mid_slope_ref, latent_ref = [refs.pop(0) for _ in range(5)]
     in_ref, base_ref, one_ref, two_ref = [refs.pop(0) for _ in range(4)]
     new_in, new_base, new_one, new_two = [refs.pop(0) for _ in range(4)]
     places, channels = base_ref.shape
     sides = (slice(0, channels), slice(channels, 2 * channels))
-    spans = (slice(0, places), slice(places, 2 * places))
-
-    halves = []
-    for member, span in enumerate(spans):
-        total = slopes[0][member : member + 1, :] * units[0][span, :].astype(F32)
-        others = iter(units[1:])
-        for slope_ref, size in zip(slopes[1:], groups):
-            for which in range(size):
-                place = which * len(spans) + member
-                unit_ref = next(others)
-                total = total + slope_ref[place : place + 1, :] * unit_ref[span, :].astype(F32)
-        halves.append(total)
-    cotangent = jnp.concatenate(halves, axis=1)
+
+    def weighed(pair, ones, lines):
+        outer, inner = pair
+        unit = outer[...].astype(F32) + dot_turned(inner[...], both(*ones))
+        return unit * jnp.concatenate(lines, axis=1)
+
+    ones = [packet[0:channels, :] for packet in packets]
+    own_lines = [own_slope[member : member + 1, :] for member in range(batch)]
+    cotangent = weighed(own_terms, (ones[0], ones[0]), own_lines)
+    halves = [None] * batch
+    places_left = iter(terms)
+    for which in range(0, judges, 2):
+        for member in range(batch):
+            lines = []
+            for judge in (which, which + 1):
+                place = judge * batch + member
+                lines.append(slope_ref[place : place + 1, :])
+            part = weighed(next(places_left), (ones[1 + which], ones[2 + which]), lines)
+            part = part[:, sides[0]] + part[:, sides[1]]
+            halves[member] = part if halves[member] is None else halves[member] + part
+    cotangent = cotangent + jnp.concatenate(halves, axis=1)
     cotangent_half = cotangent.astype(BF16)
     one = one_ref[...].astype(BF16)
     two = two_ref[...].astype(BF16) * BF16(0.5)
@@ -434,14 +436,16 @@
         gen_forward(latent_ref[step + 1], w_in, base, w_one, w_two, refs)
 
 
-def gen_back(step, units, slopes, groups, stored, latents, weights):
+def gen_back(step, packets, own_terms, terms, slopes, stored, latents, weights):
     places, channels = weights[1].shape
-    operands = list(units) + list(slopes) + list(stored[1:]) + [latents] + list(weights)
+    batch = stored[0].shape[0] // places
+    operands = list(packets) + list(own_terms) + list(terms) + list(slopes)
+    operands = operands + list(stored[1:]) + [latents] + list(weights)
     outs = [shape(member.shape, F32) for member in weights]
     if step < STEPS - 1:
         outs = outs + stored_shapes(places, channels)
-    body = functools.partial(gen_back_body, step, len(units), groups)
-    flops = 12 * 2 * 1024 * 128 * 128
+    body = functools.partial(gen_back_body, step, len(packets) - 1, batch)
+    flops = 24 * 2 * 1024 * 128 * 128
     results = call(body, operands, outs, flops=flops)
     return results[:4], results[4:]
 
@@ -510,7 +514,6 @@
 
 
 EDGES = (("col", 1), ("row", 1), ("row", 0), ("col", 0))
-GROUPS = ((0, 1, 2, 3),)
 
 
 def on_device(
@@ -532,19 +535,14 @@
                 [member[0, 0] for member in (g_in, g_base, g_one, g_two)],
             )
         fakes = stored[0]
-        returns = [None] * len(EDGES)
-        units = [None] * len(EDGES)
-        own_grads, own_unit, after = judge_own(packet, fakes, reals_rows, stored[1], step, batch, reals)
-        slopes = [after]
-        for group in GROUPS:
-            grads, some, after = judge_others([arrived[i] for i in group], fakes, batch, after)
-            slopes.append(after)
-            for i, grad, unit in zip(group, grads, some):
-                returns[i] = paired(grad, *EDGES[i])
-                units[i] = unit
-        units = [own_unit] + [units[i] for group in GROUPS for i in group]
-        sizes = [len(group) for group in GROUPS]
-        gens, stored = gen_back(step, units, slopes, sizes, stored, latents, gens)
+        own_grads, *own_terms, own_slope = judge_own(
+            packet, fakes, reals_rows, stored[1], step, batch, reals
+        )
+        grads, terms, slope = judge_others(arrived, fakes, batch, own_slope)
+        returns = [paired(grad, *edge) for grad, edge in zip(grads, EDGES)]
+        gens, stored = gen_back(
+            step, [packet] + arrived, own_terms, terms, [own_slope, slope], stored, latents, gens
+        )
         results = disc_update(
             own_grads, returns, gens[0], discs, verdict if is_last else None, batch, reals
         )

time: 51.7 us -> 50.6 us (0.979)
  waiting for transfers between devices: 7.81 us -> 6.94 us
    ppermute x16, waiting for transfers between devices: 7.81 us -> 6.94 us  [paired(): return lax.ppermute(block, axis, route)]
  transfers between devices with their start and end apart: 16 -> 16, of which waited for: 7 -> 7; matrix products, arithmetic and copies ran while one was open for 0% -> 0% of each run, Pallas kernels for 22% -> 23%
where the time goes in v3:
time: 50.6 us; the launch traced here: 50.4 us
  starting transfers between devices  21.9 us (43%)
  Pallas kernels  20.9 us (41%)
  waiting for transfers between devices  6.94 us (14%)
  between operations  0.73 us (1%)
    ppermute x16, starting transfers between devices, paired(): return lax.ppermute(block, axis, route)  21.9 us
    pallas_call x10, Pallas kernels, call(): pl.pallas_call(body, out_shape=tuple(out_shape), in_specs=[pl.BlockSpec(m...  20.9 us
    ppermute x16, waiting for transfers between devices, paired(): return lax.ppermute(block, axis, route)  6.94 us
  transfers between devices with their start and end apart: 16, of which 7 were waited for; matrix products, arithmetic and copies ran while one was open for 0% of the time, Pallas kernels for 23%

profile of v3, /device:TPU:0, one launch (start us, length us, event | category | flops | bytes accessed | tf_op | source)
XLA Modules:
  0.0 50.4 jit_solution(10699265668796214858)
XLA Ops:
  0.6 0.9 %shard_map.170 = (bf16[272,128]{1,0:T(8,128)(2,1)S(1)}, f32[128,128]{1,0:T(8,128)S(1)}, f32[128,128]{1,0:T(8,128)S(1)}, f32[1,128]{1,0:T(1,128)S(1)}) custom-call(f32[128,128]{1,0:T(8,128)} %bitcast.24, f32[128,128]{1,0:T(8,128)} %bitcast.25, f32[1,128]{1,0:T(1,128)} %bitcast.28), custom_call_target="tpu_custom_call" | custom-call | tf_op jit(solution)/shard_map/pallas_call | solution.py:64
  1.6 5.7 %collective-permute-start = (bf16[272,128]{1,0:T(8,128)(2,1)S(1)}, bf16[272,128]{1,0:T(8,128)(2,1)S(1)}, u32[]{:S(2)}, u32[]{:S(2)}) collective-permute-start(bf16[272,128]{1,0:T(8,128)(2,1)S(1)} %get-tuple-element.79.packet_ref.refs_0_), channel_id=1, source_target_pairs={{1,2},{2,1},{3,4},{4,3},{5,6},{6,5},{7,8},{8,7},{9,10},{10,9},{11,... | collective-permute-start | bytes 208904 | tf_op jit(solution)/shard_map/ppermute | solution.py:513
  7.2 3.5 %collective-permute-start.1 = (bf16[272,128]{1,0:T(8,128)(2,1)S(1)}, bf16[272,128]{1,0:T(8,128)(2,1)S(1)}, u32[]{:S(2)}, u32[]{:S(2)}) collective-permute-start(bf16[272,128]{1,0:T(8,128)(2,1)S(1)} %get-tuple-element.79.packet_ref.refs_0_), channel_id=1, source_target_pairs={{16,32},{32,16},{48,64},{64,48},{80,96},{96,80},{112,0},{0,112},{1... | collective-permute-start | bytes 208904 | tf_op jit(solution)/shard_map/ppermute | solution.py:513
  10.7 2.1 %shard_map.171 = (f32[128,128]{1,0:T(8,128)S(1)}, f32[1024,128]{1,0:T(8,128)S(1)}, f32[128,128]{1,0:T(8,128)S(1)}, f32[128,128]{1,0:T(8,128)S(1)}, f32[2,8,128]{...) custom-call(s32[2,2]{1,0:T(2,128)} %bitcast.26, ...), custom_call_target="tpu_custom_call" | custom-call | flops 134217728 | bytes 134217 | tf_op jit(solution)/shard_map/pallas_call | solution.py:64
  12.8 2.3 %shard_map.172 = (f32[272,128]{1,0:T(8,128)S(1)}, bf16[1024,256]{1,0:T(8,128)(2,1)S(1)}, bf16[1024,256]{1,0:T(8,128)(2,1)S(1)}, f32[8,128]{1,0:T(8,128)S(1)}) custom-call(bf16[272,128]{1,0:T(8,128)(2,1)S(1)} %get-tuple-element.79.packet_ref.refs_0_, bf16[2048,128]{1,0:T(8,128)(2,1)S(1)} %get-tuple-element.80.fakes_ref.refs_4_, ...), custom_call_target="tpu_custom_call" | custom-call | flops 805306368 | bytes 805306 | tf_op jit(solution)/shard_map/pallas_call | solution.py:64
  15.1 3.8 %shard_map.173 = (bf16[272,128]{1,0:T(8,128)(2,1)S(1)}, bf16[272,128]{1,0:T(8,128)(2,1)S(1)}, bf16[272,128]{1,0:T(8,128)(2,1)S(1)}, bf16[272,128]{1,0:T(8,128)(2...) custom-call(bf16[272,128]{1,0:T(8,128)(2,1)S(1)} %collective-permute, ...), custom_call_target="tpu_custom_call" | custom-call | flops 1610612736 | bytes 1610612 | tf_op jit(solution)/shard_map/pallas_call | solution.py:64
  19.0 1.6 %collective-permute-start.4 = (bf16[272,128]{1,0:T(8,128)(2,1)S(1)}, bf16[272,128]{1,0:T(8,128)(2,1)S(1)}, u32[]{:S(2)}, u32[]{:S(2)}) collective-permute-start(bf16[272,128]{1,0:T(8,128)(2,1)S(1)} %get-tuple-element.85), channel_id=1, source_target_pairs={{1,2},{2,1},{3,4},{4,3},{5,6},{6,5},{7,8},{8,7},{9,10},{10,9},{11,... | collective-permute-start | bytes 208904 | tf_op jit(solution)/shard_map/ppermute | solution.py:513
  20.6 1.6 %collective-permute-start.5 = (bf16[272,128]{1,0:T(8,128)(2,1)S(1)}, bf16[272,128]{1,0:T(8,128)(2,1)S(1)}, u32[]{:S(2)}, u32[]{:S(2)}) collective-permute-start(bf16[272,128]{1,0:T(8,128)(2,1)S(1)} %get-tuple-element.86), channel_id=1, source_target_pairs={{16,32},{32,16},{48,64},{64,48},{80,96},{96,80},{112,0},{0,112},{1... | collective-permute-start | bytes 208904 | tf_op jit(solution)/shard_map/ppermute | solution.py:513
  22.6 2.4 %shard_map.174 = (f32[128,128]{1,0:T(8,128)S(1)}, f32[1024,128]{1,0:T(8,128)S(1)}, f32[128,128]{1,0:T(8,128)S(1)}, f32[128,128]{1,0:T(8,128)S(1)}, bf16[2048,128...) custom-call(bf16[272,128]{1,0:T(8,128)(2,1)S(1)} %get-tuple-element., ...), custom_call_target="tpu_custom_call" | custom-call | flops 805306368 | bytes 805306 | tf_op jit(solution)/shard_map/pallas_call | solution.py:64
  25.0 1.4 %collective-permute-done.4.refs_0_ = bf16[272,128]{1,0:T(8,128)(2,1)S(1)} collective-permute-done((bf16[272,128]{1,0:T(8,128)(2,1)S(1)}, bf16[272,128]{1,0:T(8,128)(2,1)S(1)}, u32[]{:S(2)}, u32[]{:S(2)}) %collective-permute-start.4) | collective-permute-done | bytes 69664 | tf_op jit(solution)/shard_map/ppermute | solution.py:513
  26.4 0.7 %collective-permute-done.5.refs_1_ = bf16[272,128]{1,0:T(8,128)(2,1)S(1)} collective-permute-done((bf16[272,128]{1,0:T(8,128)(2,1)S(1)}, bf16[272,128]{1,0:T(8,128)(2,1)S(1)}, u32[]{:S(2)}, u32[]{:S(2)}) %collective-permute-start.5) | collective-permute-done | bytes 69664 | tf_op jit(solution)/shard_map/ppermute | solution.py:513
  27.1 0.8 %collective-permute-done.6.refs_2_ = bf16[272,128]{1,0:T(8,128)(2,1)S(1)} collective-permute-done((bf16[272,128]{1,0:T(8,128)(2,1)S(1)}, bf16[272,128]{1,0:T(8,128)(2,1)S(1)}, u32[]{:S(2)}, u32[]{:S(2)}) %collective-permute-start.6) | collective-permute-done | bytes 69664 | tf_op jit(solution)/shard_map/ppermute | solution.py:513
  28.0 2.6 %collective-permute-start.8 = (bf16[272,128]{1,0:T(8,128)(2,1)S(1)}, bf16[272,128]{1,0:T(8,128)(2,1)S(1)}, u32[]{:S(2)}, u32[]{:S(2)}) collective-permute-start(bf16[272,128]{1,0:T(8,128)(2,1)S(1)} %get-tuple-element.112.packet_ref.refs_0_), channel_id=1, source_target_pairs={{1,2},{2,1},{3,4},{4,3},{5,6},{6,5},{7,8},{8,7},{9,10},{10,9},{11,... | collective-permute-start | bytes 208904 | tf_op jit(solution)/shard_map/ppermute | solution.py:513
  30.6 1.5 %collective-permute-start.9 = (bf16[272,128]{1,0:T(8,128)(2,1)S(1)}, bf16[272,128]{1,0:T(8,128)(2,1)S(1)}, u32[]{:S(2)}, u32[]{:S(2)}) collective-permute-start(bf16[272,128]{1,0:T(8,128)(2,1)S(1)} %get-tuple-element.112.packet_ref.refs_0_), channel_id=1, source_target_pairs={{16,32},{32,16},{48,64},{64,48},{80,96},{96,80},{112,0},{0,112},{1... | collective-permute-start | bytes 208904 | tf_op jit(solution)/shard_map/ppermute | solution.py:513
  32.1 1.0 %collective-permute-start.10 = (bf16[272,128]{1,0:T(8,128)(2,1)S(1)}, bf16[272,128]{1,0:T(8,128)(2,1)S(1)}, u32[]{:S(2)}, u32[]{:S(2)}) collective-permute-start(bf16[272,128]{1,0:T(8,128)(2,1)S(1)} %get-tuple-element.112.packet_ref.refs_0_), channel_id=1, source_target_pairs={{0,16},{16,0},{32,48},{48,32},{64,80},{80,64},{96,112},{112,96},{1... | collective-permute-start | bytes 208904 | tf_op jit(solution)/shard_map/ppermute | solution.py:513
  33.0 2.3 %shard_map.176 = (f32[272,128]{1,0:T(8,128)S(1)}, bf16[1024,256]{1,0:T(8,128)(2,1)S(1)}, bf16[1024,256]{1,0:T(8,128)(2,1)S(1)}, f32[8,128]{1,0:T(8,128)S(1)}) custom-call(bf16[272,128]{1,0:T(8,128)(2,1)S(1)} %get-tuple-element.112.packet_ref.refs_0_, bf16[2048,128]{1,0:T(8,128)(2,1)S(1)} %get-tuple-element.113.fakes_ref.refs_4_, ...), custom_call_target="tpu_custom_call" | custom-call | flops 805306368 | bytes 805306 | tf_op jit(solution)/shard_map/pallas_call | solution.py:64
  35.6 1.5 %collective-permute-done.9.refs_1_.refs_2_ = bf16[272,128]{1,0:T(8,128)(2,1)S(1)} collective-permute-done((bf16[272,128]{1,0:T(8,128)(2,1)S(1)}, bf16[272,128]{1,0:T(8,128)(2,1)S(1)}, u32[]{:S(2)}, u32[]{:S(2)}) %collective-permute-start.9) | collective-permute-done | bytes 69664 | tf_op jit(solution)/shard_map/ppermute | solution.py:513
  37.1 3.8 %shard_map.177 = (bf16[272,128]{1,0:T(8,128)(2,1)S(1)}, bf16[272,128]{1,0:T(8,128)(2,1)S(1)}, bf16[272,128]{1,0:T(8,128)(2,1)S(1)}, bf16[272,128]{1,0:T(8,128)(2...) custom-call(bf16[272,128]{1,0:T(8,128)(2,1)S(1)} %collective-permute, ...), custom_call_target="tpu_custom_call" | custom-call | flops 1610612736 | bytes 1610612 | tf_op jit(solution)/shard_map/pallas_call | solution.py:64
  41.0 2.4 %collective-permute-start.12 = (bf16[272,128]{1,0:T(8,128)(2,1)S(1)}, bf16[272,128]{1,0:T(8,128)(2,1)S(1)}, u32[]{:S(2)}, u32[]{:S(2)}) collective-permute-start(bf16[272,128]{1,0:T(8,128)(2,1)S(1)} %get-tuple-element.138), channel_id=1, source_target_pairs={{1,2},{2,1},{3,4},{4,3},{5,6},{6,5},{7,8},{8,7},{9,10},{10,9},{11,... | collective-permute-start | bytes 208904 | tf_op jit(solution)/shard_map/ppermute | solution.py:513
  43.3 1.2 %collective-permute-start.13 = (bf16[272,128]{1,0:T(8,128)(2,1)S(1)}, bf16[272,128]{1,0:T(8,128)(2,1)S(1)}, u32[]{:S(2)}, u32[]{:S(2)}) collective-permute-start(bf16[272,128]{1,0:T(8,128)(2,1)S(1)} %get-tuple-element.139), channel_id=1, source_target_pairs={{16,32},{32,16},{48,64},{64,48},{80,96},{96,80},{112,0},{0,112},{1... | collective-permute-start | bytes 208904 | tf_op jit(solution)/shard_map/ppermute | solution.py:513
  45.0 2.5 %shard_map.178 = (f32[128,128]{1,0:T(8,128)}, f32[1024,128]{1,0:T(8,128)}, f32[128,128]{1,0:T(8,128)}, f32[128,128]{1,0:T(8,128)}) custom-call(bf16[272,128]{1,0:T(8,128)(2,1)S(1)} %get-tuple-element.112.packet_ref.refs_0_, bf16[272,128]{1,0:T(8,128)(2,1)S(1)} %collective-permute-done.8.refs_0_.refs_1_, ...), custom_call_target="tpu_custom_call" | custom-call | flops 805306368 | bytes 805306 | tf_op jit(solution)/shard_map/pallas_call | solution.py:64
  47.5 1.6 %collective-permute-done.12.refs_0_ = bf16[272,128]{1,0:T(8,128)(2,1)S(1)} collective-permute-done((bf16[272,128]{1,0:T(8,128)(2,1)S(1)}, bf16[272,128]{1,0:T(8,128)(2,1)S(1)}, u32[]{:S(2)}, u32[]{:S(2)}) %collective-permute-start.12) | collective-permute-done | bytes 69664 | tf_op jit(solution)/shard_map/ppermute | solution.py:513
  49.1 0.6 %collective-permute-done.13.refs_1_ = bf16[272,128]{1,0:T(8,128)(2,1)S(1)} collective-permute-done((bf16[272,128]{1,0:T(8,128)(2,1)S(1)}, bf16[272,128]{1,0:T(8,128)(2,1)S(1)}, u32[]{:S(2)}, u32[]{:S(2)}) %collective-permute-start.13) | collective-permute-done | bytes 69664 | tf_op jit(solution)/shard_map/ppermute | solution.py:513
  49.7 0.7 %shard_map.179 = (f32[128,128]{1,0:T(8,128)}, f32[128,128]{1,0:T(8,128)}, f32[1,128]{1,0:T(1,128)}, f32[2,12]{1,0:T(2,128)}) custom-call(f32[272,128]{1,0:T(8,128)S(1)} %get-tuple-element.137.grads_ref, bf16[272,128]{1,0:T(8,128)(2,1)S(1)} %collective-permute-done.12.refs_0_, bf16[272,128]{1,0:T(8,128)(2,1)S(1)} %collective-permute-done.13.refs_1_, ...), custom_call_target="tpu_custom_call" | custom-call | tf_op jit(solution)/shard_map/pallas_call | solution.py:64
  (18 shorter events, 1.3 us)
Async XLA Ops:
  1.6 13.5 %collective-permute-start = (bf16[272,128]{1,0:T(8,128)(2,1)S(1)}, bf16[272,128]{1,0:T(8,128)(2,1)S(1)}, u32[]{:S(2)}, u32[]{:S(2)}) collective-permute-start(bf16[272,128]{1,0:T(8,128)(2,1)S(1)} %get-tuple-element.79.packet_ref.refs_0_), channel_id=1, source_target_pairs={{1,2},{2,1},{3,4},{4,3},{5,6},{6,5},{7,8},{8,7},{9,10},{10,9},{11,... | collective-permute-start | bytes 208904 | tf_op jit(solution)/shard_map/ppermute | solution.py:513
  7.2 7.9 %collective-permute-start.1 = (bf16[272,128]{1,0:T(8,128)(2,1)S(1)}, bf16[272,128]{1,0:T(8,128)(2,1)S(1)}, u32[]{:S(2)}, u32[]{:S(2)}) collective-permute-start(bf16[272,128]{1,0:T(8,128)(2,1)S(1)} %get-tuple-element.79.packet_ref.refs_0_), channel_id=1, source_target_pairs={{16,32},{32,16},{48,64},{64,48},{80,96},{96,80},{112,0},{0,112},{1... | collective-permute-start | bytes 208904 | tf_op jit(solution)/shard_map/ppermute | solution.py:513
  10.7 4.4 %collective-permute-start.2 = (bf16[272,128]{1,0:T(8,128)(2,1)S(1)}, bf16[272,128]{1,0:T(8,128)(2,1)S(1)}, u32[]{:S(2)}, u32[]{:S(2)}) collective-permute-start(bf16[272,128]{1,0:T(8,128)(2,1)S(1)} %get-tuple-element.79.packet_ref.refs_0_), channel_id=1, source_target_pairs={{0,16},{16,0},{32,48},{48,32},{64,80},{80,64},{96,112},{112,96},{1... | collective-permute-start | bytes 208904 | tf_op jit(solution)/shard_map/ppermute | solution.py:513
  10.7 4.4 %collective-permute-start.3 = (bf16[272,128]{1,0:T(8,128)(2,1)S(1)}, bf16[272,128]{1,0:T(8,128)(2,1)S(1)}, u32[]{:S(2)}, u32[]{:S(2)}) collective-permute-start(bf16[272,128]{1,0:T(8,128)(2,1)S(1)} %get-tuple-element.79.packet_ref.refs_0_), channel_id=1, source_target_pairs={{0,1},{1,0},{2,3},{3,2},{4,5},{5,4},{6,7},{7,6},{8,9},{9,8},{10,11... | collective-permute-start | bytes 208904 | tf_op jit(solution)/shard_map/ppermute | solution.py:513
  19.0 7.4 %collective-permute-start.4 = (bf16[272,128]{1,0:T(8,128)(2,1)S(1)}, bf16[272,128]{1,0:T(8,128)(2,1)S(1)}, u32[]{:S(2)}, u32[]{:S(2)}) collective-permute-start(bf16[272,128]{1,0:T(8,128)(2,1)S(1)} %get-tuple-element.85), channel_id=1, source_target_pairs={{1,2},{2,1},{3,4},{4,3},{5,6},{6,5},{7,8},{8,7},{9,10},{10,9},{11,... | collective-permute-start | bytes 208904 | tf_op jit(solution)/shard_map/ppermute | solution.py:513
  20.6 6.5 %collective-permute-start.5 = (bf16[272,128]{1,0:T(8,128)(2,1)S(1)}, bf16[272,128]{1,0:T(8,128)(2,1)S(1)}, u32[]{:S(2)}, u32[]{:S(2)}) collective-permute-start(bf16[272,128]{1,0:T(8,128)(2,1)S(1)} %get-tuple-element.86), channel_id=1, source_target_pairs={{16,32},{32,16},{48,64},{64,48},{80,96},{96,80},{112,0},{0,112},{1... | collective-permute-start | bytes 208904 | tf_op jit(solution)/shard_map/ppermute | solution.py:513
  22.3 5.7 %collective-permute-start.6 = (bf16[272,128]{1,0:T(8,128)(2,1)S(1)}, bf16[272,128]{1,0:T(8,128)(2,1)S(1)}, u32[]{:S(2)}, u32[]{:S(2)}) collective-permute-start(bf16[272,128]{1,0:T(8,128)(2,1)S(1)} %get-tuple-element.87), channel_id=1, source_target_pairs={{0,16},{16,0},{32,48},{48,32},{64,80},{80,64},{96,112},{112,96},{1... | collective-permute-start | bytes 208904 | tf_op jit(solution)/shard_map/ppermute | solution.py:513
  22.6 5.3 %collective-permute-start.7 = (bf16[272,128]{1,0:T(8,128)(2,1)S(1)}, bf16[272,128]{1,0:T(8,128)(2,1)S(1)}, u32[]{:S(2)}, u32[]{:S(2)}) collective-permute-start(bf16[272,128]{1,0:T(8,128)(2,1)S(1)} %get-tuple-element.88), channel_id=1, source_target_pairs={{0,1},{1,0},{2,3},{3,2},{4,5},{5,4},{6,7},{7,6},{8,9},{9,8},{10,11... | collective-permute-start | bytes 208904 | tf_op jit(solution)/shard_map/ppermute | solution.py:513
  28.0 7.6 %collective-permute-start.8 = (bf16[272,128]{1,0:T(8,128)(2,1)S(1)}, bf16[272,128]{1,0:T(8,128)(2,1)S(1)}, u32[]{:S(2)}, u32[]{:S(2)}) collective-permute-start(bf16[272,128]{1,0:T(8,128)(2,1)S(1)} %get-tuple-element.112.packet_ref.refs_0_), channel_id=1, source_target_pairs={{1,2},{2,1},{3,4},{4,3},{5,6},{6,5},{7,8},{8,7},{9,10},{10,9},{11,... | collective-permute-start | bytes 208904 | tf_op jit(solution)/shard_map/ppermute | solution.py:513
  30.6 6.5 %collective-permute-start.9 = (bf16[272,128]{1,0:T(8,128)(2,1)S(1)}, bf16[272,128]{1,0:T(8,128)(2,1)S(1)}, u32[]{:S(2)}, u32[]{:S(2)}) collective-permute-start(bf16[272,128]{1,0:T(8,128)(2,1)S(1)} %get-tuple-element.112.packet_ref.refs_0_), channel_id=1, source_target_pairs={{16,32},{32,16},{48,64},{64,48},{80,96},{96,80},{112,0},{0,112},{1... | collective-permute-start | bytes 208904 | tf_op jit(solution)/shard_map/ppermute | solution.py:513
  32.1 5.1 %collective-permute-start.10 = (bf16[272,128]{1,0:T(8,128)(2,1)S(1)}, bf16[272,128]{1,0:T(8,128)(2,1)S(1)}, u32[]{:S(2)}, u32[]{:S(2)}) collective-permute-start(bf16[272,128]{1,0:T(8,128)(2,1)S(1)} %get-tuple-element.112.packet_ref.refs_0_), channel_id=1, source_target_pairs={{0,16},{16,0},{32,48},{48,32},{64,80},{80,64},{96,112},{112,96},{1... | collective-permute-start | bytes 208904 | tf_op jit(solution)/shard_map/ppermute | solution.py:513
  33.0 4.1 %collective-permute-start.11 = (bf16[272,128]{1,0:T(8,128)(2,1)S(1)}, bf16[272,128]{1,0:T(8,128)(2,1)S(1)}, u32[]{:S(2)}, u32[]{:S(2)}) collective-permute-start(bf16[272,128]{1,0:T(8,128)(2,1)S(1)} %get-tuple-element.112.packet_ref.refs_0_), channel_id=1, source_target_pairs={{0,1},{1,0},{2,3},{3,2},{4,5},{5,4},{6,7},{7,6},{8,9},{9,8},{10,11... | collective-permute-start | bytes 208904 | tf_op jit(solution)/shard_map/ppermute | solution.py:513
  41.0 8.1 %collective-permute-start.12 = (bf16[272,128]{1,0:T(8,128)(2,1)S(1)}, bf16[272,128]{1,0:T(8,128)(2,1)S(1)}, u32[]{:S(2)}, u32[]{:S(2)}) collective-permute-start(bf16[272,128]{1,0:T(8,128)(2,1)S(1)} %get-tuple-element.138), channel_id=1, source_target_pairs={{1,2},{2,1},{3,4},{4,3},{5,6},{6,5},{7,8},{8,7},{9,10},{10,9},{11,... | collective-permute-start | bytes 208904 | tf_op jit(solution)/shard_map/ppermute | solution.py:513
  43.3 6.4 %collective-permute-start.13 = (bf16[272,128]{1,0:T(8,128)(2,1)S(1)}, bf16[272,128]{1,0:T(8,128)(2,1)S(1)}, u32[]{:S(2)}, u32[]{:S(2)}) collective-permute-start(bf16[272,128]{1,0:T(8,128)(2,1)S(1)} %get-tuple-element.139), channel_id=1, source_target_pairs={{16,32},{32,16},{48,64},{64,48},{80,96},{96,80},{112,0},{0,112},{1... | collective-permute-start | bytes 208904 | tf_op jit(solution)/shard_map/ppermute | solution.py:513
  44.5 5.2 %collective-permute-start.14 = (bf16[272,128]{1,0:T(8,128)(2,1)S(1)}, bf16[272,128]{1,0:T(8,128)(2,1)S(1)}, u32[]{:S(2)}, u32[]{:S(2)}) collective-permute-start(bf16[272,128]{1,0:T(8,128)(2,1)S(1)} %get-tuple-element.140), channel_id=1, source_target_pairs={{0,16},{16,0},{32,48},{48,32},{64,80},{80,64},{96,112},{112,96},{1... | collective-permute-start | bytes 208904 | tf_op jit(solution)/shard_map/ppermute | solution.py:513
  45.0 4.7 %collective-permute-start.15 = (bf16[272,128]{1,0:T(8,128)(2,1)S(1)}, bf16[272,128]{1,0:T(8,128)(2,1)S(1)}, u32[]{:S(2)}, u32[]{:S(2)}) collective-permute-start(bf16[272,128]{1,0:T(8,128)(2,1)S(1)} %get-tuple-element.141), channel_id=1, source_target_pairs={{0,1},{1,0},{2,3},{3,2},{4,5},{5,4},{6,7},{7,6},{8,9},{9,8},{10,11... | collective-permute-start | bytes 208904 | tf_op jit(solution)/shard_map/ppermute | solution.py:513

commit v4 on v3

--- a/solution.py
+++ b/solution.py
@@ -154,14 +154,12 @@
     inner_half = product.astype(BF16) * slope_first
     channels = inner_half.shape[1] // 2
     sides = [slice(0, channels), slice(channels, 2 * channels)]
-    grad_two = [dot_rows(first_half[:, s], outer_half[:, s]) for s in sides]
+    square = dot_rows(first_half, outer_half)
+    grad_two = [square[s, s] for s in sides]
     yield
     result.append((outer_half, inner_half))
-    if shared:
-        wide = dot_rows(images, inner_half)
-        grad_one = [wide[:, s] for s in sides]
-    else:
-        grad_one = [dot_rows(images[:, s], inner_half[:, s]) for s in sides]
+    wide = dot_rows(images, inner_half)
+    grad_one = [wide[:, s] if shared else wide[s, s] for s in sides]
     for i, s in enumerate(sides):
         result.append((grad_one[i], grad_two[i], sums[:, s]))
 
@@ -416,8 +414,10 @@
     two = two_ref[...].astype(BF16) * BF16(0.5)
     inner_half = (dot_turned(cotangent_half, both(two, two)).astype(BF16) * mid_slope_ref[...])
     outer = (cotangent + dot_turned(inner_half, both(one, one))) * gen_slope_ref[...].astype(F32)
-    grad_two = [dot_rows(middle_ref[:, side], cotangent_half[:, side]) for side in sides]
-    grad_one = [dot_rows(hidden_ref[:, side], inner_half[:, side]) for side in sides]
+    square_two = dot_rows(middle_ref[...], cotangent_half)
+    square_one = dot_rows(hidden_ref[...], inner_half)
+    grad_two = [square_two[side, side] for side in sides]
+    grad_one = [square_one[side, side] for side in sides]
     sums = jnp.sum(jnp.sum(outer.reshape(-1, 8, 2 * channels), axis=0), axis=0, keepdims=True)
     latent_turned = latent_ref[step].T
     grad_in = [

time: 50.6 us -> 49.9 us (0.986)
  Pallas kernels: 20.9 us -> 20 us
    pallas_call x10, Pallas kernels: 20.9 us -> 20 us  [call(): pl.pallas_call(body, out_shape=tuple(out_shape), in_specs=[pl.BlockSpec(m...]
where the time goes in v4:
time: 49.9 us; the launch traced here: 49.7 us
  starting transfers between devices  21.9 us (44%)
  Pallas kernels  20 us (40%)
  waiting for transfers between devices  7.13 us (14%)
  between operations  0.73 us (1%)
    ppermute x16, starting transfers between devices, paired(): return lax.ppermute(block, axis, route)  21.9 us
    pallas_call x10, Pallas kernels, call(): pl.pallas_call(body, out_shape=tuple(out_shape), in_specs=[pl.BlockSpec(m...  20 us
    ppermute x16, waiting for transfers between devices, paired(): return lax.ppermute(block, axis, route)  7.13 us
  transfers between devices with their start and end apart: 16, of which 7 were waited for; matrix products, arithmetic and copies ran while one was open for 0% of the time, Pallas kernels for 23%

profile of v4, /device:TPU:0, one launch (start us, length us, event | category | flops | bytes accessed | tf_op | source)
XLA Modules:
  0.0 49.7 jit_solution(1428734577705449891)
XLA Ops:
  0.6 0.9 %shard_map.170 = (bf16[272,128]{1,0:T(8,128)(2,1)S(1)}, f32[128,128]{1,0:T(8,128)S(1)}, f32[128,128]{1,0:T(8,128)S(1)}, f32[1,128]{1,0:T(1,128)S(1)}) custom-call(f32[128,128]{1,0:T(8,128)} %bitcast.24, f32[128,128]{1,0:T(8,128)} %bitcast.25, f32[1,128]{1,0:T(1,128)} %bitcast.28), custom_call_target="tpu_custom_call" | custom-call | tf_op jit(solution)/shard_map/pallas_call | solution.py:64
  1.6 5.7 %collective-permute-start = (bf16[272,128]{1,0:T(8,128)(2,1)S(1)}, bf16[272,128]{1,0:T(8,128)(2,1)S(1)}, u32[]{:S(2)}, u32[]{:S(2)}) collective-permute-start(bf16[272,128]{1,0:T(8,128)(2,1)S(1)} %get-tuple-element.79.packet_ref.refs_0_), channel_id=1, source_target_pairs={{1,2},{2,1},{3,4},{4,3},{5,6},{6,5},{7,8},{8,7},{9,10},{10,9},{11,... | collective-permute-start | bytes 208904 | tf_op jit(solution)/shard_map/ppermute | solution.py:513
  7.2 3.5 %collective-permute-start.1 = (bf16[272,128]{1,0:T(8,128)(2,1)S(1)}, bf16[272,128]{1,0:T(8,128)(2,1)S(1)}, u32[]{:S(2)}, u32[]{:S(2)}) collective-permute-start(bf16[272,128]{1,0:T(8,128)(2,1)S(1)} %get-tuple-element.79.packet_ref.refs_0_), channel_id=1, source_target_pairs={{16,32},{32,16},{48,64},{64,48},{80,96},{96,80},{112,0},{0,112},{1... | collective-permute-start | bytes 208904 | tf_op jit(solution)/shard_map/ppermute | solution.py:513
  10.7 2.1 %shard_map.171 = (f32[128,128]{1,0:T(8,128)S(1)}, f32[1024,128]{1,0:T(8,128)S(1)}, f32[128,128]{1,0:T(8,128)S(1)}, f32[128,128]{1,0:T(8,128)S(1)}, f32[2,8,128]{...) custom-call(s32[2,2]{1,0:T(2,128)} %bitcast.26, ...), custom_call_target="tpu_custom_call" | custom-call | flops 134217728 | bytes 134217 | tf_op jit(solution)/shard_map/pallas_call | solution.py:64
  12.8 2.2 %shard_map.172 = (f32[272,128]{1,0:T(8,128)S(1)}, bf16[1024,256]{1,0:T(8,128)(2,1)S(1)}, bf16[1024,256]{1,0:T(8,128)(2,1)S(1)}, f32[8,128]{1,0:T(8,128)S(1)}) custom-call(bf16[272,128]{1,0:T(8,128)(2,1)S(1)} %get-tuple-element.79.packet_ref.refs_0_, bf16[2048,128]{1,0:T(8,128)(2,1)S(1)} %get-tuple-element.80.fakes_ref.refs_4_, ...), custom_call_target="tpu_custom_call" | custom-call | flops 805306368 | bytes 805306 | tf_op jit(solution)/shard_map/pallas_call | solution.py:64
  15.0 3.5 %shard_map.173 = (bf16[272,128]{1,0:T(8,128)(2,1)S(1)}, bf16[272,128]{1,0:T(8,128)(2,1)S(1)}, bf16[272,128]{1,0:T(8,128)(2,1)S(1)}, bf16[272,128]{1,0:T(8,128)(2...) custom-call(bf16[272,128]{1,0:T(8,128)(2,1)S(1)} %collective-permute, ...), custom_call_target="tpu_custom_call" | custom-call | flops 1610612736 | bytes 1610612 | tf_op jit(solution)/shard_map/pallas_call | solution.py:64
  18.5 1.6 %collective-permute-start.4 = (bf16[272,128]{1,0:T(8,128)(2,1)S(1)}, bf16[272,128]{1,0:T(8,128)(2,1)S(1)}, u32[]{:S(2)}, u32[]{:S(2)}) collective-permute-start(bf16[272,128]{1,0:T(8,128)(2,1)S(1)} %get-tuple-element.85), channel_id=1, source_target_pairs={{1,2},{2,1},{3,4},{4,3},{5,6},{6,5},{7,8},{8,7},{9,10},{10,9},{11,... | collective-permute-start | bytes 208904 | tf_op jit(solution)/shard_map/ppermute | solution.py:513
  20.2 1.8 %collective-permute-start.5 = (bf16[272,128]{1,0:T(8,128)(2,1)S(1)}, bf16[272,128]{1,0:T(8,128)(2,1)S(1)}, u32[]{:S(2)}, u32[]{:S(2)}) collective-permute-start(bf16[272,128]{1,0:T(8,128)(2,1)S(1)} %get-tuple-element.86), channel_id=1, source_target_pairs={{16,32},{32,16},{48,64},{64,48},{80,96},{96,80},{112,0},{0,112},{1... | collective-permute-start | bytes 208904 | tf_op jit(solution)/shard_map/ppermute | solution.py:513
  22.2 2.4 %shard_map.174 = (f32[128,128]{1,0:T(8,128)S(1)}, f32[1024,128]{1,0:T(8,128)S(1)}, f32[128,128]{1,0:T(8,128)S(1)}, f32[128,128]{1,0:T(8,128)S(1)}, bf16[2048,128...) custom-call(bf16[272,128]{1,0:T(8,128)(2,1)S(1)} %get-tuple-element., ...), custom_call_target="tpu_custom_call" | custom-call | flops 805306368 | bytes 805306 | tf_op jit(solution)/shard_map/pallas_call | solution.py:64
  24.6 1.4 %collective-permute-done.4.refs_0_ = bf16[272,128]{1,0:T(8,128)(2,1)S(1)} collective-permute-done((bf16[272,128]{1,0:T(8,128)(2,1)S(1)}, bf16[272,128]{1,0:T(8,128)(2,1)S(1)}, u32[]{:S(2)}, u32[]{:S(2)}) %collective-permute-start.4) | collective-permute-done | bytes 69664 | tf_op jit(solution)/shard_map/ppermute | solution.py:513
  26.0 0.7 %collective-permute-done.5.refs_1_ = bf16[272,128]{1,0:T(8,128)(2,1)S(1)} collective-permute-done((bf16[272,128]{1,0:T(8,128)(2,1)S(1)}, bf16[272,128]{1,0:T(8,128)(2,1)S(1)}, u32[]{:S(2)}, u32[]{:S(2)}) %collective-permute-start.5) | collective-permute-done | bytes 69664 | tf_op jit(solution)/shard_map/ppermute | solution.py:513
  26.6 0.8 %collective-permute-done.6.refs_2_ = bf16[272,128]{1,0:T(8,128)(2,1)S(1)} collective-permute-done((bf16[272,128]{1,0:T(8,128)(2,1)S(1)}, bf16[272,128]{1,0:T(8,128)(2,1)S(1)}, u32[]{:S(2)}, u32[]{:S(2)}) %collective-permute-start.6) | collective-permute-done | bytes 69664 | tf_op jit(solution)/shard_map/ppermute | solution.py:513
  27.6 2.6 %collective-permute-start.8 = (bf16[272,128]{1,0:T(8,128)(2,1)S(1)}, bf16[272,128]{1,0:T(8,128)(2,1)S(1)}, u32[]{:S(2)}, u32[]{:S(2)}) collective-permute-start(bf16[272,128]{1,0:T(8,128)(2,1)S(1)} %get-tuple-element.112.packet_ref.refs_0_), channel_id=1, source_target_pairs={{1,2},{2,1},{3,4},{4,3},{5,6},{6,5},{7,8},{8,7},{9,10},{10,9},{11,... | collective-permute-start | bytes 208904 | tf_op jit(solution)/shard_map/ppermute | solution.py:513
  30.2 1.5 %collective-permute-start.9 = (bf16[272,128]{1,0:T(8,128)(2,1)S(1)}, bf16[272,128]{1,0:T(8,128)(2,1)S(1)}, u32[]{:S(2)}, u32[]{:S(2)}) collective-permute-start(bf16[272,128]{1,0:T(8,128)(2,1)S(1)} %get-tuple-element.112.packet_ref.refs_0_), channel_id=1, source_target_pairs={{16,32},{32,16},{48,64},{64,48},{80,96},{96,80},{112,0},{0,112},{1... | collective-permute-start | bytes 208904 | tf_op jit(solution)/shard_map/ppermute | solution.py:513
  31.6 1.0 %collective-permute-start.10 = (bf16[272,128]{1,0:T(8,128)(2,1)S(1)}, bf16[272,128]{1,0:T(8,128)(2,1)S(1)}, u32[]{:S(2)}, u32[]{:S(2)}) collective-permute-start(bf16[272,128]{1,0:T(8,128)(2,1)S(1)} %get-tuple-element.112.packet_ref.refs_0_), channel_id=1, source_target_pairs={{0,16},{16,0},{32,48},{48,32},{64,80},{80,64},{96,112},{112,96},{1... | collective-permute-start | bytes 208904 | tf_op jit(solution)/shard_map/ppermute | solution.py:513
  32.6 2.2 %shard_map.176 = (f32[272,128]{1,0:T(8,128)S(1)}, bf16[1024,256]{1,0:T(8,128)(2,1)S(1)}, bf16[1024,256]{1,0:T(8,128)(2,1)S(1)}, f32[8,128]{1,0:T(8,128)S(1)}) custom-call(bf16[272,128]{1,0:T(8,128)(2,1)S(1)} %get-tuple-element.112.packet_ref.refs_0_, bf16[2048,128]{1,0:T(8,128)(2,1)S(1)} %get-tuple-element.113.fakes_ref.refs_4_, ...), custom_call_target="tpu_custom_call" | custom-call | flops 805306368 | bytes 805306 | tf_op jit(solution)/shard_map/pallas_call | solution.py:64
  35.2 1.5 %collective-permute-done.9.refs_1_.refs_2_ = bf16[272,128]{1,0:T(8,128)(2,1)S(1)} collective-permute-done((bf16[272,128]{1,0:T(8,128)(2,1)S(1)}, bf16[272,128]{1,0:T(8,128)(2,1)S(1)}, u32[]{:S(2)}, u32[]{:S(2)}) %collective-permute-start.9) | collective-permute-done | bytes 69664 | tf_op jit(solution)/shard_map/ppermute | solution.py:513
  36.7 3.5 %shard_map.177 = (bf16[272,128]{1,0:T(8,128)(2,1)S(1)}, bf16[272,128]{1,0:T(8,128)(2,1)S(1)}, bf16[272,128]{1,0:T(8,128)(2,1)S(1)}, bf16[272,128]{1,0:T(8,128)(2...) custom-call(bf16[272,128]{1,0:T(8,128)(2,1)S(1)} %collective-permute, ...), custom_call_target="tpu_custom_call" | custom-call | flops 1610612736 | bytes 1610612 | tf_op jit(solution)/shard_map/pallas_call | solution.py:64
  40.2 2.4 %collective-permute-start.12 = (bf16[272,128]{1,0:T(8,128)(2,1)S(1)}, bf16[272,128]{1,0:T(8,128)(2,1)S(1)}, u32[]{:S(2)}, u32[]{:S(2)}) collective-permute-start(bf16[272,128]{1,0:T(8,128)(2,1)S(1)} %get-tuple-element.138), channel_id=1, source_target_pairs={{1,2},{2,1},{3,4},{4,3},{5,6},{6,5},{7,8},{8,7},{9,10},{10,9},{11,... | collective-permute-start | bytes 208904 | tf_op jit(solution)/shard_map/ppermute | solution.py:513
  42.6 1.1 %collective-permute-start.13 = (bf16[272,128]{1,0:T(8,128)(2,1)S(1)}, bf16[272,128]{1,0:T(8,128)(2,1)S(1)}, u32[]{:S(2)}, u32[]{:S(2)}) collective-permute-start(bf16[272,128]{1,0:T(8,128)(2,1)S(1)} %get-tuple-element.139), channel_id=1, source_target_pairs={{16,32},{32,16},{48,64},{64,48},{80,96},{96,80},{112,0},{0,112},{1... | collective-permute-start | bytes 208904 | tf_op jit(solution)/shard_map/ppermute | solution.py:513
  44.3 2.5 %shard_map.178 = (f32[128,128]{1,0:T(8,128)}, f32[1024,128]{1,0:T(8,128)}, f32[128,128]{1,0:T(8,128)}, f32[128,128]{1,0:T(8,128)}) custom-call(bf16[272,128]{1,0:T(8,128)(2,1)S(1)} %get-tuple-element.112.packet_ref.refs_0_, bf16[272,128]{1,0:T(8,128)(2,1)S(1)} %collective-permute-done.8.refs_0_.refs_1_, ...), custom_call_target="tpu_custom_call" | custom-call | flops 805306368 | bytes 805306 | tf_op jit(solution)/shard_map/pallas_call | solution.py:64
  46.8 1.6 %collective-permute-done.12.refs_0_ = bf16[272,128]{1,0:T(8,128)(2,1)S(1)} collective-permute-done((bf16[272,128]{1,0:T(8,128)(2,1)S(1)}, bf16[272,128]{1,0:T(8,128)(2,1)S(1)}, u32[]{:S(2)}, u32[]{:S(2)}) %collective-permute-start.12) | collective-permute-done | bytes 69664 | tf_op jit(solution)/shard_map/ppermute | solution.py:513
  48.3 0.7 %collective-permute-done.13.refs_1_ = bf16[272,128]{1,0:T(8,128)(2,1)S(1)} collective-permute-done((bf16[272,128]{1,0:T(8,128)(2,1)S(1)}, bf16[272,128]{1,0:T(8,128)(2,1)S(1)}, u32[]{:S(2)}, u32[]{:S(2)}) %collective-permute-start.13) | collective-permute-done | bytes 69664 | tf_op jit(solution)/shard_map/ppermute | solution.py:513
  49.0 0.7 %shard_map.179 = (f32[128,128]{1,0:T(8,128)}, f32[128,128]{1,0:T(8,128)}, f32[1,128]{1,0:T(1,128)}, f32[2,12]{1,0:T(2,128)}) custom-call(f32[272,128]{1,0:T(8,128)S(1)} %get-tuple-element.137.grads_ref, bf16[272,128]{1,0:T(8,128)(2,1)S(1)} %collective-permute-done.12.refs_0_, bf16[272,128]{1,0:T(8,128)(2,1)S(1)} %collective-permute-done.13.refs_1_, ...), custom_call_target="tpu_custom_call" | custom-call | tf_op jit(solution)/shard_map/pallas_call | solution.py:64
  (18 shorter events, 1.3 us)
Async XLA Ops:
  1.6 13.4 %collective-permute-start = (bf16[272,128]{1,0:T(8,128)(2,1)S(1)}, bf16[272,128]{1,0:T(8,128)(2,1)S(1)}, u32[]{:S(2)}, u32[]{:S(2)}) collective-permute-start(bf16[272,128]{1,0:T(8,128)(2,1)S(1)} %get-tuple-element.79.packet_ref.refs_0_), channel_id=1, source_target_pairs={{1,2},{2,1},{3,4},{4,3},{5,6},{6,5},{7,8},{8,7},{9,10},{10,9},{11,... | collective-permute-start | bytes 208904 | tf_op jit(solution)/shard_map/ppermute | solution.py:513
  7.2 7.8 %collective-permute-start.1 = (bf16[272,128]{1,0:T(8,128)(2,1)S(1)}, bf16[272,128]{1,0:T(8,128)(2,1)S(1)}, u32[]{:S(2)}, u32[]{:S(2)}) collective-permute-start(bf16[272,128]{1,0:T(8,128)(2,1)S(1)} %get-tuple-element.79.packet_ref.refs_0_), channel_id=1, source_target_pairs={{16,32},{32,16},{48,64},{64,48},{80,96},{96,80},{112,0},{0,112},{1... | collective-permute-start | bytes 208904 | tf_op jit(solution)/shard_map/ppermute | solution.py:513
  10.7 4.3 %collective-permute-start.2 = (bf16[272,128]{1,0:T(8,128)(2,1)S(1)}, bf16[272,128]{1,0:T(8,128)(2,1)S(1)}, u32[]{:S(2)}, u32[]{:S(2)}) collective-permute-start(bf16[272,128]{1,0:T(8,128)(2,1)S(1)} %get-tuple-element.79.packet_ref.refs_0_), channel_id=1, source_target_pairs={{0,16},{16,0},{32,48},{48,32},{64,80},{80,64},{96,112},{112,96},{1... | collective-permute-start | bytes 208904 | tf_op jit(solution)/shard_map/ppermute | solution.py:513
  10.7 4.3 %collective-permute-start.3 = (bf16[272,128]{1,0:T(8,128)(2,1)S(1)}, bf16[272,128]{1,0:T(8,128)(2,1)S(1)}, u32[]{:S(2)}, u32[]{:S(2)}) collective-permute-start(bf16[272,128]{1,0:T(8,128)(2,1)S(1)} %get-tuple-element.79.packet_ref.refs_0_), channel_id=1, source_target_pairs={{0,1},{1,0},{2,3},{3,2},{4,5},{5,4},{6,7},{7,6},{8,9},{9,8},{10,11... | collective-permute-start | bytes 208904 | tf_op jit(solution)/shard_map/ppermute | solution.py:513
  18.5 7.4 %collective-permute-start.4 = (bf16[272,128]{1,0:T(8,128)(2,1)S(1)}, bf16[272,128]{1,0:T(8,128)(2,1)S(1)}, u32[]{:S(2)}, u32[]{:S(2)}) collective-permute-start(bf16[272,128]{1,0:T(8,128)(2,1)S(1)} %get-tuple-element.85), channel_id=1, source_target_pairs={{1,2},{2,1},{3,4},{4,3},{5,6},{6,5},{7,8},{8,7},{9,10},{10,9},{11,... | collective-permute-start | bytes 208904 | tf_op jit(solution)/shard_map/ppermute | solution.py:513
  20.2 6.5 %collective-permute-start.5 = (bf16[272,128]{1,0:T(8,128)(2,1)S(1)}, bf16[272,128]{1,0:T(8,128)(2,1)S(1)}, u32[]{:S(2)}, u32[]{:S(2)}) collective-permute-start(bf16[272,128]{1,0:T(8,128)(2,1)S(1)} %get-tuple-element.86), channel_id=1, source_target_pairs={{16,32},{32,16},{48,64},{64,48},{80,96},{96,80},{112,0},{0,112},{1... | collective-permute-start | bytes 208904 | tf_op jit(solution)/shard_map/ppermute | solution.py:513
  21.9 5.5 %collective-permute-start.6 = (bf16[272,128]{1,0:T(8,128)(2,1)S(1)}, bf16[272,128]{1,0:T(8,128)(2,1)S(1)}, u32[]{:S(2)}, u32[]{:S(2)}) collective-permute-start(bf16[272,128]{1,0:T(8,128)(2,1)S(1)} %get-tuple-element.87), channel_id=1, source_target_pairs={{0,16},{16,0},{32,48},{48,32},{64,80},{80,64},{96,112},{112,96},{1... | collective-permute-start | bytes 208904 | tf_op jit(solution)/shard_map/ppermute | solution.py:513
  22.2 5.3 %collective-permute-start.7 = (bf16[272,128]{1,0:T(8,128)(2,1)S(1)}, bf16[272,128]{1,0:T(8,128)(2,1)S(1)}, u32[]{:S(2)}, u32[]{:S(2)}) collective-permute-start(bf16[272,128]{1,0:T(8,128)(2,1)S(1)} %get-tuple-element.88), channel_id=1, source_target_pairs={{0,1},{1,0},{2,3},{3,2},{4,5},{5,4},{6,7},{7,6},{8,9},{9,8},{10,11... | collective-permute-start | bytes 208904 | tf_op jit(solution)/shard_map/ppermute | solution.py:513
  27.6 7.6 %collective-permute-start.8 = (bf16[272,128]{1,0:T(8,128)(2,1)S(1)}, bf16[272,128]{1,0:T(8,128)(2,1)S(1)}, u32[]{:S(2)}, u32[]{:S(2)}) collective-permute-start(bf16[272,128]{1,0:T(8,128)(2,1)S(1)} %get-tuple-element.112.packet_ref.refs_0_), channel_id=1, source_target_pairs={{1,2},{2,1},{3,4},{4,3},{5,6},{6,5},{7,8},{8,7},{9,10},{10,9},{11,... | collective-permute-start | bytes 208904 | tf_op jit(solution)/shard_map/ppermute | solution.py:513
  30.2 6.5 %collective-permute-start.9 = (bf16[272,128]{1,0:T(8,128)(2,1)S(1)}, bf16[272,128]{1,0:T(8,128)(2,1)S(1)}, u32[]{:S(2)}, u32[]{:S(2)}) collective-permute-start(bf16[272,128]{1,0:T(8,128)(2,1)S(1)} %get-tuple-element.112.packet_ref.refs_0_), channel_id=1, source_target_pairs={{16,32},{32,16},{48,64},{64,48},{80,96},{96,80},{112,0},{0,112},{1... | collective-permute-start | bytes 208904 | tf_op jit(solution)/shard_map/ppermute | solution.py:513
  31.6 5.1 %collective-permute-start.10 = (bf16[272,128]{1,0:T(8,128)(2,1)S(1)}, bf16[272,128]{1,0:T(8,128)(2,1)S(1)}, u32[]{:S(2)}, u32[]{:S(2)}) collective-permute-start(bf16[272,128]{1,0:T(8,128)(2,1)S(1)} %get-tuple-element.112.packet_ref.refs_0_), channel_id=1, source_target_pairs={{0,16},{16,0},{32,48},{48,32},{64,80},{80,64},{96,112},{112,96},{1... | collective-permute-start | bytes 208904 | tf_op jit(solution)/shard_map/ppermute | solution.py:513
  32.6 4.1 %collective-permute-start.11 = (bf16[272,128]{1,0:T(8,128)(2,1)S(1)}, bf16[272,128]{1,0:T(8,128)(2,1)S(1)}, u32[]{:S(2)}, u32[]{:S(2)}) collective-permute-start(bf16[272,128]{1,0:T(8,128)(2,1)S(1)} %get-tuple-element.112.packet_ref.refs_0_), channel_id=1, source_target_pairs={{0,1},{1,0},{2,3},{3,2},{4,5},{5,4},{6,7},{7,6},{8,9},{9,8},{10,11... | collective-permute-start | bytes 208904 | tf_op jit(solution)/shard_map/ppermute | solution.py:513
  40.2 8.1 %collective-permute-start.12 = (bf16[272,128]{1,0:T(8,128)(2,1)S(1)}, bf16[272,128]{1,0:T(8,128)(2,1)S(1)}, u32[]{:S(2)}, u32[]{:S(2)}) collective-permute-start(bf16[272,128]{1,0:T(8,128)(2,1)S(1)} %get-tuple-element.138), channel_id=1, source_target_pairs={{1,2},{2,1},{3,4},{4,3},{5,6},{6,5},{7,8},{8,7},{9,10},{10,9},{11,... | collective-permute-start | bytes 208904 | tf_op jit(solution)/shard_map/ppermute | solution.py:513
  42.6 6.4 %collective-permute-start.13 = (bf16[272,128]{1,0:T(8,128)(2,1)S(1)}, bf16[272,128]{1,0:T(8,128)(2,1)S(1)}, u32[]{:S(2)}, u32[]{:S(2)}) collective-permute-start(bf16[272,128]{1,0:T(8,128)(2,1)S(1)} %get-tuple-element.139), channel_id=1, source_target_pairs={{16,32},{32,16},{48,64},{64,48},{80,96},{96,80},{112,0},{0,112},{1... | collective-permute-start | bytes 208904 | tf_op jit(solution)/shard_map/ppermute | solution.py:513
  43.8 5.3 %collective-permute-start.14 = (bf16[272,128]{1,0:T(8,128)(2,1)S(1)}, bf16[272,128]{1,0:T(8,128)(2,1)S(1)}, u32[]{:S(2)}, u32[]{:S(2)}) collective-permute-start(bf16[272,128]{1,0:T(8,128)(2,1)S(1)} %get-tuple-element.140), channel_id=1, source_target_pairs={{0,16},{16,0},{32,48},{48,32},{64,80},{80,64},{96,112},{112,96},{1... | collective-permute-start | bytes 208904 | tf_op jit(solution)/shard_map/ppermute | solution.py:513
  44.3 4.8 %collective-permute-start.15 = (bf16[272,128]{1,0:T(8,128)(2,1)S(1)}, bf16[272,128]{1,0:T(8,128)(2,1)S(1)}, u32[]{:S(2)}, u32[]{:S(2)}) collective-permute-start(bf16[272,128]{1,0:T(8,128)(2,1)S(1)} %get-tuple-element.141), channel_id=1, source_target_pairs={{0,1},{1,0},{2,3},{3,2},{4,5},{5,4},{6,7},{7,6},{8,9},{9,8},{10,11... | collective-permute-start | bytes 208904 | tf_op jit(solution)/shard_map/ppermute | solution.py:513

commit v5 on v4

--- a/solution.py
+++ b/solution.py
@@ -204,16 +204,29 @@
     return totals
 
 
-def judge_own_body(step, batch, reals, packet_ref, fakes_ref, reals_ref, _, grads_ref, outer_ref, inner_ref, slope_ref, lines_ref):
+def own_grads(triples, signs, out_row, places, grads_ref, lines_ref):
+    channels = out_row.shape[1]
+    count = len(signs)
+    verdicts, minus, slopes = verdict_lines(triples, [out_row] * count, signs, places, lines_ref)
+    total_one, total_two, total_out = weigh(triples, [slopes[i : i + 1, :] for i in range(count)])
+    grads_ref[0:channels, :] = total_one
+    grads_ref[channels:HEAD, :] = total_two
+    grads_ref[HEAD : HEAD + 8, :] = verdicts
+    grads_ref[HEAD + 8 : PACKET, :] = jnp.broadcast_to(total_out, (8, channels))
+    return minus
+
+
+def judge_own_body(
+    step, batch, reals, packet_ref, fakes_ref, reals_ref, _, grads_ref, outer_ref, inner_ref, slope_ref, lines_ref
+):
     rows, channels = fakes_ref.shape
     places = rows // batch
     one, two, out_row = unpack(packet_ref)
-    out_pair = twice(out_row)
     pairs = []
     for member in range(batch):
         span = slice(member * places, (member + 1) * places)
         images = jnp.concatenate([fakes_ref[span, :], reals_ref[step * reals + member]], axis=1)
-        pairs.append((images, (one, one), (two, two), out_pair, False))
+        pairs.append((images, (one, one), (two, two), twice(out_row), False))
     results = judge_pairs(pairs)
     for member, result in enumerate(results):
         side = slice(member * channels, (member + 1) * channels)
@@ -221,27 +234,55 @@
         inner_ref[:, side] = result[0][1][:, 0:channels]
     triples = [result[1] for result in results] + [result[2] for result in results]
     signs = [1] * batch + [0] * reals
-    verdicts, minus, slopes = verdict_lines(triples, [out_row] * len(signs), signs, places, lines_ref)
-    total_one, total_two, total_out = weigh(triples, [slopes[i : i + 1, :] for i in range(len(signs))])
-    slope_ref[...] = minus
-    grads_ref[0:channels, :] = total_one
-    grads_ref[channels:HEAD, :] = total_two
-    grads_ref[HEAD : HEAD + 8, :] = verdicts
-    grads_ref[HEAD + 8 : PACKET, :] = jnp.broadcast_to(total_out, (8, channels))
+    slope_ref[...] = own_grads(triples, signs, out_row, places, grads_ref, lines_ref)
+
+
+def judge_fakes_body(batch, packet_ref, fakes_ref, grads_ref, outer_ref, inner_ref, slope_ref, lines_ref):
+    rows, channels = fakes_ref.shape
+    places = rows // batch
+    one, two, out_row = unpack(packet_ref)
+    images = jnp.concatenate([fakes_ref[0:places, :], fakes_ref[places:rows, :]], axis=1)
+    ((terms, *triples),) = judge_pairs([(images, (one, one), (two, two), twice(out_row), False)])
+    outer_ref[...], inner_ref[...] = terms
+    slope_ref[...] = own_grads(triples, [1] * batch, out_row, places, grads_ref, lines_ref)
+
+
+def judge_reals_body(step, reals, packet_ref, reals_ref, _, grads_ref, lines_ref):
+    places = reals_ref.shape[1]
+    one, two, out_row = unpack(packet_ref)
+    images = jnp.concatenate([reals_ref[step * reals], reals_ref[step * reals + 1]], axis=1)
+    ((_, *triples),) = judge_pairs([(images, (one, one), (two, two), twice(out_row), False)])
+    own_grads(triples, [0] * reals, out_row, places, grads_ref, lines_ref)
+
+
+def own_shapes(rows, channels, batch):
+    wide = (rows // batch, batch * channels)
+    return [shape((PACKET, channels), F32), shape(wide, BF16), shape(wide, BF16), shape((8, channels), F32)]
 
 
 def judge_own(packet, fakes, reals_rows, after, step, batch, reals):
     rows, channels = fakes.shape
-    wide = (rows // batch, batch * channels)
-    outs = [
-        shape((PACKET, channels), F32),
-        shape(wide, BF16),
-        shape(wide, BF16),
-        shape((8, channels), F32),
-    ]
     body = functools.partial(judge_own_body, step, batch, reals)
     flops = 4 * 6 * 2 * 1024 * 128 * 128
-    return call(body, [packet, fakes, reals_rows, after], outs, [pltpu.VMEM((8, channels), F32)], flops=flops)
+    scratch = [pltpu.VMEM((8, channels), F32)]
+    operands = [packet, fakes, reals_rows, after]
+    return call(body, operands, own_shapes(rows, channels, batch), scratch, flops=flops)
+
+
+def judge_fakes(packet, fakes, batch):
+    rows, channels = fakes.shape
+    body = functools.partial(judge_fakes_body, batch)
+    flops = 2 * 6 * 2 * 1024 * 128 * 128
+    scratch = [pltpu.VMEM((8, channels), F32)]
+    return call(body, [packet, fakes], own_shapes(rows, channels, batch), scratch, flops=flops)
+
+
+def judge_reals(packet, reals_rows, after, step, reals):
+    channels = packet.shape[1]
+    body = functools.partial(judge_reals_body, step, reals)
+    flops = 2 * 6 * 2 * 1024 * 128 * 128
+    scratch = [pltpu.VMEM((8, channels), F32)]
+    return call(body, [packet, reals_rows, after], [shape((PACKET, channels), F32)], scratch, flops=flops)[0]
 
 
 def judge_others_body(judges, batch, *refs):
@@ -450,8 +491,10 @@
     return results[:4], results[4:]
 
 
-def disc_update_body(batch, reals, is_last, grads_ref, *refs):
+def disc_update_body(batch, reals, is_last, *refs):
     refs = list(refs)
+    grads_ref = refs.pop(0)
+    reals_ref = None if is_last else refs.pop(0)
     returns = [refs.pop(0) for _ in range(4)]
     refs.pop(0)
     params = [refs.pop(0) for _ in range(3)]
@@ -463,6 +506,11 @@
     two = grads_ref[channels:HEAD, :]
     out = grads_ref[HEAD + 8 : HEAD + 9, :]
     verdicts = [grads_ref[HEAD + i : HEAD + 1 + i, :] for i in range(batch + reals)]
+    if reals_ref is not None:
+        one = one + reals_ref[0:channels, :]
+        two = two + reals_ref[channels:HEAD, :]
+        out = out + reals_ref[HEAD + 8 : HEAD + 9, :]
+        verdicts[batch:] = [reals_ref[HEAD + i : HEAD + 1 + i, :] for i in range(reals)]
     tails = []
     for back in returns:
         one = one + back[0:channels, :].astype(F32)
@@ -494,7 +542,7 @@
 
 def disc_update(grads, returns, after, params, before, batch, reals):
     is_last = before is not None
-    operands = [grads] + list(returns) + [after] + list(params) + ([before] if is_last else [])
+    operands = list(grads) + list(returns) + [after] + list(params) + ([before] if is_last else [])
     outs = [shape(member.shape, F32) for member in params]
     if is_last:
         outs = outs + [shape((STEPS, 5 * batch + reals), F32)]
@@ -535,16 +583,19 @@
                 [member[0, 0] for member in (g_in, g_base, g_one, g_two)],
             )
         fakes = stored[0]
-        own_grads, *own_terms, own_slope = judge_own(
-            packet, fakes, reals_rows, stored[1], step, batch, reals
-        )
+        if step == 0:
+            own, *own_terms, own_slope = judge_fakes(packet, fakes, batch)
+        else:
+            own, *own_terms, own_slope = judge_own(packet, fakes, reals_rows, stored[1], step, batch, reals)
+        arrived = arrived[::-1]
         grads, terms, slope = judge_others(arrived, fakes, batch, own_slope)
-        returns = [paired(grad, *edge) for grad, edge in zip(grads, EDGES)]
+        returns = [paired(grad, *edge) for grad, edge in zip(grads[::-1], EDGES)]
         gens, stored = gen_back(
             step, [packet] + arrived, own_terms, terms, [own_slope, slope], stored, latents, gens
         )
+        own = [own] if step else [own, judge_reals(packet, reals_rows, slope, step, reals)]
         results = disc_update(
-            own_grads, returns, gens[0], discs, verdict if is_last else None, batch, reals
+            own, returns, gens[0], discs, verdict if is_last else None, batch, reals
         )
         discs = results[:3]
         verdict = results[3]

time: 49.9 us -> 50.2 us (level)
    pallas_call x10 -> x11, Pallas kernels: 20 us -> 20.3 us  [call(): pl.pallas_call(body, out_shape=tuple(out_shape), in_specs=[pl.BlockSpec(m...]
  transfers between devices with their start and end apart: 16 -> 16, of which waited for: 7 -> 9; matrix products, arithmetic and copies ran while one was open for 0% -> 0% of each run, Pallas kernels for 23% -> 23%
where the time goes in v5:
time: 50.2 us; the launch traced here: 50 us
  starting transfers between devices  21.9 us (44%)
  Pallas kernels  20.3 us (40%)
  waiting for transfers between devices  7.16 us (14%)
  between operations  0.73 us (1%)
    ppermute x16, starting transfers between devices, paired(): return lax.ppermute(block, axis, route)  21.9 us
    pallas_call x11, Pallas kernels, call(): pl.pallas_call(body, out_shape=tuple(out_shape), in_specs=[pl.BlockSpec(m...  20.3 us
    ppermute x16, waiting for transfers between devices, paired(): return lax.ppermute(block, axis, route)  7.16 us
  transfers between devices with their start and end apart: 16, of which 9 were waited for; matrix products, arithmetic and copies ran while one was open for 0% of the time, Pallas kernels for 23%

profile of v5, /device:TPU:0, one launch (start us, length us, event | category | flops | bytes accessed | tf_op | source)
XLA Modules:
  0.0 50.0 jit_solution(681294654852761720)
XLA Ops:
  0.6 0.9 %shard_map.170 = (bf16[272,128]{1,0:T(8,128)(2,1)S(1)}, f32[128,128]{1,0:T(8,128)S(1)}, f32[128,128]{1,0:T(8,128)S(1)}, f32[1,128]{1,0:T(1,128)S(1)}) custom-call(f32[128,128]{1,0:T(8,128)} %bitcast.24, f32[128,128]{1,0:T(8,128)} %bitcast.25, f32[1,128]{1,0:T(1,128)} %bitcast.28), custom_call_target="tpu_custom_call" | custom-call | tf_op jit(solution)/shard_map/pallas_call | solution.py:64
  1.6 5.7 %collective-permute-start.3 = (bf16[272,128]{1,0:T(8,128)(2,1)S(1)}, bf16[272,128]{1,0:T(8,128)(2,1)S(1)}, u32[]{:S(2)}, u32[]{:S(2)}) collective-permute-start(bf16[272,128]{1,0:T(8,128)(2,1)S(1)} %get-tuple-element.79.packet_ref.refs_0_), channel_id=1, source_target_pairs={{1,2},{2,1},{3,4},{4,3},{5,6},{6,5},{7,8},{8,7},{9,10},{10,9},{11,... | collective-permute-start | bytes 208904 | tf_op jit(solution)/shard_map/ppermute | solution.py:561
  7.2 3.5 %collective-permute-start.2 = (bf16[272,128]{1,0:T(8,128)(2,1)S(1)}, bf16[272,128]{1,0:T(8,128)(2,1)S(1)}, u32[]{:S(2)}, u32[]{:S(2)}) collective-permute-start(bf16[272,128]{1,0:T(8,128)(2,1)S(1)} %get-tuple-element.79.packet_ref.refs_0_), channel_id=1, source_target_pairs={{16,32},{32,16},{48,64},{64,48},{80,96},{96,80},{112,0},{0,112},{1... | collective-permute-start | bytes 208904 | tf_op jit(solution)/shard_map/ppermute | solution.py:561
  10.7 2.1 %shard_map.171 = (f32[128,128]{1,0:T(8,128)S(1)}, f32[1024,128]{1,0:T(8,128)S(1)}, f32[128,128]{1,0:T(8,128)S(1)}, f32[128,128]{1,0:T(8,128)S(1)}, f32[2,8,128]{...) custom-call(s32[2,2]{1,0:T(2,128)} %bitcast.26, ...), custom_call_target="tpu_custom_call" | custom-call | flops 134217728 | bytes 134217 | tf_op jit(solution)/shard_map/pallas_call | solution.py:64
  12.8 1.2 %shard_map.172 = (f32[272,128]{1,0:T(8,128)S(1)}, bf16[1024,256]{1,0:T(8,128)(2,1)S(1)}, bf16[1024,256]{1,0:T(8,128)(2,1)S(1)}, f32[8,128]{1,0:T(8,128)S(1)}) custom-call(bf16[272,128]{1,0:T(8,128)(2,1)S(1)} %get-tuple-element.79.packet_ref.refs_0_, bf16[2048,128]{1,0:T(8,128)(2,1)S(1)} %get-tuple-element.80.fakes_ref.refs_4_), custom_call_target="tpu_custom_call" | custom-call | flops 402653184 | bytes 402653 | tf_op jit(solution)/shard_map/pallas_call | solution.py:64
  14.1 0.9 %collective-permute-done.1.refs_1_.refs_2_ = bf16[272,128]{1,0:T(8,128)(2,1)S(1)} collective-permute-done((bf16[272,128]{1,0:T(8,128)(2,1)S(1)}, bf16[272,128]{1,0:T(8,128)(2,1)S(1)}, u32[]{:S(2)}, u32[]{:S(2)}) %collective-permute-start.1) | collective-permute-done | bytes 69664 | tf_op jit(solution)/shard_map/ppermute | solution.py:561
  15.0 3.5 %shard_map.173 = (bf16[272,128]{1,0:T(8,128)(2,1)S(1)}, bf16[272,128]{1,0:T(8,128)(2,1)S(1)}, bf16[272,128]{1,0:T(8,128)(2,1)S(1)}, bf16[272,128]{1,0:T(8,128)(2...) custom-call(bf16[272,128]{1,0:T(8,128)(2,1)S(1)} %collective-permute, ...), custom_call_target="tpu_custom_call" | custom-call | flops 1610612736 | bytes 1610612 | tf_op jit(solution)/shard_map/pallas_call | solution.py:64
  18.5 1.2 %collective-permute-start.4 = (bf16[272,128]{1,0:T(8,128)(2,1)S(1)}, bf16[272,128]{1,0:T(8,128)(2,1)S(1)}, u32[]{:S(2)}, u32[]{:S(2)}) collective-permute-start(bf16[272,128]{1,0:T(8,128)(2,1)S(1)} %get-tuple-element.85), channel_id=1, source_target_pairs={{1,2},{2,1},{3,4},{4,3},{5,6},{6,5},{7,8},{8,7},{9,10},{10,9},{11,... | collective-permute-start | bytes 208904 | tf_op jit(solution)/shard_map/ppermute | solution.py:561
  19.7 2.2 %collective-permute-start.5 = (bf16[272,128]{1,0:T(8,128)(2,1)S(1)}, bf16[272,128]{1,0:T(8,128)(2,1)S(1)}, u32[]{:S(2)}, u32[]{:S(2)}) collective-permute-start(bf16[272,128]{1,0:T(8,128)(2,1)S(1)} %get-tuple-element.86), channel_id=1, source_target_pairs={{16,32},{32,16},{48,64},{64,48},{80,96},{96,80},{112,0},{0,112},{1... | collective-permute-start | bytes 208904 | tf_op jit(solution)/shard_map/ppermute | solution.py:561
  21.9 1.2 %shard_map.174.refs_1_ = f32[272,128]{1,0:T(8,128)S(1)} custom-call(bf16[272,128]{1,0:T(8,128)(2,1)S(1)} %get-tuple-element.79.packet_ref.refs_0_, bf16[4,1024,128]{2,1,0:T(8,128)(2,1)S(1)} %get-tuple-element.82.reals_ref, f32[8,128]{1,0:T(8,128)S(1)} %get-tuple-element.84._.refs_16_), custom_call_target="tpu_custom_call" | custom-call | flops 402653184 | bytes 402653 | tf_op jit(solution)/shard_map/pallas_call | solution.py:64
  23.2 2.4 %shard_map.175 = (f32[128,128]{1,0:T(8,128)S(1)}, f32[1024,128]{1,0:T(8,128)S(1)}, f32[128,128]{1,0:T(8,128)S(1)}, f32[128,128]{1,0:T(8,128)S(1)}, bf16[2048,128...) custom-call(bf16[272,128]{1,0:T(8,128)(2,1)S(1)} %get-tuple-element., ...), custom_call_target="tpu_custom_call" | custom-call | flops 805306368 | bytes 805306 | tf_op jit(solution)/shard_map/pallas_call | solution.py:64
  26.2 0.7 %collective-permute-done.6.refs_4_ = bf16[272,128]{1,0:T(8,128)(2,1)S(1)} collective-permute-done((bf16[272,128]{1,0:T(8,128)(2,1)S(1)}, bf16[272,128]{1,0:T(8,128)(2,1)S(1)}, u32[]{:S(2)}, u32[]{:S(2)}) %collective-permute-start.6) | collective-permute-done | bytes 69664 | tf_op jit(solution)/shard_map/ppermute | solution.py:561
  27.0 3.3 %collective-permute-start.11 = (bf16[272,128]{1,0:T(8,128)(2,1)S(1)}, bf16[272,128]{1,0:T(8,128)(2,1)S(1)}, u32[]{:S(2)}, u32[]{:S(2)}) collective-permute-start(bf16[272,128]{1,0:T(8,128)(2,1)S(1)} %get-tuple-element.112.packet_ref.refs_0_), channel_id=1, source_target_pairs={{1,2},{2,1},{3,4},{4,3},{5,6},{6,5},{7,8},{8,7},{9,10},{10,9},{11,... | collective-permute-start | bytes 208904 | tf_op jit(solution)/shard_map/ppermute | solution.py:561
  30.2 1.3 %collective-permute-start.10 = (bf16[272,128]{1,0:T(8,128)(2,1)S(1)}, bf16[272,128]{1,0:T(8,128)(2,1)S(1)}, u32[]{:S(2)}, u32[]{:S(2)}) collective-permute-start(bf16[272,128]{1,0:T(8,128)(2,1)S(1)} %get-tuple-element.112.packet_ref.refs_0_), channel_id=1, source_target_pairs={{16,32},{32,16},{48,64},{64,48},{80,96},{96,80},{112,0},{0,112},{1... | collective-permute-start | bytes 208904 | tf_op jit(solution)/shard_map/ppermute | solution.py:561
  31.5 0.6 %collective-permute-start.9 = (bf16[272,128]{1,0:T(8,128)(2,1)S(1)}, bf16[272,128]{1,0:T(8,128)(2,1)S(1)}, u32[]{:S(2)}, u32[]{:S(2)}) collective-permute-start(bf16[272,128]{1,0:T(8,128)(2,1)S(1)} %get-tuple-element.112.packet_ref.refs_0_), channel_id=1, source_target_pairs={{0,16},{16,0},{32,48},{48,32},{64,80},{80,64},{96,112},{112,96},{1... | collective-permute-start | bytes 208904 | tf_op jit(solution)/shard_map/ppermute | solution.py:561
  32.2 2.2 %shard_map.177 = (f32[272,128]{1,0:T(8,128)S(1)}, bf16[1024,256]{1,0:T(8,128)(2,1)S(1)}, bf16[1024,256]{1,0:T(8,128)(2,1)S(1)}, f32[8,128]{1,0:T(8,128)S(1)}) custom-call(bf16[272,128]{1,0:T(8,128)(2,1)S(1)} %get-tuple-element.112.packet_ref.refs_0_, bf16[2048,128]{1,0:T(8,128)(2,1)S(1)} %get-tuple-element.113.fakes_ref.refs_4_, ...), custom_call_target="tpu_custom_call" | custom-call | flops 805306368 | bytes 805306 | tf_op jit(solution)/shard_map/pallas_call | solution.py:64
  34.4 2.2 %collective-permute-done.10.refs_2_.refs_3_ = bf16[272,128]{1,0:T(8,128)(2,1)S(1)} collective-permute-done((bf16[272,128]{1,0:T(8,128)(2,1)S(1)}, bf16[272,128]{1,0:T(8,128)(2,1)S(1)}, u32[]{:S(2)}, u32[]{:S(2)}) %collective-permute-start.10) | collective-permute-done | bytes 69664 | tf_op jit(solution)/shard_map/ppermute | solution.py:561
  36.6 3.5 %shard_map.178 = (bf16[272,128]{1,0:T(8,128)(2,1)S(1)}, bf16[272,128]{1,0:T(8,128)(2,1)S(1)}, bf16[272,128]{1,0:T(8,128)(2,1)S(1)}, bf16[272,128]{1,0:T(8,128)(2...) custom-call(bf16[272,128]{1,0:T(8,128)(2,1)S(1)} %collective-permute, ...), custom_call_target="tpu_custom_call" | custom-call | flops 1610612736 | bytes 1610612 | tf_op jit(solution)/shard_map/pallas_call | solution.py:64
  40.2 2.4 %collective-permute-start.12 = (bf16[272,128]{1,0:T(8,128)(2,1)S(1)}, bf16[272,128]{1,0:T(8,128)(2,1)S(1)}, u32[]{:S(2)}, u32[]{:S(2)}) collective-permute-start(bf16[272,128]{1,0:T(8,128)(2,1)S(1)} %get-tuple-element.138), channel_id=1, source_target_pairs={{1,2},{2,1},{3,4},{4,3},{5,6},{6,5},{7,8},{8,7},{9,10},{10,9},{11,... | collective-permute-start | bytes 208904 | tf_op jit(solution)/shard_map/ppermute | solution.py:561
  42.6 1.7 %collective-permute-start.13 = (bf16[272,128]{1,0:T(8,128)(2,1)S(1)}, bf16[272,128]{1,0:T(8,128)(2,1)S(1)}, u32[]{:S(2)}, u32[]{:S(2)}) collective-permute-start(bf16[272,128]{1,0:T(8,128)(2,1)S(1)} %get-tuple-element.139), channel_id=1, source_target_pairs={{16,32},{32,16},{48,64},{64,48},{80,96},{96,80},{112,0},{0,112},{1... | collective-permute-start | bytes 208904 | tf_op jit(solution)/shard_map/ppermute | solution.py:561
  44.3 2.5 %shard_map.179 = (f32[128,128]{1,0:T(8,128)}, f32[1024,128]{1,0:T(8,128)}, f32[128,128]{1,0:T(8,128)}, f32[128,128]{1,0:T(8,128)}) custom-call(bf16[272,128]{1,0:T(8,128)(2,1)S(1)} %get-tuple-element.112.packet_ref.refs_0_, bf16[272,128]{1,0:T(8,128)(2,1)S(1)} %collective-permute-done.8.refs_0_.refs_1_, ...), custom_call_target="tpu_custom_call" | custom-call | flops 805306368 | bytes 805306 | tf_op jit(solution)/shard_map/pallas_call | solution.py:64
  46.8 1.2 %collective-permute-done.12.refs_1_ = bf16[272,128]{1,0:T(8,128)(2,1)S(1)} collective-permute-done((bf16[272,128]{1,0:T(8,128)(2,1)S(1)}, bf16[272,128]{1,0:T(8,128)(2,1)S(1)}, u32[]{:S(2)}, u32[]{:S(2)}) %collective-permute-start.12) | collective-permute-done | bytes 69664 | tf_op jit(solution)/shard_map/ppermute | solution.py:561
  48.0 1.1 %collective-permute-done.13.refs_2_ = bf16[272,128]{1,0:T(8,128)(2,1)S(1)} collective-permute-done((bf16[272,128]{1,0:T(8,128)(2,1)S(1)}, bf16[272,128]{1,0:T(8,128)(2,1)S(1)}, u32[]{:S(2)}, u32[]{:S(2)}) %collective-permute-start.13) | collective-permute-done | bytes 69664 | tf_op jit(solution)/shard_map/ppermute | solution.py:561
  49.4 0.7 %shard_map.180 = (f32[128,128]{1,0:T(8,128)}, f32[128,128]{1,0:T(8,128)}, f32[1,128]{1,0:T(1,128)}, f32[2,12]{1,0:T(2,128)}) custom-call(f32[272,128]{1,0:T(8,128)S(1)} %get-tuple-element.137.refs_0_, bf16[272,128]{1,0:T(8,128)(2,1)S(1)} %collective-permute-done.12.refs_1_, bf16[272,128]{1,0:T(8,128)(2,1)S(1)} %collective-permute-done.13.refs_2_, ...), custom_call_target="tpu_custom_call" | custom-call | tf_op jit(solution)/shard_map/pallas_call | solution.py:64
  (19 shorter events, 1.1 us)
Async XLA Ops:
  1.6 12.5 %collective-permute-start.3 = (bf16[272,128]{1,0:T(8,128)(2,1)S(1)}, bf16[272,128]{1,0:T(8,128)(2,1)S(1)}, u32[]{:S(2)}, u32[]{:S(2)}) collective-permute-start(bf16[272,128]{1,0:T(8,128)(2,1)S(1)} %get-tuple-element.79.packet_ref.refs_0_), channel_id=1, source_target_pairs={{1,2},{2,1},{3,4},{4,3},{5,6},{6,5},{7,8},{8,7},{9,10},{10,9},{11,... | collective-permute-start | bytes 208904 | tf_op jit(solution)/shard_map/ppermute | solution.py:561
  7.2 6.8 %collective-permute-start.2 = (bf16[272,128]{1,0:T(8,128)(2,1)S(1)}, bf16[272,128]{1,0:T(8,128)(2,1)S(1)}, u32[]{:S(2)}, u32[]{:S(2)}) collective-permute-start(bf16[272,128]{1,0:T(8,128)(2,1)S(1)} %get-tuple-element.79.packet_ref.refs_0_), channel_id=1, source_target_pairs={{16,32},{32,16},{48,64},{64,48},{80,96},{96,80},{112,0},{0,112},{1... | collective-permute-start | bytes 208904 | tf_op jit(solution)/shard_map/ppermute | solution.py:561
  10.7 4.3 %collective-permute-start.1 = (bf16[272,128]{1,0:T(8,128)(2,1)S(1)}, bf16[272,128]{1,0:T(8,128)(2,1)S(1)}, u32[]{:S(2)}, u32[]{:S(2)}) collective-permute-start(bf16[272,128]{1,0:T(8,128)(2,1)S(1)} %get-tuple-element.79.packet_ref.refs_0_), channel_id=1, source_target_pairs={{0,16},{16,0},{32,48},{48,32},{64,80},{80,64},{96,112},{112,96},{1... | collective-permute-start | bytes 208904 | tf_op jit(solution)/shard_map/ppermute | solution.py:561
  10.7 4.3 %collective-permute-start = (bf16[272,128]{1,0:T(8,128)(2,1)S(1)}, bf16[272,128]{1,0:T(8,128)(2,1)S(1)}, u32[]{:S(2)}, u32[]{:S(2)}) collective-permute-start(bf16[272,128]{1,0:T(8,128)(2,1)S(1)} %get-tuple-element.79.packet_ref.refs_0_), channel_id=1, source_target_pairs={{0,1},{1,0},{2,3},{3,2},{4,5},{5,4},{6,7},{7,6},{8,9},{9,8},{10,11... | collective-permute-start | bytes 208904 | tf_op jit(solution)/shard_map/ppermute | solution.py:561
  18.5 7.5 %collective-permute-start.4 = (bf16[272,128]{1,0:T(8,128)(2,1)S(1)}, bf16[272,128]{1,0:T(8,128)(2,1)S(1)}, u32[]{:S(2)}, u32[]{:S(2)}) collective-permute-start(bf16[272,128]{1,0:T(8,128)(2,1)S(1)} %get-tuple-element.85), channel_id=1, source_target_pairs={{1,2},{2,1},{3,4},{4,3},{5,6},{6,5},{7,8},{8,7},{9,10},{10,9},{11,... | collective-permute-start | bytes 208904 | tf_op jit(solution)/shard_map/ppermute | solution.py:561
  19.7 6.5 %collective-permute-start.5 = (bf16[272,128]{1,0:T(8,128)(2,1)S(1)}, bf16[272,128]{1,0:T(8,128)(2,1)S(1)}, u32[]{:S(2)}, u32[]{:S(2)}) collective-permute-start(bf16[272,128]{1,0:T(8,128)(2,1)S(1)} %get-tuple-element.86), channel_id=1, source_target_pairs={{16,32},{32,16},{48,64},{64,48},{80,96},{96,80},{112,0},{0,112},{1... | collective-permute-start | bytes 208904 | tf_op jit(solution)/shard_map/ppermute | solution.py:561
  21.9 4.9 %collective-permute-start.6 = (bf16[272,128]{1,0:T(8,128)(2,1)S(1)}, bf16[272,128]{1,0:T(8,128)(2,1)S(1)}, u32[]{:S(2)}, u32[]{:S(2)}) collective-permute-start(bf16[272,128]{1,0:T(8,128)(2,1)S(1)} %get-tuple-element.87), channel_id=1, source_target_pairs={{0,16},{16,0},{32,48},{48,32},{64,80},{80,64},{96,112},{112,96},{1... | collective-permute-start | bytes 208904 | tf_op jit(solution)/shard_map/ppermute | solution.py:561
  21.9 4.9 %collective-permute-start.7 = (bf16[272,128]{1,0:T(8,128)(2,1)S(1)}, bf16[272,128]{1,0:T(8,128)(2,1)S(1)}, u32[]{:S(2)}, u32[]{:S(2)}) collective-permute-start(bf16[272,128]{1,0:T(8,128)(2,1)S(1)} %get-tuple-element.88), channel_id=1, source_target_pairs={{0,1},{1,0},{2,3},{3,2},{4,5},{5,4},{6,7},{7,6},{8,9},{9,8},{10,11... | collective-permute-start | bytes 208904 | tf_op jit(solution)/shard_map/ppermute | solution.py:561
  27.0 7.4 %collective-permute-start.11 = (bf16[272,128]{1,0:T(8,128)(2,1)S(1)}, bf16[272,128]{1,0:T(8,128)(2,1)S(1)}, u32[]{:S(2)}, u32[]{:S(2)}) collective-permute-start(bf16[272,128]{1,0:T(8,128)(2,1)S(1)} %get-tuple-element.112.packet_ref.refs_0_), channel_id=1, source_target_pairs={{1,2},{2,1},{3,4},{4,3},{5,6},{6,5},{7,8},{8,7},{9,10},{10,9},{11,... | collective-permute-start | bytes 208904 | tf_op jit(solution)/shard_map/ppermute | solution.py:561
  30.2 6.4 %collective-permute-start.10 = (bf16[272,128]{1,0:T(8,128)(2,1)S(1)}, bf16[272,128]{1,0:T(8,128)(2,1)S(1)}, u32[]{:S(2)}, u32[]{:S(2)}) collective-permute-start(bf16[272,128]{1,0:T(8,128)(2,1)S(1)} %get-tuple-element.112.packet_ref.refs_0_), channel_id=1, source_target_pairs={{16,32},{32,16},{48,64},{64,48},{80,96},{96,80},{112,0},{0,112},{1... | collective-permute-start | bytes 208904 | tf_op jit(solution)/shard_map/ppermute | solution.py:561
  31.5 5.1 %collective-permute-start.9 = (bf16[272,128]{1,0:T(8,128)(2,1)S(1)}, bf16[272,128]{1,0:T(8,128)(2,1)S(1)}, u32[]{:S(2)}, u32[]{:S(2)}) collective-permute-start(bf16[272,128]{1,0:T(8,128)(2,1)S(1)} %get-tuple-element.112.packet_ref.refs_0_), channel_id=1, source_target_pairs={{0,16},{16,0},{32,48},{48,32},{64,80},{80,64},{96,112},{112,96},{1... | collective-permute-start | bytes 208904 | tf_op jit(solution)/shard_map/ppermute | solution.py:561
  32.2 4.5 %collective-permute-start.8 = (bf16[272,128]{1,0:T(8,128)(2,1)S(1)}, bf16[272,128]{1,0:T(8,128)(2,1)S(1)}, u32[]{:S(2)}, u32[]{:S(2)}) collective-permute-start(bf16[272,128]{1,0:T(8,128)(2,1)S(1)} %get-tuple-element.112.packet_ref.refs_0_), channel_id=1, source_target_pairs={{0,1},{1,0},{2,3},{3,2},{4,5},{5,4},{6,7},{7,6},{8,9},{9,8},{10,11... | collective-permute-start | bytes 208904 | tf_op jit(solution)/shard_map/ppermute | solution.py:561
  40.2 7.9 %collective-permute-start.12 = (bf16[272,128]{1,0:T(8,128)(2,1)S(1)}, bf16[272,128]{1,0:T(8,128)(2,1)S(1)}, u32[]{:S(2)}, u32[]{:S(2)}) collective-permute-start(bf16[272,128]{1,0:T(8,128)(2,1)S(1)} %get-tuple-element.138), channel_id=1, source_target_pairs={{1,2},{2,1},{3,4},{4,3},{5,6},{6,5},{7,8},{8,7},{9,10},{10,9},{11,... | collective-permute-start | bytes 208904 | tf_op jit(solution)/shard_map/ppermute | solution.py:561
  42.6 6.5 %collective-permute-start.13 = (bf16[272,128]{1,0:T(8,128)(2,1)S(1)}, bf16[272,128]{1,0:T(8,128)(2,1)S(1)}, u32[]{:S(2)}, u32[]{:S(2)}) collective-permute-start(bf16[272,128]{1,0:T(8,128)(2,1)S(1)} %get-tuple-element.139), channel_id=1, source_target_pairs={{16,32},{32,16},{48,64},{64,48},{80,96},{96,80},{112,0},{0,112},{1... | collective-permute-start | bytes 208904 | tf_op jit(solution)/shard_map/ppermute | solution.py:561
  44.3 5.1 %collective-permute-start.14 = (bf16[272,128]{1,0:T(8,128)(2,1)S(1)}, bf16[272,128]{1,0:T(8,128)(2,1)S(1)}, u32[]{:S(2)}, u32[]{:S(2)}) collective-permute-start(bf16[272,128]{1,0:T(8,128)(2,1)S(1)} %get-tuple-element.140), channel_id=1, source_target_pairs={{0,16},{16,0},{32,48},{48,32},{64,80},{80,64},{96,112},{112,96},{1... | collective-permute-start | bytes 208904 | tf_op jit(solution)/shard_map/ppermute | solution.py:561
  44.3 5.1 %collective-permute-start.15 = (bf16[272,128]{1,0:T(8,128)(2,1)S(1)}, bf16[272,128]{1,0:T(8,128)(2,1)S(1)}, u32[]{:S(2)}, u32[]{:S(2)}) collective-permute-start(bf16[272,128]{1,0:T(8,128)(2,1)S(1)} %get-tuple-element.141), channel_id=1, source_target_pairs={{0,1},{1,0},{2,3},{3,2},{4,5},{5,4},{6,7},{7,6},{8,9},{9,8},{10,11... | collective-permute-start | bytes 208904 | tf_op jit(solution)/shard_map/ppermute | solution.py:561
